TPU v7x, 256 devices: a whole 4x4x8 slice. The times are simulated.
256 devices in a mesh: dp: 32 (over x_hi, z, core), proto: 8 (over y, x_lo).
Axes of the slice: x: 4 (x_hi: 2, x_lo: 2; x = x_hi * 2 + x_lo), y: 4, z: 8, core: 2. Of those that a mesh axis runs over, the one named last changes fastest.
Arguments:
- view_one: bfloat16 [8192, 256], P('dp'), may hold values from -6 to 6
- view_two: bfloat16 [8192, 256], P('dp'), may hold values from -6 to 6
- prototypes: float32 [8, 16384, 256], P('proto', 'dp'), may hold values from -6 to 6
- moment_first: float32 [8, 16384, 256], P('proto', 'dp'), may hold values from -4 to 4
- moment_second: float32 [8, 16384, 256], P('proto', 'dp'), may hold values from 0.25 to 4
Outputs:
- new_prototypes: float32 [8, 16384, 256], P('proto', 'dp')
- new_first: float32 [8, 16384, 256], P('proto', 'dp')
- new_second: float32 [8, 16384, 256], P('proto', 'dp')
- proto_grad: float32 [8, 16384, 256], P('proto', 'dp')
All inputs are finite; a program needn't handle non-finite values.
Results may differ from a plain program's by a relative error of at most 0.0019.
The roundings to bfloat16 on the way count: a program that leaves them out, or rounds other values in their place, can miss the bound.
Values may be sent and summed in bfloat16 or wider, within the bound.
No kernel may reach another device: no remote copies, remote signals or barrier semaphores. Data moves between devices by JAX's collectives and lax.ppermute only.
A program may use at most 128 MiB of HBM per device.

v0:
```python
import jax
import jax.numpy as jnp
from jax import lax
from jax.sharding import PartitionSpec as P

K = 131072
ITERS = 3


def normalize(values):
    values = values.astype(jnp.float32)
    return values / jnp.sqrt(jnp.sum(values * values, axis=-1, keepdims=True) + 1e-06)


def contract_last(left, right):
    return lax.dot_general(
        left, right, (((1,), (1,)), ((), ())), preferred_element_type=jnp.float32
    )


def contract_first(left, right):
    return lax.dot_general(
        left, right, (((0,), (0,)), ((), ())), preferred_element_type=jnp.float32
    )


def body(view_one, view_two, prototypes, moment_first, moment_second):
    unit = normalize(prototypes[0])
    book = unit.astype(jnp.bfloat16)
    first_rows = normalize(view_one).astype(jnp.bfloat16)
    second_rows = normalize(view_two).astype(jnp.bfloat16)
    local_rows = first_rows.shape[0]
    batch_rows = local_rows * lax.axis_size("dp")
    stacked = jnp.concatenate([first_rows, second_rows], axis=0)
    scores = contract_last(stacked, lax.all_gather(book[None], "dp", axis=1, tiled=True)[0])
    first = scores[:local_rows]
    second = scores[local_rows:]
    expd = jnp.exp(first / 0.05)
    scale_b = jnp.ones((expd.shape[0],), jnp.float32)
    scale_a = jnp.ones((expd.shape[1],), jnp.float32)
    for step in range(ITERS):
        scale_a = 1.0 / (K * lax.psum(jnp.sum(expd * scale_b[:, None], axis=0), "dp"))
        scale_b = 1.0 / (batch_rows * lax.psum(jnp.sum(expd * scale_a[None, :], axis=1), "proto"))
    codes = batch_rows * expd * scale_a[None, :] * scale_b[:, None]
    expo_second = jnp.exp(second / 0.1)
    total = lax.psum(jnp.sum(expo_second, axis=1), "proto")
    probs = expo_second / total[:, None]
    grads_in = ((probs - codes) * (K / (32 * 0.1))).astype(jnp.bfloat16)
    grad = lax.psum_scatter(
        contract_first(grads_in, second_rows), "dp", scatter_dimension=0, tiled=True
    )
    new_first = 0.9 * moment_first[0] + 0.1 * grad
    new_second = 0.95 * moment_second[0] + 0.05 * grad * grad
    new_prototypes = unit - 0.05 * new_first / (jnp.sqrt(new_second) + 1e-08)
    return (new_prototypes[None], new_first[None], new_second[None], grad[None])


def solution(mesh):
    in_specs = (
        P("dp", None),
        P("dp", None),
        P("proto", "dp", None),
        P("proto", "dp", None),
        P("proto", "dp", None),
    )
    out_specs = (
        P("proto", "dp", None),
        P("proto", "dp", None),
        P("proto", "dp", None),
        P("proto", "dp", None),
    )
    return jax.shard_map(body, mesh=mesh, in_specs=in_specs, out_specs=out_specs, check_vma=False)
```

profile of v0, /device:TPU:1, one launch (start us, length us, event | category | flops | bytes accessed | tf_op | source)
XLA Modules:
  0.0 1161.7 jit_solution(12889223849708571741)
XLA Ops:
  7.2 0.0 all-gather.2.cloned.1.call-start
  7.2 1.2 fusion.7
  8.4 1.9 divide_convert_fusion
  10.3 0.0 all-gather.2.cloned.1.call-update
  10.3 0.0 all-reduce.5.cloned.1.call-start
  10.4 1.0 fusion.10
  11.4 1.0 fusion.12
  12.4 1.1 fusion.11
  13.6 103.5 %all-gather.2.cloned.1.call-done = bf16[1,16384,256]{2,1,0:T(8,128)(2,1)} async-done(((bf16[1,512,256]{2,1,0:T(8,128)(2,1)}), bf16[1,16384,256]{2,1,0:T(8,128)(2,1)}) %all-gather.2.cloned.1.call-update) | async-done | bytes 8388624 | tf_op jit(solution)/shard_map/all_gather | solution.py:35
  117.0 16.6 %fusion.3 = f32[512,16384]{1,0:T(8,128)} fusion(bf16[1,16384,256]{2,1,0:T(8,128)(2,1)} %all-gather.2.cloned.1.call-done, bf16[256,256]{1,0:T(8,128)(2,1)S(1)} %get-tuple-element.14, bf16[256,256]{1,0:T(8,128)(2,1)S(1)} %get-tuple-element.13), kind=kOutput, calls=%fused_computation.11 | convolution fusion | flops 4295491584 | bytes 42205184 | tf_op jit(solution)/shard_map/dot_general | solution.py:16
  133.6 8.9 fusion.23
  142.5 0.0 all-reduce.5.cloned.1.call-update
  142.6 0.0 all-reduce.7.cloned.1.call-start
  142.6 227.9 %all-reduce.5.cloned.1.call-done = f32[16384]{0:T(1024)} async-done(((f32[16384]{0:T(1024)}), f32[16384]{0:T(1024)}) %all-reduce.5.cloned.1.call-update) | async-done | bytes 65552 | tf_op jit(solution)/shard_map/psum | solution.py:42
  370.6 0.9 multiply_divide_fusion.2
  371.4 12.2 %fusion.2 = (f32[256]{0:T(256)S(1)}, f32[256]{0:T(256)S(1)}) fusion(f32[512,16384]{1,0:T(8,128)} %fusion.3, f32[16384]{0:T(1024)S(1)} %multiply_divide_fusion.2), kind=kLoop, calls=%fused_computation.10 | loop fusion | flops 20971008 | bytes 33622016 | tf_op jit(solution)/shard_map/reduce_sum | solution.py:46
  383.6 15.0 %psum.51 = f32[256]{0:T(256)S(1)} all-reduce(f32[256]{0:T(256)S(1)} %get-tuple-element.5), channel_id=1, replica_groups=mesh['dp'=32,'proto'=8] {'proto'}, use_global_device_ids=true, to_apply=%region_8.0 | all-reduce | flops 256 | bytes 2048 | tf_op jit(solution)/shard_map/psum | solution.py:43
  398.6 8.2 multiply_reduce_fusion.3
  406.8 0.0 all-reduce.7.cloned.1.call-update
  406.8 0.0 all-reduce.9.cloned.1.call-start
  406.9 229.5 %all-reduce.7.cloned.1.call-done = f32[16384]{0:T(1024)} async-done(((f32[16384]{0:T(1024)}), f32[16384]{0:T(1024)}) %all-reduce.7.cloned.1.call-update) | async-done | bytes 65552 | tf_op jit(solution)/shard_map/psum | solution.py:42
  636.4 0.9 multiply_divide_fusion.1
  637.3 7.5 multiply_reduce_fusion.2
  644.8 15.0 %psum.53 = f32[256]{0:T(256)S(1)} all-reduce(f32[256]{0:T(256)S(1)} %multiply_reduce_fusion.2), channel_id=1, replica_groups=mesh['dp'=32,'proto'=8] {'proto'}, use_global_device_ids=true, to_apply=%region_12.0 | all-reduce | flops 256 | bytes 2048 | tf_op jit(solution)/shard_map/psum | solution.py:43
  659.8 8.2 multiply_reduce_fusion.1
  667.9 0.0 all-reduce.9.cloned.1.call-update
  668.0 0.0 reduce-scatter.2.cloned.1.call-start
  668.0 229.5 %all-reduce.9.cloned.1.call-done = f32[16384]{0:T(1024)} async-done(((f32[16384]{0:T(1024)}), f32[16384]{0:T(1024)}) %all-reduce.9.cloned.1.call-update) | async-done | bytes 65552 | tf_op jit(solution)/shard_map/psum | solution.py:42
  897.6 0.9 broadcast_multiply_fusion
  898.4 7.5 multiply_reduce_fusion
  905.9 15.2 %all-reduce = (f32[256]{0:T(256)S(1)}, f32[256]{0:T(256)S(1)}) all-reduce(f32[256]{0:T(256)S(1)} %multiply_reduce_fusion, f32[256]{0:T(256)S(1)} %get-tuple-element.4), channel_id=1, replica_groups=mesh['dp'=32,'proto'=8] {'proto'}, use_global_device_ids=true, to_apply=%region_16.0 | all-reduce | flops 512 | bytes 4096 | tf_op jit(solution)/shard_map/psum | solution.py:43
  921.1 17.6 %fusion.5 = f32[16384,256]{1,0:T(8,128)} fusion(bf16[256,256]{1,0:T(8,128)(2,1)S(1)} %get-tuple-element.14, f32[512,16384]{1,0:T(8,128)} %fusion.3, f32[256]{0:T(256)S(1)} %multiply_divide_fusion.3, f32[16384]{0:T(1024)S(1)} %get-tuple-element.11, f32[256]{0:T(256)S(1)} %get-tuple-element.7), kind=kOutput, calls=%fused_computation.13 | convolution fusion | flops 2181038080 | bytes 50530304 | tf_op jit(solution)/shard_map/dot_general | solution.py:22
  938.7 0.0 copy-start
  938.7 0.0 copy-start.1
  938.7 0.0 copy-start.2
  938.7 0.0 reduce-scatter.2.cloned.1.call-update
  938.8 213.9 %reduce-scatter.2.cloned.1.call-done = f32[512,256]{1,0:T(8,128)} async-done(((f32[16384,256]{1,0:T(8,128)}), f32[512,256]{1,0:T(8,128)}) %reduce-scatter.2.cloned.1.call-update) | async-done | bytes 524304 | tf_op jit(solution)/shard_map/reduce_scatter | solution.py:49
  1152.6 0.0 copy-done
  1152.6 0.0 copy-done.1
  1152.7 0.0 copy-done.2
  1152.7 2.5 fusion.18
  (6 shorter events, 0.0 us)
Async XLA Ops:
  7.2 109.9 %all-gather.2.cloned.1.call-start = ((), (), s32[]{:S(2)}) async-start(), calls=%async_computation.1 | async-start | bytes 8650752 | tf_op jit(solution)/shard_map/all_gather | solution.py:35
  10.3 360.2 %all-reduce.5.cloned.1.call-start = ((), (), s32[]{:S(2)}) async-start(), calls=%async_computation.2 | async-start | bytes 131072 | tf_op jit(solution)/shard_map/psum | solution.py:42
  142.6 493.8 %all-reduce.7.cloned.1.call-start = ((), (), s32[]{:S(2)}) async-start(), calls=%async_computation.3 | async-start | bytes 131072 | tf_op jit(solution)/shard_map/psum | solution.py:42
  406.8 490.7 %all-reduce.9.cloned.1.call-start = ((), (), s32[]{:S(2)}) async-start(), calls=%async_computation.4 | async-start | bytes 131072 | tf_op jit(solution)/shard_map/psum | solution.py:42
  668.0 484.7 %reduce-scatter.2.cloned.1.call-start = ((), (), s32[]{:S(2)}) async-start(), calls=%async_computation.5 | async-start | bytes 17301504 | tf_op jit(solution)/shard_map/reduce_scatter | solution.py:49
  938.7 213.9 %copy-start = (f32[1,512,256]{2,1,0:T(8,128)S(1)}, f32[1,512,256]{2,1,0:T(8,128)}, u32[]{:S(2)}) copy-start(f32[1,512,256]{2,1,0:T(8,128)} %param.7) | copy-start | bytes 1572868
  938.7 213.9 %copy-start.1 = (f32[1,512,256]{2,1,0:T(8,128)S(1)}, f32[1,512,256]{2,1,0:T(8,128)}, u32[]{:S(2)}) copy-start(f32[1,512,256]{2,1,0:T(8,128)} %param.9) | copy-start | bytes 1572868
  938.7 213.9 %copy-start.2 = (f32[1,512,256]{2,1,0:T(8,128)S(1)}, f32[1,512,256]{2,1,0:T(8,128)}, u32[]{:S(2)}) copy-start(f32[1,512,256]{2,1,0:T(8,128)} %param.8) | copy-start | bytes 1572868
Sparse Core Ops, SparseCore 0:
  11.3 105.6 all-gather.1
  142.7 227.8 all-reduce.4
  406.9 229.4 all-reduce.6
  668.1 229.4 all-reduce.8
  938.9 213.7 reduce-scatter.1
where the time goes:
time: 1170 us; the launch traced here: 1160 us
  waiting for transfers between devices  1000 us (85%)
  other arithmetic  63.7 us (5%)
  blocking collectives  45.2 us (4%)
  matrix products  34.2 us (3%)
  between operations  13.8 us (1%)
    psum x3, waiting for transfers between devices, body(): lax.psum(jnp.sum(expd * scale_b[:, None], axis=0), 'dp')  687 us
    reduce_scatter x1, waiting for transfers between devices, body(): lax.psum_scatter(contract_first(grads_in, second_rows), 'dp', scatter_dim...  214 us
    all_gather x1, waiting for transfers between devices, body(): lax.all_gather(book[None], 'dp', axis=1, tiled=True)[0]  103 us
    psum x3, blocking collectives, body(): lax.psum(jnp.sum(expd * scale_a[None, :], axis=1), 'proto')  45.2 us
    reduce_sum x3, other arithmetic, body(): jnp.sum(expd * scale_b[:, None], axis=0)  25.2 us
  transfers between devices with their start and end apart: 5, of which 5 were waited for; matrix products, arithmetic and copies ran while one was open for 0% of the time, Pallas kernels for 0%

commit v1 on v0

v1 whole, which is shorter than its diff:
```python
import jax
import jax.numpy as jnp
from jax import lax
from jax.sharding import Mesh, PartitionSpec as P

K = 131072
ITERS = 3
ROWS_BY = ("xh", "z")
COLUMN_GROUP = ("c", "y")
ROW_GROUP = ("xh", "z", "xl")


def normalize(values):
    values = values.astype(jnp.float32)
    return values / jnp.sqrt(jnp.sum(values * values, axis=-1, keepdims=True) + 1e-06)


def contract_last(left, right):
    return lax.dot_general(
        left, right, (((1,), (1,)), ((), ())), preferred_element_type=jnp.float32
    )


def share(values, axes):
    count = lax.axis_size(axes)
    return lax.all_to_all(
        jnp.broadcast_to(values[None], (count,) + values.shape), axes, 0, 0, tiled=True
    )


def body(view_one, view_two, prototypes, moment_first, moment_second):
    core, along_y = lax.axis_index("c"), lax.axis_index("y")
    unit = normalize(prototypes[0])
    book = unit.astype(jnp.bfloat16)
    local = jnp.stack(
        [normalize(view_one).astype(jnp.bfloat16), normalize(view_two).astype(jnp.bfloat16)]
    )
    rows = lax.all_gather(local, ("xh", "z", "c"), axis=1, tiled=True)
    batch_rows = rows.shape[1]

    count_y = lax.axis_size("y")
    pieces = [book] + [
        lax.ppermute(book, "y", [((i + k) % count_y, i) for i in range(count_y)])
        for k in range(1, count_y)
    ]
    mine = jnp.stack(pieces)
    other = lax.ppermute(mine, "c", [(0, 1), (1, 0)])
    both = jnp.stack([mine, other])
    group = both.shape[0] * both.shape[1]
    owned = book.shape[0]
    shelf = both.reshape(group * owned, -1)
    order = jnp.stack([(core + i) % 2 * count_y + (along_y + k) % count_y for i in range(2) for k in range(count_y)])

    part = local.shape[1] // count_y
    slices = lax.dynamic_slice_in_dim(local, along_y * part, part, 1)
    mine_one = share(slices[0], ROWS_BY).reshape(-1, local.shape[2])
    mine_two = share(slices[1], ROWS_BY).reshape(-1, local.shape[2])
    held = mine_one.shape[0]

    expd = jnp.exp(contract_last(shelf, mine_one) / 0.05)
    row_total = jnp.sum(jnp.exp(contract_last(shelf, mine_two) / 0.1), axis=0)
    scale_b = jnp.ones((held,), jnp.float32)
    for step in range(ITERS):
        columns = jnp.sum(expd * scale_b[None, :], axis=1).reshape(group, owned)
        columns = jnp.zeros_like(columns).at[order].set(columns)
        columns = jnp.sum(share(columns, COLUMN_GROUP), axis=0)
        scale_a = 1.0 / (K * columns)
        sums = jnp.sum(expd * scale_a[order].reshape(-1, 1), axis=0)
        if step == ITERS - 1:
            sums = jnp.stack([sums, row_total])
        sums = jnp.sum(share(sums, ROW_GROUP), axis=0)
        scale_b = 1.0 / (batch_rows * (sums[0] if step == ITERS - 1 else sums))
    everyone = share(jnp.stack([scale_b, sums[1]]), COLUMN_GROUP)
    everyone = everyone.reshape(2, count_y, 2, -1, part).transpose(2, 3, 0, 1, 4).reshape(2, batch_rows)
    scale_b, total = everyone
    scale_a = scale_a[order[0]]

    expd = jnp.exp(contract_last(book, rows[0]) / 0.05)
    codes = batch_rows * expd * scale_a[:, None] * scale_b[None, :]
    probs = jnp.exp(contract_last(book, rows[1]) / 0.1) / total[None, :]
    grads_in = ((probs - codes) * (K / (32 * 0.1))).astype(jnp.bfloat16)
    grad = lax.dot_general(
        grads_in, rows[1], (((1,), (0,)), ((), ())), preferred_element_type=jnp.float32
    )
    new_first = 0.9 * moment_first[0] + 0.1 * grad
    new_second = 0.95 * moment_second[0] + 0.05 * grad * grad
    new_prototypes = unit - 0.05 * new_first / (jnp.sqrt(new_second) + 1e-08)
    return (new_prototypes[None], new_first[None], new_second[None], grad[None])


def solution(mesh):
    fine = Mesh(mesh.devices.reshape(2, 8, 2, 4, 2), ("xh", "z", "c", "y", "xl"))
    dp, proto = ("xh", "z", "c"), ("y", "xl")
    owned = P(proto, dp, None)
    return jax.shard_map(
        body,
        mesh=fine,
        in_specs=(P(dp, None), P(dp, None), owned, owned, owned),
        out_specs=(owned, owned, owned, owned),
        check_vma=False,
    )
```

time: 1170 us -> 245 us (0.21)
  waiting for transfers between devices: 1000 us -> 61.9 us
  starting transfers between devices: 0.21 us -> 42.7 us
  other arithmetic: 63.7 us -> 45.9 us
    psum x3 -> x0, waiting for transfers between devices: 687 us -> none  [body(): lax.psum(jnp.sum(expd * scale_b[:, None], axis=0), 'dp')]
    reduce_scatter x1 -> x0, waiting for transfers between devices: 214 us -> none  [body(): lax.psum_scatter(contract_first(grads_in, second_rows), 'dp', scatter_dim...]
    all_gather x1, waiting for transfers between devices: 103 us -> 0.01 us  [body(): rows = lax.all_gather(local, ('xh', 'z', 'c'), axis=1, tiled=True)]
    all_to_all x0 -> x6, waiting for transfers between devices: none -> 48.7 us  [share(): lax.all_to_all(jnp.broadcast_to(values[None], (count,) + values.shape), a...]
    psum x3 -> x0, blocking collectives: 45.2 us -> none  [body(): lax.psum(jnp.sum(expd * scale_a[None, :], axis=1), 'proto')]
    all_to_all x0 -> x3, blocking collectives: none -> 37.6 us  [share(): lax.all_to_all(jnp.broadcast_to(values[None], (count,) + values.shape), a...]
    all_to_all x0 -> x6, starting transfers between devices: none -> 37.5 us  [share(): lax.all_to_all(jnp.broadcast_to(values[None], (count,) + values.shape), a...]
    reduce_sum x6 -> x11, other arithmetic: 52.4 us -> 35.3 us  [the longest x3 20.8 us: body(): sums = jnp.sum(expd * scale_a[order].reshape(-1, 1), axis=0)]
  transfers between devices with their start and end apart: 5 -> 11, of which waited for: 5 -> 8; matrix products, arithmetic and copies ran while one was open for 0% -> 25% of each run, Pallas kernels for 0% -> 0%
where the time goes in v1:
time: 245 us; the launch traced here: 244 us
  waiting for transfers between devices  61.9 us (25%)
  other arithmetic  45.9 us (19%)
  starting transfers between devices  42.7 us (17%)
  blocking collectives  37.6 us (15%)
  matrix products  33 us (13%)
  between operations  14.5 us (6%)
  local copies, waits for them, and re-layouts  8.66 us (4%)
    all_to_all x6, waiting for transfers between devices, share(): lax.all_to_all(jnp.broadcast_to(values[None], (count,) + values.shape), a...  48.7 us
    all_to_all x3, blocking collectives, share(): lax.all_to_all(jnp.broadcast_to(values[None], (count,) + values.shape), a...  37.6 us
    all_to_all x6, starting transfers between devices, share(): lax.all_to_all(jnp.broadcast_to(values[None], (count,) + values.shape), a...  37.5 us
    dot_general x3, matrix products, contract_last(): lax.dot_general(left, right, (((1,), (1,)), ((), ())), preferred_element_...  21.3 us
    reduce_sum x3, other arithmetic, body(): sums = jnp.sum(expd * scale_a[order].reshape(-1, 1), axis=0)  20.8 us
    reduce_sum x2, other arithmetic, body(): columns = jnp.sum(expd * scale_b[None, :], axis=1).reshape(group, owned)  14.2 us
    ppermute x3, waiting for transfers between devices, body(): lax.ppermute(book, 'y', [((i + k) % count_y, i) for i in range(count_y)])  13.2 us
    dot_general x1, matrix products, body(): lax.dot_general(grads_in, rows[1], (((1,), (0,)), ((), ())), preferred_el...  11.7 us
  transfers between devices with their start and end apart: 11, of which 8 were waited for; matrix products, arithmetic and copies ran while one was open for 25% of the time, Pallas kernels for 0%

profile of v1, /device:TPU:1, one launch (start us, length us, event | category | flops | bytes accessed | tf_op | source)
XLA Modules:
  0.0 244.3 jit_solution(14785265303030038725)
XLA Ops:
  7.2 0.0 all-gather.2.cloned.1.call-start
  7.2 1.0 fusion.6
  8.2 1.0 fusion.4
  9.3 1.1 fusion.13
  10.4 0.7 pad_maximum_fusion.2
  11.1 0.0 all-gather.2.cloned.1.call-update
  11.2 1.2 fusion.3
  12.4 1.2 fusion.15
  13.5 3.6 %collective-permute-start = (bf16[512,256]{1,0:T(8,128)(2,1)S(1)}, bf16[512,256]{1,0:T(8,128)(2,1)S(1)}, u32[]{:S(2)}, u32[]{:S(2)}) collective-permute-start(bf16[512,256]{1,0:T(8,128)(2,1)S(1)} %fusion.15), channel_id=1, source_target_pairs={{2,0},{4,2},{6,4},{0,6},{3,1},{5,3},{7,5},{1,7},{10,8},{12,10},{14... | collective-permute-start | bytes 786440 | tf_op jit(solution)/shard_map/ppermute | solution.py:43
  17.2 0.3 collective-permute-start.1
  17.5 0.7 collective-permute-start.2
  18.2 1.2 divide_convert_fusion
  19.4 8.2 %collective-permute-done = bf16[512,256]{1,0:T(8,128)(2,1)S(1)} collective-permute-done((bf16[512,256]{1,0:T(8,128)(2,1)S(1)}, bf16[512,256]{1,0:T(8,128)(2,1)S(1)}, u32[]{:S(2)}, u32[]{:S(2)}) %collective-permute-start) | collective-permute-done | bytes 262176 | tf_op jit(solution)/shard_map/ppermute | solution.py:43
  27.7 5.0 %collective-permute-done.2 = bf16[512,256]{1,0:T(8,128)(2,1)S(1)} collective-permute-done((bf16[512,256]{1,0:T(8,128)(2,1)S(1)}, bf16[512,256]{1,0:T(8,128)(2,1)S(1)}, u32[]{:S(2)}, u32[]{:S(2)}) %collective-permute-start.2) | collective-permute-done | bytes 262176 | tf_op jit(solution)/shard_map/ppermute | solution.py:43
  32.6 0.2 fusion.28
  32.8 0.5 collective-permute-start.3
  33.3 0.8 broadcast_in_dim.31
  34.2 10.8 %all-to-all-start = ((bf16[16,64,256]{2,1,0:T(8,128)(2,1)}), bf16[16,64,256]{2,1,0:T(8,128)(2,1)}, u32[]{:S(2)}, u32[]{:S(2)}) async-start(bf16[16,64,256]{2,1,0:T(8,128)(2,1)} %broadcast_in_dim.31), calls=%async_computation | async-start | bytes 1048576 | tf_op jit(solution)/shard_map/all_to_all | solution.py:26
  45.0 0.1 stack.89
  45.1 1.4 pad_maximum_fusion
  46.6 16.4 %all-to-all-done = bf16[16,64,256]{2,1,0:T(8,128)(2,1)} async-done(((bf16[16,64,256]{2,1,0:T(8,128)(2,1)}), bf16[16,64,256]{2,1,0:T(8,128)(2,1)}, u32[]{:S(2)}, u32[]{:S(2)}) %all-to-all-start) | async-done | bytes 524320 | tf_op jit(solution)/shard_map/all_to_all | solution.py:26
  63.0 8.4 %fusion.30 = (f32[4096]{0:T(1024)S(1)}, f32[4096,1024]{1,0:T(8,128)}) fusion(bf16[4096,256]{1,0:T(8,128)(2,1)S(1)} %bitcast.86, bf16[1024,256]{1,0:T(8,128)(2,1)} %bitcast.13), kind=kOutput, calls=%fused_computation.76 | convolution fusion | flops 2155868160 | bytes 19415040 | tf_op jit(solution)/shard_map/dot_general | solution.py:19
  71.4 0.6 scatter_custom_fusion
  72.0 0.7 broadcast_in_dim.32
  72.7 6.0 %all-to-all-start.1 = ((f32[8,8,512]{2,1,0:T(8,128)}), f32[8,8,512]{2,1,0:T(8,128)S(1)}, u32[]{:S(2)}, u32[]{:S(2)}) async-start(f32[8,8,512]{2,1,0:T(8,128)} %broadcast_in_dim.32), calls=%async_computation.1 | async-start | bytes 262144 | tf_op jit(solution)/shard_map/all_to_all | solution.py:26
  78.8 5.5 %all-to-all-done.1 = f32[8,8,512]{2,1,0:T(8,128)S(1)} async-done(((f32[8,8,512]{2,1,0:T(8,128)}), f32[8,8,512]{2,1,0:T(8,128)S(1)}, u32[]{:S(2)}, u32[]{:S(2)}) %all-to-all-start.1) | async-done | bytes 131104 | tf_op jit(solution)/shard_map/all_to_all | solution.py:26
  84.3 0.6 gather_fusion
  84.9 7.0 %multiply_reduce_fusion.4 = f32[1024]{0:T(1024)S(1)} fusion(f32[4096,1024]{1,0:T(8,128)} %get-tuple-element.16, f32[4096]{0:T(1024)S(1)} %bitcast.97), kind=kLoop, calls=%fused_computation.12 | loop fusion | flops 8387584 | bytes 16797696 | tf_op jit(solution)/shard_map/reduce_sum | solution.py:68
  91.9 0.1 broadcast_in_dim.33
  92.0 15.9 %all_to_all.47 = f32[32,1,1024]{2,1,0:T(1,128)S(1)} all-to-all(f32[32,1,1024]{2,1,0:T(1,128)S(1)} %broadcast_in_dim.33), channel_id=1, replica_groups=mesh['xh'=2,'z'=8,'c'=2,'y'=4,'xl'=2] {'xh','z','xl'}, dimensions={0} | all-to-all | bytes 262144 | tf_op jit(solution)/shard_map/all_to_all | solution.py:26
  107.8 0.1 reduce_sum.150
  107.9 7.2 %multiply_reduce_fusion.3 = f32[4096]{0:T(1024)S(1)} fusion(f32[4096,1024]{1,0:T(8,128)} %get-tuple-element.16, f32[1024]{0:T(1024)S(1)} %multiply_divide_fusion.4), kind=kLoop, calls=%fused_computation.11 | loop fusion | flops 8384512 | bytes 16797696 | tf_op jit(solution)/shard_map/reduce_sum | solution.py:64
  115.2 0.6 scatter_custom_fusion.1
  115.8 8.6 %all_to_all.48 = f32[8,8,512]{2,1,0:T(8,128)S(1)} all-to-all(f32[8,8,512]{2,1,0:T(8,128)S(1)} %broadcast_in_dim.34), channel_id=1, replica_groups=mesh['xh'=2,'z'=8,'c'=2,'y'=4,'xl'=2] {'c','y'}, dimensions={0} | all-to-all | bytes 262144 | tf_op jit(solution)/shard_map/all_to_all | solution.py:26
  124.5 0.6 gather_fusion.1
  125.0 6.9 %multiply_reduce_fusion.2 = f32[1024]{0:T(1024)S(1)} fusion(f32[4096,1024]{1,0:T(8,128)} %get-tuple-element.16, f32[4096]{0:T(1024)S(1)} %bitcast.99), kind=kLoop, calls=%fused_computation.10 | loop fusion | flops 8387584 | bytes 16797696 | tf_op jit(solution)/shard_map/reduce_sum | solution.py:68
  132.0 0.1 broadcast_in_dim.35
  132.0 13.1 %all_to_all.49 = f32[32,1,1024]{2,1,0:T(1,128)S(1)} all-to-all(f32[32,1,1024]{2,1,0:T(1,128)S(1)} %broadcast_in_dim.35), channel_id=1, replica_groups=mesh['xh'=2,'z'=8,'c'=2,'y'=4,'xl'=2] {'xh','z','xl'}, dimensions={0} | all-to-all | bytes 262144 | tf_op jit(solution)/shard_map/all_to_all | solution.py:26
  145.1 0.8 broadcast_in_dim.38
  146.0 3.8 %all-to-all-start.6 = ((bf16[16,64,256]{2,1,0:T(8,128)(2,1)}), bf16[16,64,256]{2,1,0:T(8,128)(2,1)S(1)}, u32[]{:S(2)}, u32[]{:S(2)}) async-start(bf16[16,64,256]{2,1,0:T(8,128)(2,1)} %broadcast_in_dim.38), calls=%async_computation.6 | async-start | bytes 1048576 | tf_op jit(solution)/shard_map/all_to_all | solution.py:26
  149.7 0.1 reduce_sum.154
  149.9 7.0 %multiply_reduce_fusion.1 = f32[4096]{0:T(1024)S(1)} fusion(f32[4096,1024]{1,0:T(8,128)} %get-tuple-element.16, f32[1024]{0:T(1024)S(1)} %multiply_divide_fusion.3), kind=kLoop, calls=%fused_computation.9 | loop fusion | flops 8384512 | bytes 16797696 | tf_op jit(solution)/shard_map/reduce_sum | solution.py:64
  156.8 0.6 scatter_custom_fusion.2
  157.5 6.5 %all-to-all-done.6 = bf16[16,64,256]{2,1,0:T(8,128)(2,1)S(1)} async-done(((bf16[16,64,256]{2,1,0:T(8,128)(2,1)}), bf16[16,64,256]{2,1,0:T(8,128)(2,1)S(1)}, u32[]{:S(2)}, u32[]{:S(2)}) %all-to-all-start.6) | async-done | bytes 524320 | tf_op jit(solution)/shard_map/all_to_all | solution.py:26
  164.0 0.7 broadcast_in_dim.36
  164.7 6.4 %all-to-all-start.5 = ((f32[8,8,512]{2,1,0:T(8,128)}), f32[8,8,512]{2,1,0:T(8,128)S(1)}, u32[]{:S(2)}, u32[]{:S(2)}) async-start(f32[8,8,512]{2,1,0:T(8,128)} %broadcast_in_dim.36), calls=%async_computation.5 | async-start | bytes 262144 | tf_op jit(solution)/shard_map/all_to_all | solution.py:26
  171.1 2.6 %exponential_reduce_fusion = f32[1024]{0:T(1024)S(1)} fusion(bf16[4096,256]{1,0:T(8,128)(2,1)S(1)} %bitcast.87, bf16[1024,256]{1,0:T(8,128)(2,1)S(1)} %bitcast.89), kind=kOutput, calls=%fused_computation.7 | convolution fusion | flops 2155871232 | bytes 2625536 | tf_op jit(solution)/shard_map/dot_general | solution.py:19
  173.7 2.6 %all-to-all-done.5 = f32[8,8,512]{2,1,0:T(8,128)S(1)} async-done(((f32[8,8,512]{2,1,0:T(8,128)}), f32[8,8,512]{2,1,0:T(8,128)S(1)}, u32[]{:S(2)}, u32[]{:S(2)}) %all-to-all-start.5) | async-done | bytes 131104 | tf_op jit(solution)/shard_map/all_to_all | solution.py:26
  176.2 0.6 gather_fusion.2
  176.8 6.9 %multiply_reduce_fusion = f32[1024]{0:T(1024)S(1)} fusion(f32[4096,1024]{1,0:T(8,128)} %get-tuple-element.16, f32[4096]{0:T(1024)S(1)} %bitcast.98), kind=kLoop, calls=%fused_computation.8 | loop fusion | flops 8387584 | bytes 16797696 | tf_op jit(solution)/shard_map/reduce_sum | solution.py:68
  183.8 0.8 broadcast_in_dim.39
  184.5 5.1 %all-to-all-start.7 = ((f32[32,2,1024]{2,1,0:T(2,128)}), f32[32,2,1024]{2,1,0:T(2,128)S(1)}, u32[]{:S(2)}, u32[]{:S(2)}) async-start(f32[32,2,1024]{2,1,0:T(2,128)} %broadcast_in_dim.39), calls=%async_computation.7 | async-start | bytes 524288 | tf_op jit(solution)/shard_map/all_to_all | solution.py:26
  189.7 12.6 %all-to-all-done.7 = f32[32,2,1024]{2,1,0:T(2,128)S(1)} async-done(((f32[32,2,1024]{2,1,0:T(2,128)}), f32[32,2,1024]{2,1,0:T(2,128)S(1)}, u32[]{:S(2)}, u32[]{:S(2)}) %all-to-all-start.7) | async-done | bytes 262176 | tf_op jit(solution)/shard_map/all_to_all | solution.py:26
  202.3 0.1 reduce_sum.159
  202.5 0.6 broadcast_in_dim.40
  203.1 5.4 %all-to-all-start.8 = ((f32[8,2,1024]{2,1,0:T(2,128)}), f32[8,2,1024]{2,1,0:T(2,128)S(1)}, u32[]{:S(2)}, u32[]{:S(2)}) async-start(f32[8,2,1024]{2,1,0:T(2,128)} %broadcast_in_dim.40), calls=%async_computation.8 | async-start | bytes 131072 | tf_op jit(solution)/shard_map/all_to_all | solution.py:26
  208.5 4.9 %all-to-all-done.8 = f32[8,2,1024]{2,1,0:T(2,128)S(1)} async-done(((f32[8,2,1024]{2,1,0:T(2,128)}), f32[8,2,1024]{2,1,0:T(2,128)S(1)}, u32[]{:S(2)}, u32[]{:S(2)}) %all-to-all-start.8) | async-done | bytes 65568 | tf_op jit(solution)/shard_map/all_to_all | solution.py:26
  213.5 0.1 reshape.432
  213.6 0.1 div.115
  213.7 0.1 mul.195
  213.8 10.3 %fusion.1 = f32[512,8192]{1,0:T(8,128)} fusion(bf16[2,8192,256]{2,1,0:T(8,128)(2,1)} %all-gather.2.cloned.1.call-done, bf16[1,512,256]{2,1,0:T(8,128)(2,1)S(1)} %divide_convert_fusion), kind=kOutput, calls=%fused_computation.17 | convolution fusion | flops 2147483648 | bytes 21233664 | tf_op jit(solution)/shard_map/dot_general | solution.py:19
  224.1 11.7 %fusion = f32[512,256]{1,0:T(8,128)S(1)} fusion(f32[512,8192]{1,0:T(8,128)} %fusion.1, f32[8192]{0:T(1024)S(1)} %mul.195, f32[512]{0:T(512)S(1)} %bitcast.102, f32[8192]{0:T(1024)S(1)} %div.115, bf16[2,8192,256]{2,1,0:T(8,128)(2,1)} %all-gather.2.cloned.1.call-done, bf16[1,512,256]{2,1,0:T(8,128)(2,1)S(1)} %divide_convert_fusion), kind=kOutput, calls=%fused_computation.15 | convolution fusion | flops 4328521728 | bytes 26019840 | tf_op jit(solution)/shard_map/dot_general | solution.py:82
  235.9 0.0 copy-start.3
  235.9 1.5 fusion.12
  (40 shorter events, 0.3 us)
Async XLA Ops:
  7.2 206.7 %all-gather.2.cloned.1.call-start = ((), (), s32[]{:S(2)}) async-start(), calls=%async_computation.9 | async-start | bytes 8650752 | tf_op jit(solution)/shard_map/all_gather | solution.py:38
  13.5 14.1 %collective-permute-start = (bf16[512,256]{1,0:T(8,128)(2,1)S(1)}, bf16[512,256]{1,0:T(8,128)(2,1)S(1)}, u32[]{:S(2)}, u32[]{:S(2)}) collective-permute-start(bf16[512,256]{1,0:T(8,128)(2,1)S(1)} %fusion.15), channel_id=1, source_target_pairs={{2,0},{4,2},{6,4},{0,6},{3,1},{5,3},{7,5},{1,7},{10,8},{12,10},{14... | collective-permute-start | bytes 786440 | tf_op jit(solution)/shard_map/ppermute | solution.py:43
  17.2 10.5 %collective-permute-start.1 = (bf16[512,256]{1,0:T(8,128)(2,1)S(1)}, bf16[512,256]{1,0:T(8,128)(2,1)S(1)}, u32[]{:S(2)}, u32[]{:S(2)}) collective-permute-start(bf16[512,256]{1,0:T(8,128)(2,1)S(1)} %fusion.15), channel_id=1, source_target_pairs={{4,0},{6,2},{0,4},{2,6},{5,1},{7,3},{1,5},{3,7},{12,8},{14,10},{8,... | collective-permute-start | bytes 786440 | tf_op jit(solution)/shard_map/ppermute | solution.py:43
  17.5 15.1 %collective-permute-start.2 = (bf16[512,256]{1,0:T(8,128)(2,1)S(1)}, bf16[512,256]{1,0:T(8,128)(2,1)S(1)}, u32[]{:S(2)}, u32[]{:S(2)}) collective-permute-start(bf16[512,256]{1,0:T(8,128)(2,1)S(1)} %fusion.15), channel_id=1, source_target_pairs={{6,0},{0,2},{2,4},{4,6},{7,1},{1,3},{3,5},{5,7},{14,8},{8,10},{10,... | collective-permute-start | bytes 786440 | tf_op jit(solution)/shard_map/ppermute | solution.py:43
  32.8 12.3 %collective-permute-start.3 = (bf16[4,512,256]{2,1,0:T(8,128)(2,1)S(1)}, bf16[4,512,256]{2,1,0:T(8,128)(2,1)}, u32[]{:S(2)}, u32[]{:S(2)}) collective-permute-start(bf16[4,512,256]{2,1,0:T(8,128)(2,1)S(1)} %get-tuple-element.8), channel_id=1, source_target_pairs={{0,8},{8,0},{1,9},{9,1},{2,10},{10,2},{3,11},{11,3},{4,12},{12,4},... | collective-permute-start | bytes 3145736 | tf_op jit(solution)/shard_map/ppermute | solution.py:47
  34.2 28.8 %all-to-all-start = ((bf16[16,64,256]{2,1,0:T(8,128)(2,1)}), bf16[16,64,256]{2,1,0:T(8,128)(2,1)}, u32[]{:S(2)}, u32[]{:S(2)}) async-start(bf16[16,64,256]{2,1,0:T(8,128)(2,1)} %broadcast_in_dim.31), calls=%async_computation | async-start | bytes 1048576 | tf_op jit(solution)/shard_map/all_to_all | solution.py:26
  72.7 11.6 %all-to-all-start.1 = ((f32[8,8,512]{2,1,0:T(8,128)}), f32[8,8,512]{2,1,0:T(8,128)S(1)}, u32[]{:S(2)}, u32[]{:S(2)}) async-start(f32[8,8,512]{2,1,0:T(8,128)} %broadcast_in_dim.32), calls=%async_computation.1 | async-start | bytes 262144 | tf_op jit(solution)/shard_map/all_to_all | solution.py:26
  146.0 18.0 %all-to-all-start.6 = ((bf16[16,64,256]{2,1,0:T(8,128)(2,1)}), bf16[16,64,256]{2,1,0:T(8,128)(2,1)S(1)}, u32[]{:S(2)}, u32[]{:S(2)}) async-start(bf16[16,64,256]{2,1,0:T(8,128)(2,1)} %broadcast_in_dim.38), calls=%async_computation.6 | async-start | bytes 1048576 | tf_op jit(solution)/shard_map/all_to_all | solution.py:26
  164.7 11.6 %all-to-all-start.5 = ((f32[8,8,512]{2,1,0:T(8,128)}), f32[8,8,512]{2,1,0:T(8,128)S(1)}, u32[]{:S(2)}, u32[]{:S(2)}) async-start(f32[8,8,512]{2,1,0:T(8,128)} %broadcast_in_dim.36), calls=%async_computation.5 | async-start | bytes 262144 | tf_op jit(solution)/shard_map/all_to_all | solution.py:26
  184.5 17.8 %all-to-all-start.7 = ((f32[32,2,1024]{2,1,0:T(2,128)}), f32[32,2,1024]{2,1,0:T(2,128)S(1)}, u32[]{:S(2)}, u32[]{:S(2)}) async-start(f32[32,2,1024]{2,1,0:T(2,128)} %broadcast_in_dim.39), calls=%async_computation.7 | async-start | bytes 524288 | tf_op jit(solution)/shard_map/all_to_all | solution.py:26
  203.1 10.3 %all-to-all-start.8 = ((f32[8,2,1024]{2,1,0:T(2,128)}), f32[8,2,1024]{2,1,0:T(2,128)S(1)}, u32[]{:S(2)}, u32[]{:S(2)}) async-start(f32[8,2,1024]{2,1,0:T(2,128)} %broadcast_in_dim.40), calls=%async_computation.8 | async-start | bytes 131072 | tf_op jit(solution)/shard_map/all_to_all | solution.py:26
  224.1 11.7 %copy-start = (f32[1,512,256]{2,1,0:T(8,128)S(1)}, f32[1,512,256]{2,1,0:T(8,128)}, u32[]{:S(2)}) copy-start(f32[1,512,256]{2,1,0:T(8,128)} %param.7) | copy-start | bytes 1572868
  224.1 11.8 %copy-start.1 = (f32[1,512,256]{2,1,0:T(8,128)S(1)}, f32[1,512,256]{2,1,0:T(8,128)}, u32[]{:S(2)}) copy-start(f32[1,512,256]{2,1,0:T(8,128)} %param.9) | copy-start | bytes 1572868
  224.1 11.8 %copy-start.2 = (f32[1,512,256]{2,1,0:T(8,128)S(1)}, f32[1,512,256]{2,1,0:T(8,128)}, u32[]{:S(2)}) copy-start(f32[1,512,256]{2,1,0:T(8,128)} %param.8) | copy-start | bytes 1572868
  235.9 1.5 copy-start.3
Sparse Core Ops, SparseCore 0:
  11.4 111.6 all-gather.1

commit v2 on v0

v2 whole, which is shorter than its diff:
```python
import functools
import math

import jax
import jax.numpy as jnp
from jax import lax
from jax.experimental import pallas as pl
from jax.experimental.pallas import tpu as pltpu
from jax.sharding import Mesh, PartitionSpec as P

K = 131072
ITERS = 3
D = 256
OWNED = 512
HELD = 1024
PART = 64
GROUP = 8
BATCH = 8192
ROW_PEERS = 32
LOG2E = math.log2(math.e)
FIRST_SCALE = LOG2E / 0.05
SECOND_SCALE = LOG2E / 0.1
GRAD_SCALE = K / (32 * 0.1)
MIB = 1 << 20

VMEM = pl.BlockSpec(memory_space=pltpu.VMEM)
HBM = pl.BlockSpec(memory_space=pltpu.HBM)
ANY = pl.BlockSpec(memory_space=pl.ANY)
SMEM = pl.BlockSpec(memory_space=pltpu.SMEM)


def normalize(values):
    values = values.astype(jnp.float32)
    return values / jnp.sqrt(jnp.sum(values * values, axis=-1, keepdims=True) + 1e-06)


def contract_last(left, right):
    return lax.dot_general(
        left, right, (((1,), (1,)), ((), ())), preferred_element_type=jnp.float32
    )


def place_of(pos_ref, block):
    return (pos_ref[0] + block // 4) % 2 * 4 + (pos_ref[1] + block % 4) % 4


def book_kernel(proto_ref, book_ref):
    book_ref[...] = normalize(proto_ref[0]).astype(jnp.bfloat16)


def views_kernel(pos_ref, one_ref, two_ref, share_ref):
    for view, ref in enumerate((one_ref, two_ref)):
        rows = normalize(ref[...]).astype(jnp.bfloat16)
        for peer in range(share_ref.shape[0]):
            share_ref[peer, view] = rows


def rows_of(rows_ref, view, at, count):
    return rows_ref[at // PART : (at + count) // PART, view].reshape(count, D)


def copies_of_columns(pos_ref, columns, out_ref):
    line = lax.broadcasted_iota(jnp.int32, (GROUP, OWNED), 0)
    placed = jnp.zeros((GROUP, OWNED), jnp.float32)
    for block, values in enumerate(columns):
        placed = jnp.where(line == place_of(pos_ref, block), values, placed)
    for peer in range(GROUP):
        out_ref[peer] = placed


def expo_kernel(pos_ref, rows_ref, *refs):
    shelves, (expd_ref, out_ref) = refs[:GROUP], refs[GROUP:]
    columns = []
    for block in range(GROUP):
        shelf = shelves[block][...]
        total = jnp.zeros((8, OWNED), jnp.float32)
        for at in range(0, HELD, 256):
            tile = jnp.exp2(contract_last(rows_of(rows_ref, 0, at, 256), shelf) * FIRST_SCALE)
            expd_ref[block, at : at + 256, :] = tile
            total = total + jnp.sum(tile.reshape(32, 8, OWNED), axis=0)
        columns.append(jnp.sum(total, axis=0, keepdims=True))
    copies_of_columns(pos_ref, columns, out_ref)


def rows_as_lanes(partial_ref):
    lines = [
        jnp.sum(partial_ref[j * 128 : (j + 1) * 128, :].T, axis=0, keepdims=True) for j in range(HELD // 128)
    ]
    return jnp.concatenate(lines, axis=0)


def row_kernel(pos_ref, columns_ref, expd_ref, out_ref, scale_ref, partial_ref):
    scale_a = 1.0 / (K * jnp.sum(columns_ref[...], axis=0))
    line = lax.broadcasted_iota(jnp.int32, (GROUP, OWNED), 0)
    for block in range(GROUP):
        picked = jnp.sum(jnp.where(line == place_of(pos_ref, block), scale_a, 0.0), axis=0, keepdims=True)
        scale_ref[block] = jnp.broadcast_to(picked, (8, OWNED))

    def step(i, carry):
        at = pl.ds(pl.multiple_of(i * 64, 64), 64)
        total = jnp.zeros((8, 8, 128), jnp.float32)
        for block in range(GROUP):
            for lane in range(0, OWNED, 128):
                tile = expd_ref[block, at, lane : lane + 128].reshape(8, 8, 128)
                total = total + tile * scale_ref[block, :, lane : lane + 128][None]
        partial_ref[at, :] = total.reshape(64, 128)
        return carry

    lax.fori_loop(0, HELD // 64, step, 0)
    lines = rows_as_lanes(partial_ref)
    for peer in range(ROW_PEERS):
        out_ref[peer] = lines


def last_row_kernel(pos_ref, columns_ref, expd_ref, total_ref, out_ref, scale_ref, partial_ref):
    row_kernel(pos_ref, columns_ref, expd_ref, out_ref.at[:, 0], scale_ref, partial_ref)
    for peer in range(ROW_PEERS):
        out_ref[peer, 1] = total_ref[...]


def column_kernel(pos_ref, sums_ref, expd_ref, out_ref, scale_ref):
    scale_b = 1.0 / (BATCH * jnp.sum(sums_ref[...], axis=0))
    for j in range(HELD // 128):
        scale_ref[j * 128 : (j + 1) * 128, :] = jnp.broadcast_to(scale_b[j : j + 1, :], (128, 128)).T

    def step(i, totals):
        at = pl.ds(pl.multiple_of(i * 8, 8), 8)
        scale = scale_ref[at, :]
        return tuple(
            totals[4 * block + j] + expd_ref[block, at, 128 * j : 128 * j + 128] * scale
            for block in range(GROUP)
            for j in range(4)
        )

    zero = jnp.zeros((8, 128), jnp.float32)
    totals = lax.fori_loop(0, HELD // 8, step, (zero,) * (4 * GROUP), unroll=4)
    columns = [
        jnp.sum(jnp.concatenate(totals[4 * block : 4 * block + 4], axis=1), axis=0, keepdims=True)
        for block in range(GROUP)
    ]
    copies_of_columns(pos_ref, columns, out_ref)


def total_kernel(rows_ref, *refs):
    shelves, (out_ref, partial_ref) = refs[:GROUP], refs[GROUP:]
    partial_ref[...] = jnp.zeros_like(partial_ref)
    for block in range(GROUP):
        shelf = shelves[block][...]
        for at in range(0, HELD, 256):
            tile = jnp.exp2(contract_last(rows_of(rows_ref, 1, at, 256), shelf) * SECOND_SCALE)
            partial_ref[at : at + 256, :] += sum(tile[:, lane : lane + 128] for lane in range(0, OWNED, 128))
    out_ref[...] = rows_as_lanes(partial_ref)


def scales_kernel(sums_ref, out_ref):
    sums = jnp.sum(sums_ref[...], axis=0)
    scale_b = GRAD_SCALE / sums[0]
    scale_z = GRAD_SCALE / sums[1]
    for peer in range(out_ref.shape[0]):
        out_ref[peer, 0] = scale_b
        out_ref[peer, 1] = scale_z


def grad_kernel(half, pos_ref, scales_ref, columns_ref, book_ref, *refs):
    pieces, (out_ref, scale_ref, grads_ref) = refs[:5], refs[5:]
    scale_a = 1.0 / (K * jnp.sum(columns_ref[...], axis=0))
    line = lax.broadcasted_iota(jnp.int32, (GROUP, OWNED), 0)
    picked = jnp.sum(jnp.where(line == place_of(pos_ref, 4 * half), scale_a, 0.0), axis=0, keepdims=True)
    for j in range(OWNED // 128):
        scale_ref[j * 128 : (j + 1) * 128, :] = jnp.broadcast_to(
            picked[:, j * 128 : (j + 1) * 128], (128, 128)
        ).T
    book = book_ref[...]

    def view(block, number, at):
        if block != 2:
            return rows_of(pieces[(0, 1, None, 2)[block]], number, at, 256)
        return rows_of(pieces[3 + at // (HELD // 2)], number, at % (HELD // 2), 256)

    for block in range(4):
        place = (pos_ref[1] + block) % 4
        scale_b, scale_z = scales_ref[place, 0], scales_ref[place, 1]
        for at in range(0, HELD, 256):
            two = view(block, 1, at)
            codes = jnp.exp2(contract_last(book, view(block, 0, at)) * FIRST_SCALE)
            probs = jnp.exp2(contract_last(book, two) * SECOND_SCALE)
            tiles = []
            for j in range(0, 256, 128):
                row = (at + j) // 128
                tiles.append(
                    (
                        probs[:, j : j + 128] * scale_z[row : row + 1, :]
                        - codes[:, j : j + 128] * scale_ref[...] * scale_b[row : row + 1, :]
                    ).astype(jnp.bfloat16)
                )
            part = jnp.dot(jnp.concatenate(tiles, axis=1), two, preferred_element_type=jnp.float32)
            if block == 0 and at == 0:
                grads_ref[...] = part
            else:
                grads_ref[...] += part
    out_ref[...] = grads_ref[...]


def update_kernel(
    own_ref, other_ref, proto_ref, first_ref, second_ref, new_proto_ref, new_first_ref, new_second_ref, grad_ref
):
    grad = own_ref[...] + other_ref[...]
    new_first = 0.9 * first_ref[0] + 0.1 * grad
    new_second = 0.95 * second_ref[0] + 0.05 * grad * grad
    grad_ref[0] = grad
    new_first_ref[0] = new_first
    new_second_ref[0] = new_second
    new_proto_ref[0] = normalize(proto_ref[0]) - 0.05 * new_first / (jnp.sqrt(new_second) + 1e-08)


def params(mib):
    return pltpu.CompilerParams(vmem_limit_bytes=mib * MIB)


def f32(*shape):
    return jax.ShapeDtypeStruct(shape, jnp.float32)


def bf16(*shape):
    return jax.ShapeDtypeStruct(shape, jnp.bfloat16)


def cost(elements, size):
    return pl.CostEstimate(flops=2 * elements * D, bytes_accessed=size, transcendentals=elements)


def body(view_one, view_two, prototypes, moment_first, moment_second):
    core, along_y = lax.axis_index("c"), lax.axis_index("y")
    pos = jnp.stack([core, along_y]).astype(jnp.int32)
    groups = lax.axis_size("xh") * lax.axis_size("z")

    def exchange(copies, axes):
        return lax.all_to_all(copies, axes, 0, 0, tiled=True)

    def from_y(values, distance):
        return lax.ppermute(values, "y", [((i + distance) % 4, i) for i in range(4)])

    def from_core(values):
        return lax.ppermute(values, "c", [(0, 1), (1, 0)])

    book = pl.pallas_call(
        book_kernel,
        out_shape=bf16(OWNED, D),
        in_specs=[VMEM],
        out_specs=VMEM,
        compiler_params=params(8),
        name="book",
    )(prototypes)
    shelves = [book] + [from_y(book, k) for k in range(1, 4)]
    view_one, view_two, _ = lax.optimization_barrier((view_one, view_two, book))
    share = pl.pallas_call(
        views_kernel,
        out_shape=bf16(groups, 2, PART, D),
        grid_spec=pltpu.PrefetchScalarGridSpec(
            num_scalar_prefetch=1,
            grid=(1,),
            in_specs=[pl.BlockSpec((PART, D), lambda i, p: (p[1], 0))] * 2,
            out_specs=VMEM,
        ),
        compiler_params=params(8),
        name="views",
    )(pos, view_one, view_two)
    own_rows = exchange(share, ("xh", "z"))
    *shelves, own_rows = lax.optimization_barrier((*shelves, own_rows))
    shelves += [from_core(shelf) for shelf in shelves]

    total = pl.pallas_call(
        total_kernel,
        out_shape=f32(8, 128),
        in_specs=[VMEM] * (1 + GROUP),
        out_specs=VMEM,
        scratch_shapes=[pltpu.VMEM((HELD, 128), jnp.float32)],
        compiler_params=params(8),
        cost_estimate=cost(HELD * GROUP * OWNED, 3 * MIB),
        name="totals",
    )(own_rows, *shelves)
    *shelves, total = lax.optimization_barrier((*shelves, total))
    expd, copies = pl.pallas_call(
        expo_kernel,
        out_shape=(f32(GROUP, HELD, OWNED), f32(GROUP, GROUP, OWNED)),
        in_specs=[SMEM] + [VMEM] * (1 + GROUP),
        out_specs=(VMEM, VMEM),
        compiler_params=params(8),
        name="expo",
    )(pos, own_rows, *shelves)
    columns = exchange(copies, ("c", "y"))
    sent, columns = lax.optimization_barrier((own_rows, columns))
    after, before = from_y(sent, 1), from_y(sent, -1)
    row_scratch = [pltpu.VMEM((GROUP, 8, OWNED), jnp.float32), pltpu.VMEM((HELD, 128), jnp.float32)]
    assert ITERS == 3
    for step in range(ITERS - 1):
        copies = pl.pallas_call(
            row_kernel,
            out_shape=f32(ROW_PEERS, 8, 128),
            in_specs=[SMEM, VMEM, VMEM],
            out_specs=VMEM,
            scratch_shapes=row_scratch,
            compiler_params=params(8),
            name="row_sums",
        )(pos, columns, expd)
        sums = exchange(copies, ("xh", "z", "xl"))
        copies = pl.pallas_call(
            column_kernel,
            out_shape=f32(GROUP, GROUP, OWNED),
            in_specs=[SMEM, VMEM, VMEM],
            out_specs=VMEM,
            scratch_shapes=[pltpu.VMEM((HELD, 128), jnp.float32)],
            compiler_params=params(8),
            name="column_sums",
        )(pos, sums, expd)
        if step == 0:
            after, before, copies = lax.optimization_barrier((after, before, copies))
        else:
            far_low, far_high, copies = lax.optimization_barrier((far_low, far_high, copies))
        columns = exchange(copies, ("c", "y"))
        if step == 0:
            after, before, columns = lax.optimization_barrier((after, before, columns))
            far_low, far_high = from_y(after[: groups // 2], 1), from_y(before[groups // 2 :], -1)
    copies = pl.pallas_call(
        last_row_kernel,
        out_shape=f32(ROW_PEERS, 2, 8, 128),
        in_specs=[SMEM, VMEM, VMEM, VMEM],
        out_specs=VMEM,
        scratch_shapes=row_scratch,
        compiler_params=params(8),
        name="last_row_sums",
    )(pos, columns, expd, total)
    sums = exchange(copies, ("xh", "z", "xl"))
    copies = pl.pallas_call(
        scales_kernel,
        out_shape=f32(4, 2, 8, 128),
        in_specs=[VMEM],
        out_specs=VMEM,
        compiler_params=params(8),
        name="scales",
    )(sums)
    scales = exchange(copies, ("y",))

    def grad_of(half):
        return pl.pallas_call(
            functools.partial(grad_kernel, half),
            out_shape=f32(OWNED, D),
            in_specs=[SMEM] + [VMEM] * 8,
            out_specs=VMEM,
            scratch_shapes=[pltpu.VMEM((OWNED, 128), jnp.float32), pltpu.VMEM((OWNED, D), jnp.float32)],
            compiler_params=params(8),
            cost_estimate=cost(3 * 4 * HELD * OWNED, 6 * MIB),
            name="grad_of_own" if half == 0 else "grad_of_other",
        )(pos, scales, columns, shelves[4 * half], own_rows, after, before, far_low, far_high)

    away = grad_of(1)
    scales, away = lax.optimization_barrier((scales, away))
    own, other = grad_of(0), from_core(away)
    block = pl.BlockSpec((1, OWNED // 2, D), lambda i: (0, i, 0))
    return pl.pallas_call(
        update_kernel,
        out_shape=(f32(1, OWNED, D),) * 4,
        grid=(2,),
        in_specs=[pl.BlockSpec((OWNED // 2, D), lambda i: (i, 0))] * 2 + [block] * 3,
        out_specs=(block,) * 4,
        compiler_params=params(16),
        name="update",
    )(own, other, prototypes, moment_first, moment_second)


def solution(mesh):
    fine = Mesh(mesh.devices.reshape(2, 8, 2, 4, 2), ("xh", "z", "c", "y", "xl"))
    dp, proto = ("xh", "z", "c"), ("y", "xl")
    owned = P(proto, dp, None)
    return jax.shard_map(
        body,
        mesh=fine,
        in_specs=(P(dp, None), P(dp, None), owned, owned, owned),
        out_specs=(owned, owned, owned, owned),
        check_vma=False,
    )
```

time: 1170 us -> 171 us (0.15)
  waiting for transfers between devices: 1000 us -> 27.6 us
  other arithmetic: 63.7 us -> 0.08 us
  blocking collectives: 45.2 us -> 81 us
  matrix products: 34.2 us -> 0 us
  Pallas kernels: 0 us -> 29.7 us
  starting transfers between devices: 0.21 us -> 28.5 us
  between operations: 13.8 us -> 0.79 us
    psum x3 -> x0, waiting for transfers between devices: 687 us -> none  [body(): lax.psum(jnp.sum(expd * scale_b[:, None], axis=0), 'dp')]
    reduce_scatter x1 -> x0, waiting for transfers between devices: 214 us -> none  [body(): lax.psum_scatter(contract_first(grads_in, second_rows), 'dp', scatter_dim...]
    all_gather x1 -> x0, waiting for transfers between devices: 103 us -> none  [body(): lax.all_gather(book[None], 'dp', axis=1, tiled=True)[0]]
    all_to_all x0 -> x7, blocking collectives: none -> 81 us  [exchange(): return lax.all_to_all(copies, axes, 0, 0, tiled=True)]
    reduce_sum x9 -> x0, other arithmetic: 55.6 us -> none  [the longest x3 25.2 us: body(): jnp.sum(expd * scale_b[:, None], axis=0)]
    psum x3 -> x0, blocking collectives: 45.2 us -> none  [body(): lax.psum(jnp.sum(expd * scale_a[None, :], axis=1), 'proto')]
    dot_general x2 -> x0, matrix products: 34.2 us -> none  [the longest x1 17.6 us: contract_first(): lax.dot_general(left, right, (((0,), (0,)), ((), ())), preferred_element_...]
    pallas_call x0 -> x13, Pallas kernels: none -> 29.7 us  [the longest x2 8.75 us: grad_of(): pl.pallas_call(functools.partial(grad_kernel, half), out_shape=f32(OWNED,...]
  transfers between devices with their start and end apart: 5 -> 13, of which waited for: 5 -> 8; matrix products, arithmetic and copies ran while one was open for 0% -> 0% of each run, Pallas kernels for 0% -> 8%
where the time goes in v2:
time: 171 us
  blocking collectives  81 us (47%)
  Pallas kernels  29.7 us (17%)
  starting transfers between devices  28.5 us (17%)
  waiting for transfers between devices  27.6 us (16%)
  local copies, waits for them, and re-layouts  2.93 us (2%)
    all_to_all x7, blocking collectives, exchange(): return lax.all_to_all(copies, axes, 0, 0, tiled=True)  81 us
    ppermute x7, waiting for transfers between devices, from_y(): lax.ppermute(values, 'y', [((i + distance) % 4, i) for i in range(4)])  13.9 us
    all_to_all x1, waiting for transfers between devices, exchange(): return lax.all_to_all(copies, axes, 0, 0, tiled=True)  11.9 us
    all_to_all x1, starting transfers between devices, exchange(): return lax.all_to_all(copies, axes, 0, 0, tiled=True)  11.6 us
    ppermute x7, starting transfers between devices, from_y(): lax.ppermute(values, 'y', [((i + distance) % 4, i) for i in range(4)])  10.5 us
    pallas_call x2, Pallas kernels, grad_of(): pl.pallas_call(functools.partial(grad_kernel, half), out_shape=f32(OWNED,...  8.75 us
    ppermute x5, starting transfers between devices, from_core(): return lax.ppermute(values, 'c', [(0, 1), (1, 0)])  6.45 us
    pallas_call x2, Pallas kernels, body(): pl.pallas_call(row_kernel, out_shape=f32(ROW_PEERS, 8, 128), in_specs=[SM...  5.06 us
  transfers between devices with their start and end apart: 13, of which 8 were waited for; matrix products, arithmetic and copies ran while one was open for 0% of the time, Pallas kernels for 8%

profile of v2, /device:TPU:1, one launch (start us, length us, event | category | flops | bytes accessed | tf_op | source)
XLA Modules:
  0.0 170.6 jit_solution(10177473382623727450)
XLA Ops:
  0.6 0.0 copy-start
  0.6 1.0 copy-done
  1.7 0.2 book.1.refs_0_.book_ref
  1.9 0.1 pad_add_fusion.pos_ref
  2.0 0.0 copy-start.4
  2.0 0.9 copy-done.4
  2.9 0.0 copy-start.5
  2.9 0.9 copy-done.5
  3.8 1.7 %views.1 = bf16[16,2,64,256]{3,2,1,0:T(8,128)(2,1)} custom-call(s32[2]{0:T(128)S(1)} %pad_add_fusion.pos_ref, bf16[256,256]{1,0:T(8,128)(2,1)S(1)} %copy-done.4, bf16[256,256]{1,0:T(8,128)(2,1)S(1)} %copy-done.5), custom_call_target="tpu_custom_call" | custom-call | tf_op jit(solution)/shard_map/views/pallas_call | solution.py:256
  5.5 11.6 %all-to-all-start = ((bf16[16,2,64,256]{3,2,1,0:T(8,128)(2,1)}), bf16[16,2,64,256]{3,2,1,0:T(8,128)(2,1)S(1)}, u32[]{:S(2)}, u32[]{:S(2)}) async-start(bf16[16,2,64,256]{3,2,1,0:T(8,128)(2,1)} %views.1), calls=%async_computation | async-start | bytes 2097152 | tf_op jit(solution)/shard_map/all_to_all | solution.py:238
  17.1 1.4 collective-permute-start.2
  18.5 2.6 %collective-permute-start.1 = (bf16[512,256]{1,0:T(8,128)(2,1)S(1)}, bf16[512,256]{1,0:T(8,128)(2,1)S(1)}, u32[]{:S(2)}, u32[]{:S(2)}) collective-permute-start(bf16[512,256]{1,0:T(8,128)(2,1)S(1)} %book.1.refs_0_.book_ref), channel_id=1, source_target_pairs={{4,0},{6,2},{0,4},{2,6},{5,1},{7,3},{1,5},{3,7},{12,8},{14,10},{8,... | collective-permute-start | bytes 786440 | tf_op jit(solution)/shard_map/ppermute | solution.py:241
  21.1 1.1 collective-permute-start
  22.1 3.2 %collective-permute-done.2.refs_3_ = bf16[512,256]{1,0:T(8,128)(2,1)S(1)} collective-permute-done((bf16[512,256]{1,0:T(8,128)(2,1)S(1)}, bf16[512,256]{1,0:T(8,128)(2,1)S(1)}, u32[]{:S(2)}, u32[]{:S(2)}) %collective-permute-start.2) | collective-permute-done | bytes 262176 | tf_op jit(solution)/shard_map/ppermute | solution.py:241
  25.4 6.7 %collective-permute-done.1.refs_2_ = bf16[512,256]{1,0:T(8,128)(2,1)S(1)} collective-permute-done((bf16[512,256]{1,0:T(8,128)(2,1)S(1)}, bf16[512,256]{1,0:T(8,128)(2,1)S(1)}, u32[]{:S(2)}, u32[]{:S(2)}) %collective-permute-start.1) | collective-permute-done | bytes 262176 | tf_op jit(solution)/shard_map/ppermute | solution.py:241
  32.1 0.0 collective-permute-done.refs_1_
  32.1 11.9 %all-to-all-done.rows_ref.refs_0_ = bf16[16,2,64,256]{3,2,1,0:T(8,128)(2,1)S(1)} async-done(((bf16[16,2,64,256]{3,2,1,0:T(8,128)(2,1)}), bf16[16,2,64,256]{3,2,1,0:T(8,128)(2,1)S(1)}, u32[]{:S(2)}, u32[]{:S(2)}) %all-to-all-start) | async-done | bytes 1048608 | tf_op jit(solution)/shard_map/all_to_all | solution.py:238
  44.0 2.6 %collective-permute-start.3 = (bf16[512,256]{1,0:T(8,128)(2,1)S(1)}, bf16[512,256]{1,0:T(8,128)(2,1)S(1)}, u32[]{:S(2)}, u32[]{:S(2)}) collective-permute-start(bf16[512,256]{1,0:T(8,128)(2,1)S(1)} %book.1.refs_0_.book_ref), channel_id=1, source_target_pairs={{0,8},{8,0},{1,9},{9,1},{2,10},{10,2},{3,11},{11,3},{4,12},{12,4},... | collective-permute-start | bytes 786440 | tf_op jit(solution)/shard_map/ppermute | solution.py:244
  46.6 0.0 collective-permute-start.4
  46.6 0.5 collective-permute-start.5
  47.1 0.0 collective-permute-start.6
  47.1 0.6 collective-permute-done.3.refs_4_.book_ref
  47.8 0.4 collective-permute-done.4.refs_5_
  48.2 0.4 collective-permute-done.5.refs_6_
  48.5 0.4 collective-permute-done.6.refs_7_
  48.9 2.5 %totals.1.total_ref = f32[8,128]{1,0:T(8,128)S(1)} custom-call(bf16[16,2,64,256]{3,2,1,0:T(8,128)(2,1)S(1)} %all-to-all-done.rows_ref.refs_0_, bf16[512,256]{1,0:T(8,128)(2,1)S(1)} %book.1.refs_0_.book_ref, bf16[512,256]{1,0:T(8,128)(2,1)S(1)} %collective-permute-done.refs_1_, bf16[512,256]{1,0:T(8,128)(2,1)S(1)} %collective-permute-done.1.refs_2_, ...), custom_call_target="tpu_custom_call" | custom-call | flops 2147483648 | bytes 3145728 | tf_op jit(solution)/shard_map/totals/pallas_call | solution.py:272
  51.4 2.9 %expo.1 = (f32[8,1024,512]{2,1,0:T(8,128)S(1)}, f32[8,8,512]{2,1,0:T(8,128)S(1)}) custom-call(s32[2]{0:T(128)S(1)} %pad_add_fusion.pos_ref, bf16[16,2,64,256]{3,2,1,0:T(8,128)(2,1)S(1)} %all-to-all-done.rows_ref.refs_0_, bf16[512,256]{1,0:T(8,128)(2,1)S(1)} %book.1.refs_0_.book_ref, bf16[512,256]{1,0:T(8,128)(2,1)S(1)} %collective-permute-done.refs_1_, ...), custom_call_target="tpu_custom_call" | custom-call | tf_op jit(solution)/shard_map/expo/pallas_call | solution.py:283
  54.3 9.8 %all_to_all.40.columns_ref = f32[8,8,512]{2,1,0:T(8,128)S(1)} all-to-all(f32[8,8,512]{2,1,0:T(8,128)S(1)} %get-tuple-element.50), channel_id=1, replica_groups=mesh['xh'=2,'z'=8,'c'=2,'y'=4,'xl'=2] {'c','y'}, dimensions={0} | all-to-all | bytes 262144 | tf_op jit(solution)/shard_map/all_to_all | solution.py:238
  64.1 0.7 collective-permute-start.8
  64.8 2.0 %collective-permute-start.7 = (bf16[16,2,64,256]{3,2,1,0:T(8,128)(2,1)S(1)}, bf16[16,2,64,256]{3,2,1,0:T(8,128)(2,1)S(1)}, u32[]{:S(2)}, u32[]{:S(2)}) collective-permute-start(bf16[16,2,64,256]{3,2,1,0:T(8,128)(2,1)S(1)} %all-to-all-done.rows_ref.refs_0_), channel_id=1, source_target_pairs={{2,0},{4,2},{6,4},{0,6},{3,1},{5,3},{7,5},{1,7},{10,8},{12,10},{14... | collective-permute-start | bytes 3145736 | tf_op jit(solution)/shard_map/ppermute | solution.py:241
  66.8 2.5 %row_sums.2 = f32[32,8,128]{2,1,0:T(8,128)S(1)} custom-call(s32[2]{0:T(128)S(1)} %pad_add_fusion.pos_ref, f32[8,8,512]{2,1,0:T(8,128)S(1)} %all_to_all.40.columns_ref, f32[8,1024,512]{2,1,0:T(8,128)S(1)} %get-tuple-element.53.expd_ref), custom_call_target="tpu_custom_call" | custom-call | tf_op jit(solution)/shard_map/row_sums/pallas_call | solution.py:297
  69.4 14.2 %all_to_all.41.sums_ref = f32[32,8,128]{2,1,0:T(8,128)S(1)} all-to-all(f32[32,8,128]{2,1,0:T(8,128)S(1)} %row_sums.2), channel_id=1, replica_groups=mesh['xh'=2,'z'=8,'c'=2,'y'=4,'xl'=2] {'xh','z','xl'}, dimensions={0} | all-to-all | bytes 262144 | tf_op jit(solution)/shard_map/all_to_all | solution.py:238
  83.5 2.2 %column_sums.2 = f32[8,8,512]{2,1,0:T(8,128)S(1)} custom-call(s32[2]{0:T(128)S(1)} %pad_add_fusion.pos_ref, f32[32,8,128]{2,1,0:T(8,128)S(1)} %all_to_all.41.sums_ref, f32[8,1024,512]{2,1,0:T(8,128)S(1)} %get-tuple-element.53.expd_ref), custom_call_target="tpu_custom_call" | custom-call | tf_op jit(solution)/shard_map/column_sums/pallas_call | solution.py:307
  85.8 3.9 %collective-permute-done.8.refs_2_ = bf16[16,2,64,256]{3,2,1,0:T(8,128)(2,1)S(1)} collective-permute-done((bf16[16,2,64,256]{3,2,1,0:T(8,128)(2,1)S(1)}, bf16[16,2,64,256]{3,2,1,0:T(8,128)(2,1)S(1)}, u32[]{:S(2)}, u32[]{:S(2)}) %collective-permute-start.8) | collective-permute-done | bytes 1048608 | tf_op jit(solution)/shard_map/ppermute | solution.py:241
  89.7 0.0 collective-permute-done.7.refs_1_
  89.7 10.4 %all_to_all.42.columns_ref = f32[8,8,512]{2,1,0:T(8,128)S(1)} all-to-all(f32[8,8,512]{2,1,0:T(8,128)S(1)} %column_sums.2), channel_id=1, replica_groups=mesh['xh'=2,'z'=8,'c'=2,'y'=4,'xl'=2] {'c','y'}, dimensions={0} | all-to-all | bytes 262144 | tf_op jit(solution)/shard_map/all_to_all | solution.py:238
  100.2 0.8 collective-permute-start.10
  101.0 2.0 %collective-permute-start.9 = (bf16[8,2,64,256]{3,2,1,0:T(8,128)(2,1)S(1)}, bf16[8,2,64,256]{3,2,1,0:T(8,128)(2,1)S(1)}, u32[]{:S(2)}, u32[]{:S(2)}) collective-permute-start(bf16[8,2,64,256]{3,2,1,0:T(8,128)(2,1)S(1)} %slice.6), channel_id=1, source_target_pairs={{2,0},{4,2},{6,4},{0,6},{3,1},{5,3},{7,5},{1,7},{10,8},{12,10},{14... | collective-permute-start | bytes 1572872 | tf_op jit(solution)/shard_map/ppermute | solution.py:241
  102.9 2.5 %row_sums.3 = f32[32,8,128]{2,1,0:T(8,128)S(1)} custom-call(s32[2]{0:T(128)S(1)} %pad_add_fusion.pos_ref, f32[8,8,512]{2,1,0:T(8,128)S(1)} %all_to_all.42.columns_ref, f32[8,1024,512]{2,1,0:T(8,128)S(1)} %get-tuple-element.53.expd_ref), custom_call_target="tpu_custom_call" | custom-call | tf_op jit(solution)/shard_map/row_sums/pallas_call | solution.py:297
  105.5 14.2 %all_to_all.43.sums_ref = f32[32,8,128]{2,1,0:T(8,128)S(1)} all-to-all(f32[32,8,128]{2,1,0:T(8,128)S(1)} %row_sums.3), channel_id=1, replica_groups=mesh['xh'=2,'z'=8,'c'=2,'y'=4,'xl'=2] {'xh','z','xl'}, dimensions={0} | all-to-all | bytes 262144 | tf_op jit(solution)/shard_map/all_to_all | solution.py:238
  119.7 2.2 %column_sums.3 = f32[8,8,512]{2,1,0:T(8,128)S(1)} custom-call(s32[2]{0:T(128)S(1)} %pad_add_fusion.pos_ref, f32[32,8,128]{2,1,0:T(8,128)S(1)} %all_to_all.43.sums_ref, f32[8,1024,512]{2,1,0:T(8,128)S(1)} %get-tuple-element.53.expd_ref), custom_call_target="tpu_custom_call" | custom-call | tf_op jit(solution)/shard_map/column_sums/pallas_call | solution.py:307
  121.9 0.0 collective-permute-done.10.refs_4_
  121.9 0.0 collective-permute-done.9.refs_3_
  121.9 9.9 %all_to_all.44.columns_ref = f32[8,8,512]{2,1,0:T(8,128)S(1)} all-to-all(f32[8,8,512]{2,1,0:T(8,128)S(1)} %column_sums.3), channel_id=1, replica_groups=mesh['xh'=2,'z'=8,'c'=2,'y'=4,'xl'=2] {'c','y'}, dimensions={0} | all-to-all | bytes 262144 | tf_op jit(solution)/shard_map/all_to_all | solution.py:238
  131.8 0.0 copy-start.1
  131.8 0.0 copy-start.2
  131.8 0.0 copy-start.3
  131.8 2.5 %last_row_sums.1 = f32[32,2,8,128]{3,2,1,0:T(8,128)S(1)} custom-call(s32[2]{0:T(128)S(1)} %pad_add_fusion.pos_ref, f32[8,8,512]{2,1,0:T(8,128)S(1)} %all_to_all.44.columns_ref, f32[8,1024,512]{2,1,0:T(8,128)S(1)} %get-tuple-element.53.expd_ref, f32[8,128]{1,0:T(8,128)S(1)} %totals.1.total_ref), custom_call_target="tpu_custom_call" | custom-call | tf_op jit(solution)/shard_map/last_row_sums/pallas_call | solution.py:324
  134.4 15.9 %all_to_all.45.sums_ref = f32[32,2,8,128]{3,2,1,0:T(8,128)S(1)} all-to-all(f32[32,2,8,128]{3,2,1,0:T(8,128)S(1)} %last_row_sums.1), channel_id=1, replica_groups=mesh['xh'=2,'z'=8,'c'=2,'y'=4,'xl'=2] {'xh','z','xl'}, dimensions={0} | all-to-all | bytes 524288 | tf_op jit(solution)/shard_map/all_to_all | solution.py:238
  150.2 6.7 %all_to_all.46.scales_ref = f32[4,2,8,128]{3,2,1,0:T(8,128)S(1)} all-to-all(f32[4,2,8,128]{3,2,1,0:T(8,128)S(1)} %scales.1), channel_id=1, replica_groups=mesh['xh'=2,'z'=8,'c'=2,'y'=4,'xl'=2] {'y'}, dimensions={0} | all-to-all | bytes 65536 | tf_op jit(solution)/shard_map/all_to_all | solution.py:238
  156.9 4.4 %grad_of_other.1 = f32[512,256]{1,0:T(8,128)S(1)} custom-call(s32[2]{0:T(128)S(1)} %pad_add_fusion.pos_ref, f32[4,2,8,128]{3,2,1,0:T(8,128)S(1)} %all_to_all.46.scales_ref, f32[8,8,512]{2,1,0:T(8,128)S(1)} %all_to_all.44.columns_ref, bf16[512,256]{1,0:T(8,128)(2,1)S(1)} %collective-permute-done.3.refs_4_.book_ref, ...), custom_call_target="tpu_custom_call" | custom-call | flops 3221225472 | bytes 6291456 | tf_op jit(solution)/shard_map/grad_of_other/pallas_call | solution.py:345
  161.3 3.3 %collective-permute-start.11 = (f32[512,256]{1,0:T(8,128)S(1)}, f32[512,256]{1,0:T(8,128)S(1)}, u32[]{:S(2)}, u32[]{:S(2)}) collective-permute-start(f32[512,256]{1,0:T(8,128)S(1)} %grad_of_other.1), channel_id=1, source_target_pairs={{0,8},{8,0},{1,9},{9,1},{2,10},{10,2},{3,11},{11,3},{4,12},{12,4},... | collective-permute-start | bytes 1572872 | tf_op jit(solution)/shard_map/ppermute | solution.py:244
  164.6 4.4 %grad_of_own.1.own_ref = f32[512,256]{1,0:T(8,128)S(1)} custom-call(s32[2]{0:T(128)S(1)} %pad_add_fusion.pos_ref, f32[4,2,8,128]{3,2,1,0:T(8,128)S(1)} %all_to_all.46.scales_ref, f32[8,8,512]{2,1,0:T(8,128)S(1)} %all_to_all.44.columns_ref, bf16[512,256]{1,0:T(8,128)(2,1)S(1)} %book.1.refs_0_.book_ref, ...), custom_call_target="tpu_custom_call" | custom-call | flops 3221225472 | bytes 6291456 | tf_op jit(solution)/shard_map/grad_of_own/pallas_call | solution.py:345
  169.0 0.0 collective-permute-done.11.other_ref
  169.0 0.0 copy-done.1
  169.0 0.0 copy-done.2
  169.0 0.0 copy-done.3
  169.0 1.6 update.1
  (3 shorter events, 0.1 us)
Async XLA Ops:
  0.6 1.0 copy-start
  2.0 0.9 copy-start.4
  2.9 0.9 copy-start.5
  5.5 38.5 %all-to-all-start = ((bf16[16,2,64,256]{3,2,1,0:T(8,128)(2,1)}), bf16[16,2,64,256]{3,2,1,0:T(8,128)(2,1)S(1)}, u32[]{:S(2)}, u32[]{:S(2)}) async-start(bf16[16,2,64,256]{3,2,1,0:T(8,128)(2,1)} %views.1), calls=%async_computation | async-start | bytes 2097152 | tf_op jit(solution)/shard_map/all_to_all | solution.py:238
  17.1 8.3 %collective-permute-start.2 = (bf16[512,256]{1,0:T(8,128)(2,1)S(1)}, bf16[512,256]{1,0:T(8,128)(2,1)S(1)}, u32[]{:S(2)}, u32[]{:S(2)}) collective-permute-start(bf16[512,256]{1,0:T(8,128)(2,1)S(1)} %book.1.refs_0_.book_ref), channel_id=1, source_target_pairs={{6,0},{0,2},{2,4},{4,6},{7,1},{1,3},{3,5},{5,7},{14,8},{8,10},{10,... | collective-permute-start | bytes 786440 | tf_op jit(solution)/shard_map/ppermute | solution.py:241
  18.5 13.6 %collective-permute-start.1 = (bf16[512,256]{1,0:T(8,128)(2,1)S(1)}, bf16[512,256]{1,0:T(8,128)(2,1)S(1)}, u32[]{:S(2)}, u32[]{:S(2)}) collective-permute-start(bf16[512,256]{1,0:T(8,128)(2,1)S(1)} %book.1.refs_0_.book_ref), channel_id=1, source_target_pairs={{4,0},{6,2},{0,4},{2,6},{5,1},{7,3},{1,5},{3,7},{12,8},{14,10},{8,... | collective-permute-start | bytes 786440 | tf_op jit(solution)/shard_map/ppermute | solution.py:241
  21.1 11.0 %collective-permute-start = (bf16[512,256]{1,0:T(8,128)(2,1)S(1)}, bf16[512,256]{1,0:T(8,128)(2,1)S(1)}, u32[]{:S(2)}, u32[]{:S(2)}) collective-permute-start(bf16[512,256]{1,0:T(8,128)(2,1)S(1)} %book.1.refs_0_.book_ref), channel_id=1, source_target_pairs={{2,0},{4,2},{6,4},{0,6},{3,1},{5,3},{7,5},{1,7},{10,8},{12,10},{14... | collective-permute-start | bytes 786440 | tf_op jit(solution)/shard_map/ppermute | solution.py:241
  44.0 3.8 %collective-permute-start.3 = (bf16[512,256]{1,0:T(8,128)(2,1)S(1)}, bf16[512,256]{1,0:T(8,128)(2,1)S(1)}, u32[]{:S(2)}, u32[]{:S(2)}) collective-permute-start(bf16[512,256]{1,0:T(8,128)(2,1)S(1)} %book.1.refs_0_.book_ref), channel_id=1, source_target_pairs={{0,8},{8,0},{1,9},{9,1},{2,10},{10,2},{3,11},{11,3},{4,12},{12,4},... | collective-permute-start | bytes 786440 | tf_op jit(solution)/shard_map/ppermute | solution.py:244
  46.6 1.5 collective-permute-start.4
  46.6 1.9 %collective-permute-start.5 = (bf16[512,256]{1,0:T(8,128)(2,1)S(1)}, bf16[512,256]{1,0:T(8,128)(2,1)S(1)}, u32[]{:S(2)}, u32[]{:S(2)}) collective-permute-start(bf16[512,256]{1,0:T(8,128)(2,1)S(1)} %collective-permute-done.1.refs_2_), channel_id=1, source_target_pairs={{0,8},{8,0},{1,9},{9,1},{2,10},{10,2},{3,11},{11,3},{4,12},{12,4},... | collective-permute-start | bytes 786440 | tf_op jit(solution)/shard_map/ppermute | solution.py:244
  47.1 1.8 %collective-permute-start.6 = (bf16[512,256]{1,0:T(8,128)(2,1)S(1)}, bf16[512,256]{1,0:T(8,128)(2,1)S(1)}, u32[]{:S(2)}, u32[]{:S(2)}) collective-permute-start(bf16[512,256]{1,0:T(8,128)(2,1)S(1)} %collective-permute-done.2.refs_3_), channel_id=1, source_target_pairs={{0,8},{8,0},{1,9},{9,1},{2,10},{10,2},{3,11},{11,3},{4,12},{12,4},... | collective-permute-start | bytes 786440 | tf_op jit(solution)/shard_map/ppermute | solution.py:244
  64.1 25.6 %collective-permute-start.8 = (bf16[16,2,64,256]{3,2,1,0:T(8,128)(2,1)S(1)}, bf16[16,2,64,256]{3,2,1,0:T(8,128)(2,1)S(1)}, u32[]{:S(2)}, u32[]{:S(2)}) collective-permute-start(bf16[16,2,64,256]{3,2,1,0:T(8,128)(2,1)S(1)} %all-to-all-done.rows_ref.refs_0_), channel_id=1, source_target_pairs={{6,0},{0,2},{2,4},{4,6},{7,1},{1,3},{3,5},{5,7},{14,8},{8,10},{10,... | collective-permute-start | bytes 3145736 | tf_op jit(solution)/shard_map/ppermute | solution.py:241
  64.8 24.9 %collective-permute-start.7 = (bf16[16,2,64,256]{3,2,1,0:T(8,128)(2,1)S(1)}, bf16[16,2,64,256]{3,2,1,0:T(8,128)(2,1)S(1)}, u32[]{:S(2)}, u32[]{:S(2)}) collective-permute-start(bf16[16,2,64,256]{3,2,1,0:T(8,128)(2,1)S(1)} %all-to-all-done.rows_ref.refs_0_), channel_id=1, source_target_pairs={{2,0},{4,2},{6,4},{0,6},{3,1},{5,3},{7,5},{1,7},{10,8},{12,10},{14... | collective-permute-start | bytes 3145736 | tf_op jit(solution)/shard_map/ppermute | solution.py:241
  100.2 21.7 %collective-permute-start.10 = (bf16[8,2,64,256]{3,2,1,0:T(8,128)(2,1)S(1)}, bf16[8,2,64,256]{3,2,1,0:T(8,128)(2,1)S(1)}, u32[]{:S(2)}, u32[]{:S(2)}) collective-permute-start(bf16[8,2,64,256]{3,2,1,0:T(8,128)(2,1)S(1)} %slice.7), channel_id=1, source_target_pairs={{6,0},{0,2},{2,4},{4,6},{7,1},{1,3},{3,5},{5,7},{14,8},{8,10},{10,... | collective-permute-start | bytes 1572872 | tf_op jit(solution)/shard_map/ppermute | solution.py:241
  101.0 20.9 %collective-permute-start.9 = (bf16[8,2,64,256]{3,2,1,0:T(8,128)(2,1)S(1)}, bf16[8,2,64,256]{3,2,1,0:T(8,128)(2,1)S(1)}, u32[]{:S(2)}, u32[]{:S(2)}) collective-permute-start(bf16[8,2,64,256]{3,2,1,0:T(8,128)(2,1)S(1)} %slice.6), channel_id=1, source_target_pairs={{2,0},{4,2},{6,4},{0,6},{3,1},{5,3},{7,5},{1,7},{10,8},{12,10},{14... | collective-permute-start | bytes 1572872 | tf_op jit(solution)/shard_map/ppermute | solution.py:241
  131.8 37.2 %copy-start.1 = (f32[1,512,256]{2,1,0:T(8,128)S(1)}, f32[1,512,256]{2,1,0:T(8,128)}, u32[]{:S(2)}) copy-start(f32[1,512,256]{2,1,0:T(8,128)} %proto_ref.3) | copy-start | bytes 1572868
  131.8 37.2 %copy-start.2 = (f32[1,512,256]{2,1,0:T(8,128)S(1)}, f32[1,512,256]{2,1,0:T(8,128)}, u32[]{:S(2)}) copy-start(f32[1,512,256]{2,1,0:T(8,128)} %first_ref.1) | copy-start | bytes 1572868
  131.8 37.2 %copy-start.3 = (f32[1,512,256]{2,1,0:T(8,128)S(1)}, f32[1,512,256]{2,1,0:T(8,128)}, u32[]{:S(2)}) copy-start(f32[1,512,256]{2,1,0:T(8,128)} %second_ref.1) | copy-start | bytes 1572868
  161.3 7.7 %collective-permute-start.11 = (f32[512,256]{1,0:T(8,128)S(1)}, f32[512,256]{1,0:T(8,128)S(1)}, u32[]{:S(2)}, u32[]{:S(2)}) collective-permute-start(f32[512,256]{1,0:T(8,128)S(1)} %grad_of_other.1), channel_id=1, source_target_pairs={{0,8},{8,0},{1,9},{9,1},{2,10},{10,2},{3,11},{11,3},{4,12},{12,4},... | collective-permute-start | bytes 1572872 | tf_op jit(solution)/shard_map/ppermute | solution.py:244

commit v3 on v2

--- a/solution.py
+++ b/solution.py
@@ -13,7 +13,8 @@
 D = 256
 OWNED = 512
 HELD = 1024
-PART = 64
+PART = 32
+PLANES = 8
 GROUP = 8
 BATCH = 8192
 ROW_PEERS = 32
@@ -55,8 +56,8 @@
             share_ref[peer, view] = rows
 
 
-def rows_of(rows_ref, view, at, count):
-    return rows_ref[at // PART : (at + count) // PART, view].reshape(count, D)
+def rows_of(rows_ref, view, at):
+    return rows_ref[at // 256, :, view].reshape(256, D)
 
 
 def copies_of_columns(pos_ref, columns, out_ref):
@@ -75,7 +76,7 @@
         shelf = shelves[block][...]
         total = jnp.zeros((8, OWNED), jnp.float32)
         for at in range(0, HELD, 256):
-            tile = jnp.exp2(contract_last(rows_of(rows_ref, 0, at, 256), shelf) * FIRST_SCALE)
+            tile = jnp.exp2(contract_last(rows_of(rows_ref, 0, at), shelf) * FIRST_SCALE)
             expd_ref[block, at : at + 256, :] = tile
             total = total + jnp.sum(tile.reshape(32, 8, OWNED), axis=0)
         columns.append(jnp.sum(total, axis=0, keepdims=True))
@@ -106,7 +107,7 @@
         partial_ref[at, :] = total.reshape(64, 128)
         return carry
 
-    lax.fori_loop(0, HELD // 64, step, 0)
+    lax.fori_loop(0, HELD // 64, step, 0, unroll=16)
     lines = rows_as_lanes(partial_ref)
     for peer in range(ROW_PEERS):
         out_ref[peer] = lines
@@ -133,7 +134,7 @@
         )
 
     zero = jnp.zeros((8, 128), jnp.float32)
-    totals = lax.fori_loop(0, HELD // 8, step, (zero,) * (4 * GROUP), unroll=4)
+    totals = lax.fori_loop(0, HELD // 8, step, (zero,) * (4 * GROUP), unroll=16)
     columns = [
         jnp.sum(jnp.concatenate(totals[4 * block : 4 * block + 4], axis=1), axis=0, keepdims=True)
         for block in range(GROUP)
@@ -147,7 +148,7 @@
     for block in range(GROUP):
         shelf = shelves[block][...]
         for at in range(0, HELD, 256):
-            tile = jnp.exp2(contract_last(rows_of(rows_ref, 1, at, 256), shelf) * SECOND_SCALE)
+            tile = jnp.exp2(contract_last(rows_of(rows_ref, 1, at), shelf) * SECOND_SCALE)
             partial_ref[at : at + 256, :] += sum(tile[:, lane : lane + 128] for lane in range(0, OWNED, 128))
     out_ref[...] = rows_as_lanes(partial_ref)
 
@@ -174,8 +175,8 @@
 
     def view(block, number, at):
         if block != 2:
-            return rows_of(pieces[(0, 1, None, 2)[block]], number, at, 256)
-        return rows_of(pieces[3 + at // (HELD // 2)], number, at % (HELD // 2), 256)
+            return rows_of(pieces[(0, 1, None, 2)[block]], number, at)
+        return rows_of(pieces[3 + at // (HELD // 2)], number, at % (HELD // 2))
 
     for block in range(4):
         place = (pos_ref[1] + block) % 4
@@ -230,9 +231,7 @@
 
 
 def body(view_one, view_two, prototypes, moment_first, moment_second):
-    core, along_y = lax.axis_index("c"), lax.axis_index("y")
-    pos = jnp.stack([core, along_y]).astype(jnp.int32)
-    groups = lax.axis_size("xh") * lax.axis_size("z")
+    pos = jnp.stack([lax.axis_index(name) for name in ("c", "y", "xl")]).astype(jnp.int32)
 
     def exchange(copies, axes):
         return lax.all_to_all(copies, axes, 0, 0, tiled=True)
@@ -251,23 +250,23 @@
         compiler_params=params(8),
         name="book",
     )(prototypes)
-    shelves = [book] + [from_y(book, k) for k in range(1, 4)]
-    view_one, view_two, _ = lax.optimization_barrier((view_one, view_two, book))
     share = pl.pallas_call(
         views_kernel,
-        out_shape=bf16(groups, 2, PART, D),
+        out_shape=bf16(PLANES, 2, PART, D),
         grid_spec=pltpu.PrefetchScalarGridSpec(
             num_scalar_prefetch=1,
             grid=(1,),
-            in_specs=[pl.BlockSpec((PART, D), lambda i, p: (p[1], 0))] * 2,
+            in_specs=[pl.BlockSpec((PART, D), lambda i, p: (2 * p[1] + p[2], 0))] * 2,
             out_specs=VMEM,
         ),
         compiler_params=params(8),
         name="views",
     )(pos, view_one, view_two)
-    own_rows = exchange(share, ("xh", "z"))
-    *shelves, own_rows = lax.optimization_barrier((*shelves, own_rows))
+    shelves = [book] + [from_y(book, k) for k in range(1, 4)]
+    share = exchange(share, ("z",))
+    shelves[1], shelves[3], share = lax.optimization_barrier((shelves[1], shelves[3], share))
     shelves += [from_core(shelf) for shelf in shelves]
+    own_rows = exchange(jnp.broadcast_to(share[None], (4,) + share.shape), ("xh", "xl"))
 
     total = pl.pallas_call(
         total_kernel,
@@ -320,7 +319,7 @@
         columns = exchange(copies, ("c", "y"))
         if step == 0:
             after, before, columns = lax.optimization_barrier((after, before, columns))
-            far_low, far_high = from_y(after[: groups // 2], 1), from_y(before[groups // 2 :], -1)
+            far_low, far_high = from_y(after[:2], 1), from_y(before[2:], -1)
     copies = pl.pallas_call(
         last_row_kernel,
         out_shape=f32(ROW_PEERS, 2, 8, 128),

time: 171 us -> 167 us (0.977)
  waiting for transfers between devices: 27.6 us -> 11.5 us
  blocking collectives: 81 us -> 87.6 us
  starting transfers between devices: 28.5 us -> 35 us
  Pallas kernels: 29.7 us -> 27.1 us
    all_to_all x1 -> x2, waiting for transfers between devices: 11.9 us -> 0.86 us  [exchange(): return lax.all_to_all(copies, axes, 0, 0, tiled=True)]
    all_to_all x7, blocking collectives: 81 us -> 87.6 us  [exchange(): return lax.all_to_all(copies, axes, 0, 0, tiled=True)]
    ppermute x7, waiting for transfers between devices: 13.9 us -> 9.2 us  [from_y(): lax.ppermute(values, 'y', [((i + distance) % 4, i) for i in range(4)])]
    ppermute x5, starting transfers between devices: 6.45 us -> 10.8 us  [from_core(): return lax.ppermute(values, 'c', [(0, 1), (1, 0)])]
    all_to_all x1 -> x2, starting transfers between devices: 11.6 us -> 13 us  [exchange(): return lax.all_to_all(copies, axes, 0, 0, tiled=True)]
  transfers between devices with their start and end apart: 13 -> 14, of which waited for: 8 -> 7; matrix products, arithmetic and copies ran while one was open for 0% -> 0% of each run, Pallas kernels for 8% -> 7%
where the time goes in v3:
time: 167 us; the launch traced here: 166 us
  blocking collectives  87.6 us (52%)
  starting transfers between devices  35 us (21%)
  Pallas kernels  27.1 us (16%)
  waiting for transfers between devices  11.5 us (7%)
  local copies, waits for them, and re-layouts  4.06 us (2%)
    all_to_all x7, blocking collectives, exchange(): return lax.all_to_all(copies, axes, 0, 0, tiled=True)  87.6 us
    all_to_all x2, starting transfers between devices, exchange(): return lax.all_to_all(copies, axes, 0, 0, tiled=True)  13 us
    ppermute x7, starting transfers between devices, from_y(): lax.ppermute(values, 'y', [((i + distance) % 4, i) for i in range(4)])  11.2 us
    ppermute x5, starting transfers between devices, from_core(): return lax.ppermute(values, 'c', [(0, 1), (1, 0)])  10.8 us
    ppermute x7, waiting for transfers between devices, from_y(): lax.ppermute(values, 'y', [((i + distance) % 4, i) for i in range(4)])  9.2 us
    pallas_call x2, Pallas kernels, grad_of(): pl.pallas_call(functools.partial(grad_kernel, half), out_shape=f32(OWNED,...  8.75 us
    pallas_call x2, Pallas kernels, body(): pl.pallas_call(column_kernel, out_shape=f32(GROUP, GROUP, OWNED), in_spec...  3.97 us
    pallas_call x2, Pallas kernels, body(): pl.pallas_call(row_kernel, out_shape=f32(ROW_PEERS, 8, 128), in_specs=[SM...  3.88 us
  transfers between devices with their start and end apart: 14, of which 7 were waited for; matrix products, arithmetic and copies ran while one was open for 0% of the time, Pallas kernels for 7%

profile of v3, /device:TPU:1, one launch (start us, length us, event | category | flops | bytes accessed | tf_op | source)
XLA Modules:
  0.0 166.1 jit_solution(10495219978113392117)
XLA Ops:
  0.6 0.1 pad_add_fusion.pos_ref
  0.7 0.0 copy-start.4
  0.7 0.9 copy-done.4
  1.6 0.0 copy-start.5
  1.6 0.9 copy-done.5
  2.5 1.4 views.1
  3.9 9.0 %all-to-all-start = ((bf16[8,2,32,256]{3,2,1,0:T(8,128)(2,1)}), bf16[8,2,32,256]{3,2,1,0:T(8,128)(2,1)S(1)}, u32[]{:S(2)}, u32[]{:S(2)}) async-start(bf16[8,2,32,256]{3,2,1,0:T(8,128)(2,1)} %views.1), calls=%async_computation | async-start | bytes 524288 | tf_op jit(solution)/shard_map/all_to_all | solution.py:237
  12.9 0.0 copy-start
  12.9 1.0 copy-done
  13.9 0.2 book.1.refs_0_.book_ref
  14.1 1.4 collective-permute-start.1
  15.5 1.5 collective-permute-start
  17.0 5.4 %collective-permute-done.1.refs_3_ = bf16[512,256]{1,0:T(8,128)(2,1)S(1)} collective-permute-done((bf16[512,256]{1,0:T(8,128)(2,1)S(1)}, bf16[512,256]{1,0:T(8,128)(2,1)S(1)}, u32[]{:S(2)}, u32[]{:S(2)}) %collective-permute-start.1) | collective-permute-done | bytes 262176 | tf_op jit(solution)/shard_map/ppermute | solution.py:240
  22.4 0.0 collective-permute-done.refs_1_
  22.4 0.9 all-to-all-done
  23.3 1.1 broadcast_in_dim.2
  24.4 4.0 %all-to-all-start.1 = ((bf16[4,8,2,32,256]{4,3,2,1,0:T(8,128)(2,1)}), bf16[4,8,2,32,256]{4,3,2,1,0:T(8,128)(2,1)S(1)}, u32[]{:S(2)}, u32[]{:S(2)}) async-start(bf16[4,8,2,32,256]{4,3,2,1,0:T(8,128)(2,1)} %broadcast_in_dim.2), calls=%async_computation.1 | async-start | bytes 2097152 | tf_op jit(solution)/shard_map/all_to_all | solution.py:237
  28.4 2.9 %collective-permute-start.2 = (bf16[512,256]{1,0:T(8,128)(2,1)S(1)}, bf16[512,256]{1,0:T(8,128)(2,1)S(1)}, u32[]{:S(2)}, u32[]{:S(2)}) collective-permute-start(bf16[512,256]{1,0:T(8,128)(2,1)S(1)} %book.1.refs_0_.book_ref), channel_id=1, source_target_pairs={{4,0},{6,2},{0,4},{2,6},{5,1},{7,3},{1,5},{3,7},{12,8},{14,10},{8,... | collective-permute-start | bytes 786440 | tf_op jit(solution)/shard_map/ppermute | solution.py:240
  31.3 3.0 %collective-permute-start.3 = (bf16[512,256]{1,0:T(8,128)(2,1)S(1)}, bf16[512,256]{1,0:T(8,128)(2,1)S(1)}, u32[]{:S(2)}, u32[]{:S(2)}) collective-permute-start(bf16[512,256]{1,0:T(8,128)(2,1)S(1)} %book.1.refs_0_.book_ref), channel_id=1, source_target_pairs={{0,8},{8,0},{1,9},{9,1},{2,10},{10,2},{3,11},{11,3},{4,12},{12,4},... | collective-permute-start | bytes 786440 | tf_op jit(solution)/shard_map/ppermute | solution.py:243
  34.4 0.8 collective-permute-done.2.refs_2_
  35.1 3.9 %collective-permute-start.5 = (bf16[512,256]{1,0:T(8,128)(2,1)S(1)}, bf16[512,256]{1,0:T(8,128)(2,1)S(1)}, u32[]{:S(2)}, u32[]{:S(2)}) collective-permute-start(bf16[512,256]{1,0:T(8,128)(2,1)S(1)} %collective-permute-done.2.refs_2_), channel_id=1, source_target_pairs={{0,8},{8,0},{1,9},{9,1},{2,10},{10,2},{3,11},{11,3},{4,12},{12,4},... | collective-permute-start | bytes 786440 | tf_op jit(solution)/shard_map/ppermute | solution.py:243
  39.0 0.0 collective-permute-start.4
  39.0 0.5 collective-permute-start.6
  39.5 0.0 collective-permute-done.3.refs_4_.book_ref
  39.6 0.6 collective-permute-done.5.refs_6_
  40.2 0.4 collective-permute-done.4.refs_5_
  40.6 0.4 collective-permute-done.6.refs_7_
  40.9 0.0 all-to-all-done.1.rows_ref.refs_0_
  41.0 2.5 %totals.1.total_ref = f32[8,128]{1,0:T(8,128)S(1)} custom-call(bf16[4,8,2,32,256]{4,3,2,1,0:T(8,128)(2,1)S(1)} %all-to-all-done.1.rows_ref.refs_0_, bf16[512,256]{1,0:T(8,128)(2,1)S(1)} %book.1.refs_0_.book_ref, bf16[512,256]{1,0:T(8,128)(2,1)S(1)} %collective-permute-done.refs_1_, bf16[512,256]{1,0:T(8,128)(2,1)S(1)} %collective-permute-done.2.refs_2_, ...), custom_call_target="tpu_custom_call" | custom-call | flops 2147483648 | bytes 3145728 | tf_op jit(solution)/shard_map/totals/pallas_call | solution.py:271
  43.4 2.9 %expo.1 = (f32[8,1024,512]{2,1,0:T(8,128)S(1)}, f32[8,8,512]{2,1,0:T(8,128)S(1)}) custom-call(s32[3]{0:T(128)S(1)} %pad_add_fusion.pos_ref, bf16[4,8,2,32,256]{4,3,2,1,0:T(8,128)(2,1)S(1)} %all-to-all-done.1.rows_ref.refs_0_, bf16[512,256]{1,0:T(8,128)(2,1)S(1)} %book.1.refs_0_.book_ref, bf16[512,256]{1,0:T(8,128)(2,1)S(1)} %collective-permute-done.refs_1_, ...), custom_call_target="tpu_custom_call" | custom-call | tf_op jit(solution)/shard_map/expo/pallas_call | solution.py:282
  46.4 12.9 %all_to_all.45.columns_ref = f32[8,8,512]{2,1,0:T(8,128)S(1)} all-to-all(f32[8,8,512]{2,1,0:T(8,128)S(1)} %get-tuple-element.42), channel_id=1, replica_groups=mesh['xh'=2,'z'=8,'c'=2,'y'=4,'xl'=2] {'c','y'}, dimensions={0} | all-to-all | bytes 262144 | tf_op jit(solution)/shard_map/all_to_all | solution.py:237
  59.3 0.7 collective-permute-start.8
  60.0 2.0 %collective-permute-start.7 = (bf16[4,8,2,32,256]{4,3,2,1,0:T(8,128)(2,1)S(1)}, bf16[4,8,2,32,256]{4,3,2,1,0:T(8,128)(2,1)S(1)}, u32[]{:S(2)}, u32[]{:S(2)}) collective-permute-start(bf16[4,8,2,32,256]{4,3,2,1,0:T(8,128)(2,1)S(1)} %all-to-all-done.1.rows_ref.refs_0_), channel_id=1, source_target_pairs={{2,0},{4,2},{6,4},{0,6},{3,1},{5,3},{7,5},{1,7},{10,8},{12,10},{14... | collective-permute-start | bytes 3145736 | tf_op jit(solution)/shard_map/ppermute | solution.py:240
  62.0 1.9 %row_sums.2 = f32[32,8,128]{2,1,0:T(8,128)S(1)} custom-call(s32[3]{0:T(128)S(1)} %pad_add_fusion.pos_ref, f32[8,8,512]{2,1,0:T(8,128)S(1)} %all_to_all.45.columns_ref, f32[8,1024,512]{2,1,0:T(8,128)S(1)} %get-tuple-element.45.expd_ref), custom_call_target="tpu_custom_call" | custom-call | tf_op jit(solution)/shard_map/row_sums/pallas_call | solution.py:296
  63.9 15.9 %all_to_all.46.sums_ref = f32[32,8,128]{2,1,0:T(8,128)S(1)} all-to-all(f32[32,8,128]{2,1,0:T(8,128)S(1)} %row_sums.2), channel_id=1, replica_groups=mesh['xh'=2,'z'=8,'c'=2,'y'=4,'xl'=2] {'xh','z','xl'}, dimensions={0} | all-to-all | bytes 262144 | tf_op jit(solution)/shard_map/all_to_all | solution.py:237
  79.8 2.0 %column_sums.2 = f32[8,8,512]{2,1,0:T(8,128)S(1)} custom-call(s32[3]{0:T(128)S(1)} %pad_add_fusion.pos_ref, f32[32,8,128]{2,1,0:T(8,128)S(1)} %all_to_all.46.sums_ref, f32[8,1024,512]{2,1,0:T(8,128)S(1)} %get-tuple-element.45.expd_ref), custom_call_target="tpu_custom_call" | custom-call | tf_op jit(solution)/shard_map/column_sums/pallas_call | solution.py:306
  81.8 3.0 %collective-permute-done.8.refs_2_ = bf16[4,8,2,32,256]{4,3,2,1,0:T(8,128)(2,1)S(1)} collective-permute-done((bf16[4,8,2,32,256]{4,3,2,1,0:T(8,128)(2,1)S(1)}, bf16[4,8,2,32,256]{4,3,2,1,0:T(8,128)(2,1)S(1)}, u32[]{:S(2)}, u32[]{:S(2)}) %collective-permute-start.8) | collective-permute-done | bytes 1048608 | tf_op jit(solution)/shard_map/ppermute | solution.py:240
  84.9 0.0 collective-permute-done.7.refs_1_
  84.9 10.4 %all_to_all.47.columns_ref = f32[8,8,512]{2,1,0:T(8,128)S(1)} all-to-all(f32[8,8,512]{2,1,0:T(8,128)S(1)} %column_sums.2), channel_id=1, replica_groups=mesh['xh'=2,'z'=8,'c'=2,'y'=4,'xl'=2] {'c','y'}, dimensions={0} | all-to-all | bytes 262144 | tf_op jit(solution)/shard_map/all_to_all | solution.py:237
  95.4 0.8 collective-permute-start.10
  96.1 2.0 %collective-permute-start.9 = (bf16[2,8,2,32,256]{4,3,2,1,0:T(8,128)(2,1)S(1)}, bf16[2,8,2,32,256]{4,3,2,1,0:T(8,128)(2,1)S(1)}, u32[]{:S(2)}, u32[]{:S(2)}) collective-permute-start(bf16[2,8,2,32,256]{4,3,2,1,0:T(8,128)(2,1)S(1)} %slice.6), channel_id=1, source_target_pairs={{2,0},{4,2},{6,4},{0,6},{3,1},{5,3},{7,5},{1,7},{10,8},{12,10},{14... | collective-permute-start | bytes 1572872 | tf_op jit(solution)/shard_map/ppermute | solution.py:240
  98.1 1.9 %row_sums.3 = f32[32,8,128]{2,1,0:T(8,128)S(1)} custom-call(s32[3]{0:T(128)S(1)} %pad_add_fusion.pos_ref, f32[8,8,512]{2,1,0:T(8,128)S(1)} %all_to_all.47.columns_ref, f32[8,1024,512]{2,1,0:T(8,128)S(1)} %get-tuple-element.45.expd_ref), custom_call_target="tpu_custom_call" | custom-call | tf_op jit(solution)/shard_map/row_sums/pallas_call | solution.py:296
  100.1 15.9 %all_to_all.48.sums_ref = f32[32,8,128]{2,1,0:T(8,128)S(1)} all-to-all(f32[32,8,128]{2,1,0:T(8,128)S(1)} %row_sums.3), channel_id=1, replica_groups=mesh['xh'=2,'z'=8,'c'=2,'y'=4,'xl'=2] {'xh','z','xl'}, dimensions={0} | all-to-all | bytes 262144 | tf_op jit(solution)/shard_map/all_to_all | solution.py:237
  116.0 2.0 %column_sums.3 = f32[8,8,512]{2,1,0:T(8,128)S(1)} custom-call(s32[3]{0:T(128)S(1)} %pad_add_fusion.pos_ref, f32[32,8,128]{2,1,0:T(8,128)S(1)} %all_to_all.48.sums_ref, f32[8,1024,512]{2,1,0:T(8,128)S(1)} %get-tuple-element.45.expd_ref), custom_call_target="tpu_custom_call" | custom-call | tf_op jit(solution)/shard_map/column_sums/pallas_call | solution.py:306
  118.0 0.0 collective-permute-done.10.refs_4_
  118.0 0.0 collective-permute-done.9.refs_3_
  118.0 9.9 %all_to_all.49.columns_ref = f32[8,8,512]{2,1,0:T(8,128)S(1)} all-to-all(f32[8,8,512]{2,1,0:T(8,128)S(1)} %column_sums.3), channel_id=1, replica_groups=mesh['xh'=2,'z'=8,'c'=2,'y'=4,'xl'=2] {'c','y'}, dimensions={0} | all-to-all | bytes 262144 | tf_op jit(solution)/shard_map/all_to_all | solution.py:237
  127.9 0.0 copy-start.1
  127.9 0.0 copy-start.2
  127.9 0.0 copy-start.3
  127.9 1.9 %last_row_sums.1 = f32[32,2,8,128]{3,2,1,0:T(8,128)S(1)} custom-call(s32[3]{0:T(128)S(1)} %pad_add_fusion.pos_ref, f32[8,8,512]{2,1,0:T(8,128)S(1)} %all_to_all.49.columns_ref, f32[8,1024,512]{2,1,0:T(8,128)S(1)} %get-tuple-element.45.expd_ref, f32[8,128]{1,0:T(8,128)S(1)} %totals.1.total_ref), custom_call_target="tpu_custom_call" | custom-call | tf_op jit(solution)/shard_map/last_row_sums/pallas_call | solution.py:323
  129.8 15.9 %all_to_all.50.sums_ref = f32[32,2,8,128]{3,2,1,0:T(8,128)S(1)} all-to-all(f32[32,2,8,128]{3,2,1,0:T(8,128)S(1)} %last_row_sums.1), channel_id=1, replica_groups=mesh['xh'=2,'z'=8,'c'=2,'y'=4,'xl'=2] {'xh','z','xl'}, dimensions={0} | all-to-all | bytes 524288 | tf_op jit(solution)/shard_map/all_to_all | solution.py:237
  145.7 6.7 %all_to_all.51.scales_ref = f32[4,2,8,128]{3,2,1,0:T(8,128)S(1)} all-to-all(f32[4,2,8,128]{3,2,1,0:T(8,128)S(1)} %scales.1), channel_id=1, replica_groups=mesh['xh'=2,'z'=8,'c'=2,'y'=4,'xl'=2] {'y'}, dimensions={0} | all-to-all | bytes 65536 | tf_op jit(solution)/shard_map/all_to_all | solution.py:237
  152.4 4.4 %grad_of_other.1 = f32[512,256]{1,0:T(8,128)S(1)} custom-call(s32[3]{0:T(128)S(1)} %pad_add_fusion.pos_ref, f32[4,2,8,128]{3,2,1,0:T(8,128)S(1)} %all_to_all.51.scales_ref, f32[8,8,512]{2,1,0:T(8,128)S(1)} %all_to_all.49.columns_ref, bf16[512,256]{1,0:T(8,128)(2,1)S(1)} %collective-permute-done.3.refs_4_.book_ref, ...), custom_call_target="tpu_custom_call" | custom-call | flops 3221225472 | bytes 6291456 | tf_op jit(solution)/shard_map/grad_of_other/pallas_call | solution.py:344
  156.8 3.3 %collective-permute-start.11 = (f32[512,256]{1,0:T(8,128)S(1)}, f32[512,256]{1,0:T(8,128)S(1)}, u32[]{:S(2)}, u32[]{:S(2)}) collective-permute-start(f32[512,256]{1,0:T(8,128)S(1)} %grad_of_other.1), channel_id=1, source_target_pairs={{0,8},{8,0},{1,9},{9,1},{2,10},{10,2},{3,11},{11,3},{4,12},{12,4},... | collective-permute-start | bytes 1572872 | tf_op jit(solution)/shard_map/ppermute | solution.py:243
  160.1 4.4 %grad_of_own.1.own_ref = f32[512,256]{1,0:T(8,128)S(1)} custom-call(s32[3]{0:T(128)S(1)} %pad_add_fusion.pos_ref, f32[4,2,8,128]{3,2,1,0:T(8,128)S(1)} %all_to_all.51.scales_ref, f32[8,8,512]{2,1,0:T(8,128)S(1)} %all_to_all.49.columns_ref, bf16[512,256]{1,0:T(8,128)(2,1)S(1)} %book.1.refs_0_.book_ref, ...), custom_call_target="tpu_custom_call" | custom-call | flops 3221225472 | bytes 6291456 | tf_op jit(solution)/shard_map/grad_of_own/pallas_call | solution.py:344
  164.5 0.0 collective-permute-done.11.other_ref
  164.5 0.0 copy-done.1
  164.5 0.0 copy-done.2
  164.5 0.0 copy-done.3
  164.5 1.6 update.1
  (3 shorter events, 0.1 us)
Async XLA Ops:
  0.7 0.9 copy-start.4
  1.6 0.9 copy-start.5
  3.9 19.4 %all-to-all-start = ((bf16[8,2,32,256]{3,2,1,0:T(8,128)(2,1)}), bf16[8,2,32,256]{3,2,1,0:T(8,128)(2,1)S(1)}, u32[]{:S(2)}, u32[]{:S(2)}) async-start(bf16[8,2,32,256]{3,2,1,0:T(8,128)(2,1)} %views.1), calls=%async_computation | async-start | bytes 524288 | tf_op jit(solution)/shard_map/all_to_all | solution.py:237
  12.9 1.0 copy-start
  14.1 8.3 %collective-permute-start.1 = (bf16[512,256]{1,0:T(8,128)(2,1)S(1)}, bf16[512,256]{1,0:T(8,128)(2,1)S(1)}, u32[]{:S(2)}, u32[]{:S(2)}) collective-permute-start(bf16[512,256]{1,0:T(8,128)(2,1)S(1)} %book.1.refs_0_.book_ref), channel_id=1, source_target_pairs={{6,0},{0,2},{2,4},{4,6},{7,1},{1,3},{3,5},{5,7},{14,8},{8,10},{10,... | collective-permute-start | bytes 786440 | tf_op jit(solution)/shard_map/ppermute | solution.py:240
  15.5 6.9 %collective-permute-start = (bf16[512,256]{1,0:T(8,128)(2,1)S(1)}, bf16[512,256]{1,0:T(8,128)(2,1)S(1)}, u32[]{:S(2)}, u32[]{:S(2)}) collective-permute-start(bf16[512,256]{1,0:T(8,128)(2,1)S(1)} %book.1.refs_0_.book_ref), channel_id=1, source_target_pairs={{2,0},{4,2},{6,4},{0,6},{3,1},{5,3},{7,5},{1,7},{10,8},{12,10},{14... | collective-permute-start | bytes 786440 | tf_op jit(solution)/shard_map/ppermute | solution.py:240
  24.4 16.5 %all-to-all-start.1 = ((bf16[4,8,2,32,256]{4,3,2,1,0:T(8,128)(2,1)}), bf16[4,8,2,32,256]{4,3,2,1,0:T(8,128)(2,1)S(1)}, u32[]{:S(2)}, u32[]{:S(2)}) async-start(bf16[4,8,2,32,256]{4,3,2,1,0:T(8,128)(2,1)} %broadcast_in_dim.2), calls=%async_computation.1 | async-start | bytes 2097152 | tf_op jit(solution)/shard_map/all_to_all | solution.py:237
  28.4 6.7 %collective-permute-start.2 = (bf16[512,256]{1,0:T(8,128)(2,1)S(1)}, bf16[512,256]{1,0:T(8,128)(2,1)S(1)}, u32[]{:S(2)}, u32[]{:S(2)}) collective-permute-start(bf16[512,256]{1,0:T(8,128)(2,1)S(1)} %book.1.refs_0_.book_ref), channel_id=1, source_target_pairs={{4,0},{6,2},{0,4},{2,6},{5,1},{7,3},{1,5},{3,7},{12,8},{14,10},{8,... | collective-permute-start | bytes 786440 | tf_op jit(solution)/shard_map/ppermute | solution.py:240
  31.3 8.2 %collective-permute-start.3 = (bf16[512,256]{1,0:T(8,128)(2,1)S(1)}, bf16[512,256]{1,0:T(8,128)(2,1)S(1)}, u32[]{:S(2)}, u32[]{:S(2)}) collective-permute-start(bf16[512,256]{1,0:T(8,128)(2,1)S(1)} %book.1.refs_0_.book_ref), channel_id=1, source_target_pairs={{0,8},{8,0},{1,9},{9,1},{2,10},{10,2},{3,11},{11,3},{4,12},{12,4},... | collective-permute-start | bytes 786440 | tf_op jit(solution)/shard_map/ppermute | solution.py:243
  35.1 5.1 %collective-permute-start.5 = (bf16[512,256]{1,0:T(8,128)(2,1)S(1)}, bf16[512,256]{1,0:T(8,128)(2,1)S(1)}, u32[]{:S(2)}, u32[]{:S(2)}) collective-permute-start(bf16[512,256]{1,0:T(8,128)(2,1)S(1)} %collective-permute-done.2.refs_2_), channel_id=1, source_target_pairs={{0,8},{8,0},{1,9},{9,1},{2,10},{10,2},{3,11},{11,3},{4,12},{12,4},... | collective-permute-start | bytes 786440 | tf_op jit(solution)/shard_map/ppermute | solution.py:243
  39.0 1.5 collective-permute-start.4
  39.0 1.9 %collective-permute-start.6 = (bf16[512,256]{1,0:T(8,128)(2,1)S(1)}, bf16[512,256]{1,0:T(8,128)(2,1)S(1)}, u32[]{:S(2)}, u32[]{:S(2)}) collective-permute-start(bf16[512,256]{1,0:T(8,128)(2,1)S(1)} %collective-permute-done.1.refs_3_), channel_id=1, source_target_pairs={{0,8},{8,0},{1,9},{9,1},{2,10},{10,2},{3,11},{11,3},{4,12},{12,4},... | collective-permute-start | bytes 786440 | tf_op jit(solution)/shard_map/ppermute | solution.py:243
  59.3 25.6 %collective-permute-start.8 = (bf16[4,8,2,32,256]{4,3,2,1,0:T(8,128)(2,1)S(1)}, bf16[4,8,2,32,256]{4,3,2,1,0:T(8,128)(2,1)S(1)}, u32[]{:S(2)}, u32[]{:S(2)}) collective-permute-start(bf16[4,8,2,32,256]{4,3,2,1,0:T(8,128)(2,1)S(1)} %all-to-all-done.1.rows_ref.refs_0_), channel_id=1, source_target_pairs={{6,0},{0,2},{2,4},{4,6},{7,1},{1,3},{3,5},{5,7},{14,8},{8,10},{10,... | collective-permute-start | bytes 3145736 | tf_op jit(solution)/shard_map/ppermute | solution.py:240
  60.0 24.9 %collective-permute-start.7 = (bf16[4,8,2,32,256]{4,3,2,1,0:T(8,128)(2,1)S(1)}, bf16[4,8,2,32,256]{4,3,2,1,0:T(8,128)(2,1)S(1)}, u32[]{:S(2)}, u32[]{:S(2)}) collective-permute-start(bf16[4,8,2,32,256]{4,3,2,1,0:T(8,128)(2,1)S(1)} %all-to-all-done.1.rows_ref.refs_0_), channel_id=1, source_target_pairs={{2,0},{4,2},{6,4},{0,6},{3,1},{5,3},{7,5},{1,7},{10,8},{12,10},{14... | collective-permute-start | bytes 3145736 | tf_op jit(solution)/shard_map/ppermute | solution.py:240
  95.4 22.6 %collective-permute-start.10 = (bf16[2,8,2,32,256]{4,3,2,1,0:T(8,128)(2,1)S(1)}, bf16[2,8,2,32,256]{4,3,2,1,0:T(8,128)(2,1)S(1)}, u32[]{:S(2)}, u32[]{:S(2)}) collective-permute-start(bf16[2,8,2,32,256]{4,3,2,1,0:T(8,128)(2,1)S(1)} %slice.7), channel_id=1, source_target_pairs={{6,0},{0,2},{2,4},{4,6},{7,1},{1,3},{3,5},{5,7},{14,8},{8,10},{10,... | collective-permute-start | bytes 1572872 | tf_op jit(solution)/shard_map/ppermute | solution.py:240
  96.1 21.8 %collective-permute-start.9 = (bf16[2,8,2,32,256]{4,3,2,1,0:T(8,128)(2,1)S(1)}, bf16[2,8,2,32,256]{4,3,2,1,0:T(8,128)(2,1)S(1)}, u32[]{:S(2)}, u32[]{:S(2)}) collective-permute-start(bf16[2,8,2,32,256]{4,3,2,1,0:T(8,128)(2,1)S(1)} %slice.6), channel_id=1, source_target_pairs={{2,0},{4,2},{6,4},{0,6},{3,1},{5,3},{7,5},{1,7},{10,8},{12,10},{14... | collective-permute-start | bytes 1572872 | tf_op jit(solution)/shard_map/ppermute | solution.py:240
  127.9 36.6 %copy-start.1 = (f32[1,512,256]{2,1,0:T(8,128)S(1)}, f32[1,512,256]{2,1,0:T(8,128)}, u32[]{:S(2)}) copy-start(f32[1,512,256]{2,1,0:T(8,128)} %proto_ref.3) | copy-start | bytes 1572868
  127.9 36.6 %copy-start.2 = (f32[1,512,256]{2,1,0:T(8,128)S(1)}, f32[1,512,256]{2,1,0:T(8,128)}, u32[]{:S(2)}) copy-start(f32[1,512,256]{2,1,0:T(8,128)} %first_ref.1) | copy-start | bytes 1572868
  127.9 36.6 %copy-start.3 = (f32[1,512,256]{2,1,0:T(8,128)S(1)}, f32[1,512,256]{2,1,0:T(8,128)}, u32[]{:S(2)}) copy-start(f32[1,512,256]{2,1,0:T(8,128)} %second_ref.1) | copy-start | bytes 1572868
  156.8 7.7 %collective-permute-start.11 = (f32[512,256]{1,0:T(8,128)S(1)}, f32[512,256]{1,0:T(8,128)S(1)}, u32[]{:S(2)}, u32[]{:S(2)}) collective-permute-start(f32[512,256]{1,0:T(8,128)S(1)} %grad_of_other.1), channel_id=1, source_target_pairs={{0,8},{8,0},{1,9},{9,1},{2,10},{10,2},{3,11},{11,3},{4,12},{12,4},... | collective-permute-start | bytes 1572872 | tf_op jit(solution)/shard_map/ppermute | solution.py:243

commit v4 on v3

--- a/solution.py
+++ b/solution.py
@@ -49,9 +49,9 @@
     book_ref[...] = normalize(proto_ref[0]).astype(jnp.bfloat16)
 
 
-def views_kernel(pos_ref, one_ref, two_ref, share_ref):
-    for view, ref in enumerate((one_ref, two_ref)):
-        rows = normalize(ref[...]).astype(jnp.bfloat16)
+def views_kernel(views_ref, share_ref):
+    for view in range(2):
+        rows = normalize(views_ref[view]).astype(jnp.bfloat16)
         for peer in range(share_ref.shape[0]):
             share_ref[peer, view] = rows
 
@@ -154,52 +154,52 @@
 
 
 def scales_kernel(sums_ref, out_ref):
-    sums = jnp.sum(sums_ref[...], axis=0)
-    scale_b = GRAD_SCALE / sums[0]
-    scale_z = GRAD_SCALE / sums[1]
-    for peer in range(out_ref.shape[0]):
-        out_ref[peer, 0] = scale_b
-        out_ref[peer, 1] = scale_z
-
-
-def grad_kernel(half, pos_ref, scales_ref, columns_ref, book_ref, *refs):
-    pieces, (out_ref, scale_ref, grads_ref) = refs[:5], refs[5:]
+    out_ref[...] = GRAD_SCALE / jnp.sum(sums_ref[...], axis=0)
+
+
+def grad_kernel(halves, blocks, pos_ref, columns_ref, *refs):
+    count = len(halves)
+    refs = list(refs)
+    books = [refs.pop(0) for _ in halves]
+    scales = [refs.pop(0) for _ in blocks]
+    rows = [[refs.pop(0) for _ in range(2 if block == 2 else 1)] for block in blocks]
+    before = [refs.pop(0) for _ in halves] if 0 not in blocks else None
+    outs, scale_ref = refs[:count], refs[count]
     scale_a = 1.0 / (K * jnp.sum(columns_ref[...], axis=0))
     line = lax.broadcasted_iota(jnp.int32, (GROUP, OWNED), 0)
-    picked = jnp.sum(jnp.where(line == place_of(pos_ref, 4 * half), scale_a, 0.0), axis=0, keepdims=True)
-    for j in range(OWNED // 128):
-        scale_ref[j * 128 : (j + 1) * 128, :] = jnp.broadcast_to(
-            picked[:, j * 128 : (j + 1) * 128], (128, 128)
-        ).T
-    book = book_ref[...]
-
-    def view(block, number, at):
-        if block != 2:
-            return rows_of(pieces[(0, 1, None, 2)[block]], number, at)
-        return rows_of(pieces[3 + at // (HELD // 2)], number, at % (HELD // 2))
-
-    for block in range(4):
-        place = (pos_ref[1] + block) % 4
-        scale_b, scale_z = scales_ref[place, 0], scales_ref[place, 1]
-        for at in range(0, HELD, 256):
-            two = view(block, 1, at)
-            codes = jnp.exp2(contract_last(book, view(block, 0, at)) * FIRST_SCALE)
-            probs = jnp.exp2(contract_last(book, two) * SECOND_SCALE)
-            tiles = []
-            for j in range(0, 256, 128):
-                row = (at + j) // 128
-                tiles.append(
-                    (
-                        probs[:, j : j + 128] * scale_z[row : row + 1, :]
-                        - codes[:, j : j + 128] * scale_ref[...] * scale_b[row : row + 1, :]
-                    ).astype(jnp.bfloat16)
-                )
-            part = jnp.dot(jnp.concatenate(tiles, axis=1), two, preferred_element_type=jnp.float32)
-            if block == 0 and at == 0:
-                grads_ref[...] = part
-            else:
-                grads_ref[...] += part
-    out_ref[...] = grads_ref[...]
+    for i, half in enumerate(halves):
+        picked = jnp.sum(jnp.where(line == place_of(pos_ref, 4 * half), scale_a, 0.0), axis=0, keepdims=True)
+        for j in range(OWNED // 128):
+            scale_ref[j * 128 : (j + 1) * 128, :] = jnp.broadcast_to(
+                picked[:, j * 128 : (j + 1) * 128], (128, 128)
+            ).T
+        book = books[i][...]
+        fresh = before is None
+        for pieces, scale in zip(rows, scales):
+            scale_b, scale_z = scale[0], scale[1]
+            size = HELD // len(pieces)
+            for at in range(0, HELD, 256):
+                piece = pieces[at // size]
+                two = rows_of(piece, 1, at % size)
+                codes = jnp.exp2(contract_last(book, rows_of(piece, 0, at % size)) * FIRST_SCALE)
+                probs = jnp.exp2(contract_last(book, two) * SECOND_SCALE)
+                tiles = []
+                for j in range(0, 256, 128):
+                    row = (at + j) // 128
+                    tiles.append(
+                        (
+                            probs[:, j : j + 128] * scale_z[row : row + 1, :]
+                            - codes[:, j : j + 128] * scale_ref[...] * scale_b[row : row + 1, :]
+                        ).astype(jnp.bfloat16)
+                    )
+                part = jnp.dot(jnp.concatenate(tiles, axis=1), two, preferred_element_type=jnp.float32)
+                if fresh:
+                    outs[i][...] = part
+                elif before is not None and at == 0 and pieces is rows[0]:
+                    outs[i][...] = before[i][...] + part
+                else:
+                    outs[i][...] += part
+                fresh = False
 
 
 def update_kernel(
@@ -250,35 +250,22 @@
         compiler_params=params(8),
         name="book",
     )(prototypes)
+    start = (2 * pos[1] + pos[2]) * PART
+    parts = jnp.stack([lax.dynamic_slice_in_dim(view, start, PART) for view in (view_one, view_two)])
     share = pl.pallas_call(
         views_kernel,
         out_shape=bf16(PLANES, 2, PART, D),
-        grid_spec=pltpu.PrefetchScalarGridSpec(
-            num_scalar_prefetch=1,
-            grid=(1,),
-            in_specs=[pl.BlockSpec((PART, D), lambda i, p: (2 * p[1] + p[2], 0))] * 2,
-            out_specs=VMEM,
-        ),
+        in_specs=[VMEM],
+        out_specs=VMEM,
         compiler_params=params(8),
         name="views",
-    )(pos, view_one, view_two)
+    )(parts)
     shelves = [book] + [from_y(book, k) for k in range(1, 4)]
     share = exchange(share, ("z",))
     shelves[1], shelves[3], share = lax.optimization_barrier((shelves[1], shelves[3], share))
     shelves += [from_core(shelf) for shelf in shelves]
     own_rows = exchange(jnp.broadcast_to(share[None], (4,) + share.shape), ("xh", "xl"))
 
-    total = pl.pallas_call(
-        total_kernel,
-        out_shape=f32(8, 128),
-        in_specs=[VMEM] * (1 + GROUP),
-        out_specs=VMEM,
-        scratch_shapes=[pltpu.VMEM((HELD, 128), jnp.float32)],
-        compiler_params=params(8),
-        cost_estimate=cost(HELD * GROUP * OWNED, 3 * MIB),
-        name="totals",
-    )(own_rows, *shelves)
-    *shelves, total = lax.optimization_barrier((*shelves, total))
     expd, copies = pl.pallas_call(
         expo_kernel,
         out_shape=(f32(GROUP, HELD, OWNED), f32(GROUP, GROUP, OWNED)),
@@ -290,6 +277,17 @@
     columns = exchange(copies, ("c", "y"))
     sent, columns = lax.optimization_barrier((own_rows, columns))
     after, before = from_y(sent, 1), from_y(sent, -1)
+    total = pl.pallas_call(
+        total_kernel,
+        out_shape=f32(8, 128),
+        in_specs=[VMEM] * (1 + GROUP),
+        out_specs=VMEM,
+        scratch_shapes=[pltpu.VMEM((HELD, 128), jnp.float32)],
+        compiler_params=params(8),
+        cost_estimate=cost(HELD * GROUP * OWNED, 3 * MIB),
+        name="totals",
+    )(sent, *shelves)
+    columns, total = lax.optimization_barrier((columns, total))
     row_scratch = [pltpu.VMEM((GROUP, 8, OWNED), jnp.float32), pltpu.VMEM((HELD, 128), jnp.float32)]
     assert ITERS == 3
     for step in range(ITERS - 1):
@@ -302,6 +300,9 @@
             compiler_params=params(8),
             name="row_sums",
         )(pos, columns, expd)
+        if step == 1:
+            high, copies = lax.optimization_barrier((high, copies))
+            far_high = from_y(high, -1)
         sums = exchange(copies, ("xh", "z", "xl"))
         copies = pl.pallas_call(
             column_kernel,
@@ -319,7 +320,8 @@
         columns = exchange(copies, ("c", "y"))
         if step == 0:
             after, before, columns = lax.optimization_barrier((after, before, columns))
-            far_low, far_high = from_y(after[:2], 1), from_y(before[2:], -1)
+            low, high = after[:2], before[2:]
+            far_low = from_y(low, 1)
     copies = pl.pallas_call(
         last_row_kernel,
         out_shape=f32(ROW_PEERS, 2, 8, 128),
@@ -332,29 +334,34 @@
     sums = exchange(copies, ("xh", "z", "xl"))
     copies = pl.pallas_call(
         scales_kernel,
-        out_shape=f32(4, 2, 8, 128),
+        out_shape=f32(2, 8, 128),
         in_specs=[VMEM],
         out_specs=VMEM,
         compiler_params=params(8),
         name="scales",
     )(sums)
-    scales = exchange(copies, ("y",))
-
-    def grad_of(half):
+    scales = [copies] + [from_y(copies, k) for k in range(1, 4)]
+    row_blocks = [[own_rows], [after], [far_low, far_high], [before]]
+
+    def grad_of(halves, blocks, sums_so_far, name):
+        operands = [shelves[4 * half] for half in halves] + [scales[block] for block in blocks]
+        operands += [piece for block in blocks for piece in row_blocks[block]] + sums_so_far
         return pl.pallas_call(
-            functools.partial(grad_kernel, half),
-            out_shape=f32(OWNED, D),
-            in_specs=[SMEM] + [VMEM] * 8,
-            out_specs=VMEM,
-            scratch_shapes=[pltpu.VMEM((OWNED, 128), jnp.float32), pltpu.VMEM((OWNED, D), jnp.float32)],
+            functools.partial(grad_kernel, halves, blocks),
+            out_shape=[f32(OWNED, D)] * len(halves),
+            in_specs=[SMEM] + [VMEM] * (1 + len(operands)),
+            out_specs=[VMEM] * len(halves),
+            scratch_shapes=[pltpu.VMEM((OWNED, 128), jnp.float32)],
             compiler_params=params(8),
-            cost_estimate=cost(3 * 4 * HELD * OWNED, 6 * MIB),
-            name="grad_of_own" if half == 0 else "grad_of_other",
-        )(pos, scales, columns, shelves[4 * half], own_rows, after, before, far_low, far_high)
-
-    away = grad_of(1)
-    scales, away = lax.optimization_barrier((scales, away))
-    own, other = grad_of(0), from_core(away)
+            cost_estimate=cost(3 * len(halves) * len(blocks) * HELD * OWNED, 6 * MIB),
+            name=name,
+        )(pos, columns, *operands)
+
+    own, away = grad_of((0, 1), (0,), [], "grad_of_own_rows")
+    (away,) = grad_of((1,), (1, 3, 2), [away], "grad_of_other")
+    own, away = lax.optimization_barrier((own, away))
+    other = from_core(away)
+    (own,) = grad_of((0,), (1, 3, 2), [own], "grad_of_own")
     block = pl.BlockSpec((1, OWNED // 2, D), lambda i: (0, i, 0))
     return pl.pallas_call(
         update_kernel,

time: 167 us -> 160 us (0.958)
  blocking collectives: 87.6 us -> 80.9 us
  starting transfers between devices: 35 us -> 38.2 us
  waiting for transfers between devices: 11.5 us -> 8.92 us
    all_to_all x7 -> x6, blocking collectives: 87.6 us -> 80.9 us  [exchange(): return lax.all_to_all(copies, axes, 0, 0, tiled=True)]
    ppermute x7 -> x10, starting transfers between devices: 11.2 us -> 14.9 us  [from_y(): lax.ppermute(values, 'y', [((i + distance) % 4, i) for i in range(4)])]
    ppermute x7 -> x10, waiting for transfers between devices: 9.2 us -> 6.73 us  [from_y(): lax.ppermute(values, 'y', [((i + distance) % 4, i) for i in range(4)])]
    unnamed x12 -> x8, local copies, waits for them, and re-layouts: 2.86 us -> 1.05 us
    pallas_call x4 -> x5, Pallas kernels: 10.2 us -> 10.6 us  [the longest x3 9.7 us: grad_of(): pl.pallas_call(functools.partial(grad_kernel, halves, blocks), out_shape=...]
  transfers between devices with their start and end apart: 14 -> 17, of which waited for: 7 -> 7; matrix products, arithmetic and copies ran while one was open for 0% -> 0% of each run, Pallas kernels for 7% -> 9%
where the time goes in v4:
time: 160 us; the launch traced here: 159 us
  blocking collectives  80.9 us (51%)
  starting transfers between devices  38.2 us (24%)
  Pallas kernels  27.5 us (17%)
  waiting for transfers between devices  8.92 us (6%)
  local copies, waits for them, and re-layouts  3 us (2%)
    all_to_all x6, blocking collectives, exchange(): return lax.all_to_all(copies, axes, 0, 0, tiled=True)  80.9 us
    ppermute x10, starting transfers between devices, from_y(): lax.ppermute(values, 'y', [((i + distance) % 4, i) for i in range(4)])  14.9 us
    all_to_all x2, starting transfers between devices, exchange(): return lax.all_to_all(copies, axes, 0, 0, tiled=True)  13 us
    ppermute x5, starting transfers between devices, from_core(): return lax.ppermute(values, 'c', [(0, 1), (1, 0)])  10.2 us
    pallas_call x3, Pallas kernels, grad_of(): pl.pallas_call(functools.partial(grad_kernel, halves, blocks), out_shape=...  9.7 us
    ppermute x10, waiting for transfers between devices, from_y(): lax.ppermute(values, 'y', [((i + distance) % 4, i) for i in range(4)])  6.73 us
    pallas_call x2, Pallas kernels, body(): pl.pallas_call(column_kernel, out_shape=f32(GROUP, GROUP, OWNED), in_spec...  3.97 us
    pallas_call x2, Pallas kernels, body(): pl.pallas_call(row_kernel, out_shape=f32(ROW_PEERS, 8, 128), in_specs=[SM...  3.89 us
  transfers between devices with their start and end apart: 17, of which 7 were waited for; matrix products, arithmetic and copies ran while one was open for 0% of the time, Pallas kernels for 9%

profile of v4, /device:TPU:1, one launch (start us, length us, event | category | flops | bytes accessed | tf_op | source)
XLA Modules:
  0.0 159.4 jit_solution(988377448006248419)
XLA Ops:
  0.6 0.7 dynamic-slice_bitcast_fusion
  1.4 0.8 views.1
  2.2 9.0 %all-to-all-start = ((bf16[8,2,32,256]{3,2,1,0:T(8,128)(2,1)}), bf16[8,2,32,256]{3,2,1,0:T(8,128)(2,1)S(1)}, u32[]{:S(2)}, u32[]{:S(2)}) async-start(bf16[8,2,32,256]{3,2,1,0:T(8,128)(2,1)} %views.1), calls=%async_computation | async-start | bytes 524288 | tf_op jit(solution)/shard_map/all_to_all | solution.py:237
  11.2 0.0 copy-start
  11.2 1.0 copy-done
  12.3 0.2 book.1.refs_0_
  12.5 1.4 collective-permute-start.1
  13.8 1.5 collective-permute-start
  15.4 5.4 %collective-permute-done.1.refs_3_ = bf16[512,256]{1,0:T(8,128)(2,1)S(1)} collective-permute-done((bf16[512,256]{1,0:T(8,128)(2,1)S(1)}, bf16[512,256]{1,0:T(8,128)(2,1)S(1)}, u32[]{:S(2)}, u32[]{:S(2)}) %collective-permute-start.1) | collective-permute-done | bytes 262176 | tf_op jit(solution)/shard_map/ppermute | solution.py:240
  20.7 0.0 collective-permute-done.refs_1_
  20.7 0.9 all-to-all-done
  21.6 1.1 broadcast_in_dim.2
  22.7 4.0 %all-to-all-start.1 = ((bf16[4,8,2,32,256]{4,3,2,1,0:T(8,128)(2,1)}), bf16[4,8,2,32,256]{4,3,2,1,0:T(8,128)(2,1)S(1)}, u32[]{:S(2)}, u32[]{:S(2)}) async-start(bf16[4,8,2,32,256]{4,3,2,1,0:T(8,128)(2,1)} %broadcast_in_dim.2), calls=%async_computation.1 | async-start | bytes 2097152 | tf_op jit(solution)/shard_map/all_to_all | solution.py:237
  26.7 2.9 %collective-permute-start.2 = (bf16[512,256]{1,0:T(8,128)(2,1)S(1)}, bf16[512,256]{1,0:T(8,128)(2,1)S(1)}, u32[]{:S(2)}, u32[]{:S(2)}) collective-permute-start(bf16[512,256]{1,0:T(8,128)(2,1)S(1)} %book.1.refs_0_), channel_id=1, source_target_pairs={{4,0},{6,2},{0,4},{2,6},{5,1},{7,3},{1,5},{3,7},{12,8},{14,10},{8,... | collective-permute-start | bytes 786440 | tf_op jit(solution)/shard_map/ppermute | solution.py:240
  29.7 3.0 %collective-permute-start.3 = (bf16[512,256]{1,0:T(8,128)(2,1)S(1)}, bf16[512,256]{1,0:T(8,128)(2,1)S(1)}, u32[]{:S(2)}, u32[]{:S(2)}) collective-permute-start(bf16[512,256]{1,0:T(8,128)(2,1)S(1)} %book.1.refs_0_), channel_id=1, source_target_pairs={{0,8},{8,0},{1,9},{9,1},{2,10},{10,2},{3,11},{11,3},{4,12},{12,4},... | collective-permute-start | bytes 786440 | tf_op jit(solution)/shard_map/ppermute | solution.py:243
  32.7 0.8 collective-permute-done.2.refs_2_
  33.5 3.9 %collective-permute-start.5 = (bf16[512,256]{1,0:T(8,128)(2,1)S(1)}, bf16[512,256]{1,0:T(8,128)(2,1)S(1)}, u32[]{:S(2)}, u32[]{:S(2)}) collective-permute-start(bf16[512,256]{1,0:T(8,128)(2,1)S(1)} %collective-permute-done.2.refs_2_), channel_id=1, source_target_pairs={{0,8},{8,0},{1,9},{9,1},{2,10},{10,2},{3,11},{11,3},{4,12},{12,4},... | collective-permute-start | bytes 786440 | tf_op jit(solution)/shard_map/ppermute | solution.py:243
  37.4 0.0 collective-permute-start.4
  37.4 0.5 collective-permute-start.6
  37.9 0.1 pad_add_fusion.pos_ref
  37.9 0.0 collective-permute-done.3.refs_4_.refs_1_.refs_0_
  38.0 0.6 collective-permute-done.5.refs_6_
  38.5 0.4 collective-permute-done.4.refs_5_
  38.9 0.4 collective-permute-done.6.refs_7_
  39.3 0.0 all-to-all-done.1.rows_ref.refs_3_
  39.3 2.9 %expo.1 = (f32[8,1024,512]{2,1,0:T(8,128)S(1)}, f32[8,8,512]{2,1,0:T(8,128)S(1)}) custom-call(s32[3]{0:T(128)S(1)} %pad_add_fusion.pos_ref, bf16[4,8,2,32,256]{4,3,2,1,0:T(8,128)(2,1)S(1)} %all-to-all-done.1.rows_ref.refs_3_, bf16[512,256]{1,0:T(8,128)(2,1)S(1)} %book.1.refs_0_, bf16[512,256]{1,0:T(8,128)(2,1)S(1)} %collective-permute-done.refs_1_, ...), custom_call_target="tpu_custom_call" | custom-call | tf_op jit(solution)/shard_map/expo/pallas_call | solution.py:269
  42.2 12.9 %all_to_all.40.columns_ref = f32[8,8,512]{2,1,0:T(8,128)S(1)} all-to-all(f32[8,8,512]{2,1,0:T(8,128)S(1)} %get-tuple-element.31), channel_id=1, replica_groups=mesh['xh'=2,'z'=8,'c'=2,'y'=4,'xl'=2] {'c','y'}, dimensions={0} | all-to-all | bytes 262144 | tf_op jit(solution)/shard_map/all_to_all | solution.py:237
  55.2 0.7 collective-permute-start.8
  55.9 2.0 %collective-permute-start.7 = (bf16[4,8,2,32,256]{4,3,2,1,0:T(8,128)(2,1)S(1)}, bf16[4,8,2,32,256]{4,3,2,1,0:T(8,128)(2,1)S(1)}, u32[]{:S(2)}, u32[]{:S(2)}) collective-permute-start(bf16[4,8,2,32,256]{4,3,2,1,0:T(8,128)(2,1)S(1)} %all-to-all-done.1.rows_ref.refs_3_), channel_id=1, source_target_pairs={{2,0},{4,2},{6,4},{0,6},{3,1},{5,3},{7,5},{1,7},{10,8},{12,10},{14... | collective-permute-start | bytes 3145736 | tf_op jit(solution)/shard_map/ppermute | solution.py:240
  57.8 2.5 %totals.1.total_ref = f32[8,128]{1,0:T(8,128)S(1)} custom-call(bf16[4,8,2,32,256]{4,3,2,1,0:T(8,128)(2,1)S(1)} %all-to-all-done.1.rows_ref.refs_3_, bf16[512,256]{1,0:T(8,128)(2,1)S(1)} %book.1.refs_0_, bf16[512,256]{1,0:T(8,128)(2,1)S(1)} %collective-permute-done.refs_1_, bf16[512,256]{1,0:T(8,128)(2,1)S(1)} %collective-permute-done.2.refs_2_, ...), custom_call_target="tpu_custom_call" | custom-call | flops 2147483648 | bytes 3145728 | tf_op jit(solution)/shard_map/totals/pallas_call | solution.py:280
  60.3 1.9 %row_sums.2 = f32[32,8,128]{2,1,0:T(8,128)S(1)} custom-call(s32[3]{0:T(128)S(1)} %pad_add_fusion.pos_ref, f32[8,8,512]{2,1,0:T(8,128)S(1)} %all_to_all.40.columns_ref, f32[8,1024,512]{2,1,0:T(8,128)S(1)} %get-tuple-element.35.expd_ref), custom_call_target="tpu_custom_call" | custom-call | tf_op jit(solution)/shard_map/row_sums/pallas_call | solution.py:294
  62.3 15.9 %all_to_all.41.sums_ref = f32[32,8,128]{2,1,0:T(8,128)S(1)} all-to-all(f32[32,8,128]{2,1,0:T(8,128)S(1)} %row_sums.2), channel_id=1, replica_groups=mesh['xh'=2,'z'=8,'c'=2,'y'=4,'xl'=2] {'xh','z','xl'}, dimensions={0} | all-to-all | bytes 262144 | tf_op jit(solution)/shard_map/all_to_all | solution.py:237
  78.2 2.0 %column_sums.2 = f32[8,8,512]{2,1,0:T(8,128)S(1)} custom-call(s32[3]{0:T(128)S(1)} %pad_add_fusion.pos_ref, f32[32,8,128]{2,1,0:T(8,128)S(1)} %all_to_all.41.sums_ref, f32[8,1024,512]{2,1,0:T(8,128)S(1)} %get-tuple-element.35.expd_ref), custom_call_target="tpu_custom_call" | custom-call | tf_op jit(solution)/shard_map/column_sums/pallas_call | solution.py:307
  80.2 0.6 collective-permute-done.8.refs_5_
  80.7 0.0 collective-permute-done.7.refs_4_
  80.7 10.4 %all_to_all.42.columns_ref = f32[8,8,512]{2,1,0:T(8,128)S(1)} all-to-all(f32[8,8,512]{2,1,0:T(8,128)S(1)} %column_sums.2), channel_id=1, replica_groups=mesh['xh'=2,'z'=8,'c'=2,'y'=4,'xl'=2] {'c','y'}, dimensions={0} | all-to-all | bytes 262144 | tf_op jit(solution)/shard_map/all_to_all | solution.py:237
  91.1 1.9 %row_sums.3 = f32[32,8,128]{2,1,0:T(8,128)S(1)} custom-call(s32[3]{0:T(128)S(1)} %pad_add_fusion.pos_ref, f32[8,8,512]{2,1,0:T(8,128)S(1)} %all_to_all.42.columns_ref, f32[8,1024,512]{2,1,0:T(8,128)S(1)} %get-tuple-element.35.expd_ref), custom_call_target="tpu_custom_call" | custom-call | tf_op jit(solution)/shard_map/row_sums/pallas_call | solution.py:294
  93.2 0.8 collective-permute-start.10
  93.9 2.0 %collective-permute-start.9 = (bf16[2,8,2,32,256]{4,3,2,1,0:T(8,128)(2,1)S(1)}, bf16[2,8,2,32,256]{4,3,2,1,0:T(8,128)(2,1)S(1)}, u32[]{:S(2)}, u32[]{:S(2)}) collective-permute-start(bf16[2,8,2,32,256]{4,3,2,1,0:T(8,128)(2,1)S(1)} %slice.6), channel_id=1, source_target_pairs={{2,0},{4,2},{6,4},{0,6},{3,1},{5,3},{7,5},{1,7},{10,8},{12,10},{14... | collective-permute-start | bytes 1572872 | tf_op jit(solution)/shard_map/ppermute | solution.py:240
  95.9 15.9 %all_to_all.43.sums_ref = f32[32,8,128]{2,1,0:T(8,128)S(1)} all-to-all(f32[32,8,128]{2,1,0:T(8,128)S(1)} %row_sums.3), channel_id=1, replica_groups=mesh['xh'=2,'z'=8,'c'=2,'y'=4,'xl'=2] {'xh','z','xl'}, dimensions={0} | all-to-all | bytes 262144 | tf_op jit(solution)/shard_map/all_to_all | solution.py:237
  111.8 2.0 %column_sums.3 = f32[8,8,512]{2,1,0:T(8,128)S(1)} custom-call(s32[3]{0:T(128)S(1)} %pad_add_fusion.pos_ref, f32[32,8,128]{2,1,0:T(8,128)S(1)} %all_to_all.43.sums_ref, f32[8,1024,512]{2,1,0:T(8,128)S(1)} %get-tuple-element.35.expd_ref), custom_call_target="tpu_custom_call" | custom-call | tf_op jit(solution)/shard_map/column_sums/pallas_call | solution.py:307
  113.8 0.0 collective-permute-done.10.refs_7_
  113.8 0.0 collective-permute-done.9.refs_6_
  113.8 9.9 %all_to_all.44.columns_ref = f32[8,8,512]{2,1,0:T(8,128)S(1)} all-to-all(f32[8,8,512]{2,1,0:T(8,128)S(1)} %column_sums.3), channel_id=1, replica_groups=mesh['xh'=2,'z'=8,'c'=2,'y'=4,'xl'=2] {'c','y'}, dimensions={0} | all-to-all | bytes 262144 | tf_op jit(solution)/shard_map/all_to_all | solution.py:237
  123.7 0.0 copy-start.1
  123.7 0.0 copy-start.2
  123.7 0.0 copy-start.3
  123.7 1.9 %last_row_sums.1 = f32[32,2,8,128]{3,2,1,0:T(8,128)S(1)} custom-call(s32[3]{0:T(128)S(1)} %pad_add_fusion.pos_ref, f32[8,8,512]{2,1,0:T(8,128)S(1)} %all_to_all.44.columns_ref, f32[8,1024,512]{2,1,0:T(8,128)S(1)} %get-tuple-element.35.expd_ref, f32[8,128]{1,0:T(8,128)S(1)} %totals.1.total_ref), custom_call_target="tpu_custom_call" | custom-call | tf_op jit(solution)/shard_map/last_row_sums/pallas_call | solution.py:325
  125.7 15.9 %all_to_all.45.sums_ref = f32[32,2,8,128]{3,2,1,0:T(8,128)S(1)} all-to-all(f32[32,2,8,128]{3,2,1,0:T(8,128)S(1)} %last_row_sums.1), channel_id=1, replica_groups=mesh['xh'=2,'z'=8,'c'=2,'y'=4,'xl'=2] {'xh','z','xl'}, dimensions={0} | all-to-all | bytes 524288 | tf_op jit(solution)/shard_map/all_to_all | solution.py:237
  141.6 1.0 collective-permute-start.13
  142.6 0.1 collective-permute-start.12
  142.7 2.5 %collective-permute-start.11 = (f32[2,8,128]{2,1,0:T(8,128)S(1)}, f32[2,8,128]{2,1,0:T(8,128)S(1)}, u32[]{:S(2)}, u32[]{:S(2)}) collective-permute-start(f32[2,8,128]{2,1,0:T(8,128)S(1)} %scales.1.refs_2_), channel_id=1, source_target_pairs={{2,0},{4,2},{6,4},{0,6},{3,1},{5,3},{7,5},{1,7},{10,8},{12,10},{14... | collective-permute-start | bytes 24584 | tf_op jit(solution)/shard_map/ppermute | solution.py:240
  145.2 2.6 %grad_of_own_rows.1 = (f32[512,256]{1,0:T(8,128)S(1)}, f32[512,256]{1,0:T(8,128)S(1)}) custom-call(s32[3]{0:T(128)S(1)} %pad_add_fusion.pos_ref, f32[8,8,512]{2,1,0:T(8,128)S(1)} %all_to_all.44.columns_ref, bf16[512,256]{1,0:T(8,128)(2,1)S(1)} %book.1.refs_0_, bf16[512,256]{1,0:T(8,128)(2,1)S(1)} %collective-permute-done.3.refs_4_.refs_1_.refs_0_, ...), custom_call_target="tpu_custom_call" | custom-call | flops 1610612736 | bytes 6291456 | tf_op jit(solution)/shard_map/grad_of_own_rows/pallas_call | solution.py:349
  147.9 0.0 collective-permute-done.13.refs_3_
  147.9 0.0 collective-permute-done.12.refs_2_
  147.9 0.0 collective-permute-done.11.refs_1_
  147.9 3.5 %grad_of_other.1 = f32[512,256]{1,0:T(8,128)S(1)} custom-call(s32[3]{0:T(128)S(1)} %pad_add_fusion.pos_ref, f32[8,8,512]{2,1,0:T(8,128)S(1)} %all_to_all.44.columns_ref, bf16[512,256]{1,0:T(8,128)(2,1)S(1)} %collective-permute-done.3.refs_4_.refs_1_.refs_0_, f32[2,8,128]{2,1,0:T(8,128)S(1)} %collective-permute-done.11.refs_1_, ...), custom_call_target="tpu_custom_call" | custom-call | flops 2415919104 | bytes 6291456 | tf_op jit(solution)/shard_map/grad_of_other/pallas_call | solution.py:349
  151.4 2.8 %collective-permute-start.14 = (f32[512,256]{1,0:T(8,128)S(1)}, f32[512,256]{1,0:T(8,128)S(1)}, u32[]{:S(2)}, u32[]{:S(2)}) collective-permute-start(f32[512,256]{1,0:T(8,128)S(1)} %grad_of_other.1), channel_id=1, source_target_pairs={{0,8},{8,0},{1,9},{9,1},{2,10},{10,2},{3,11},{11,3},{4,12},{12,4},... | collective-permute-start | bytes 1572872 | tf_op jit(solution)/shard_map/ppermute | solution.py:243
  154.3 3.5 %grad_of_own.1.own_ref = f32[512,256]{1,0:T(8,128)S(1)} custom-call(s32[3]{0:T(128)S(1)} %pad_add_fusion.pos_ref, f32[8,8,512]{2,1,0:T(8,128)S(1)} %all_to_all.44.columns_ref, bf16[512,256]{1,0:T(8,128)(2,1)S(1)} %book.1.refs_0_, f32[2,8,128]{2,1,0:T(8,128)S(1)} %collective-permute-done.11.refs_1_, f32[2,8,128]{2,1,0:T(8,128)S(1)} %collective-permute-done.12.refs_2_, ...), custom_call_target="tpu_custom_call" | custom-call | flops 2415919104 | bytes 6291456 | tf_op jit(solution)/shard_map/grad_of_own/pallas_call | solution.py:349
  157.8 0.0 collective-permute-done.14.other_ref
  157.8 0.0 copy-done.1
  157.8 0.0 copy-done.2
  157.8 0.0 copy-done.3
  157.8 1.6 update.1
  (4 shorter events, 0.1 us)
Async XLA Ops:
  2.2 19.4 %all-to-all-start = ((bf16[8,2,32,256]{3,2,1,0:T(8,128)(2,1)}), bf16[8,2,32,256]{3,2,1,0:T(8,128)(2,1)S(1)}, u32[]{:S(2)}, u32[]{:S(2)}) async-start(bf16[8,2,32,256]{3,2,1,0:T(8,128)(2,1)} %views.1), calls=%async_computation | async-start | bytes 524288 | tf_op jit(solution)/shard_map/all_to_all | solution.py:237
  11.2 1.0 copy-start
  12.5 8.3 %collective-permute-start.1 = (bf16[512,256]{1,0:T(8,128)(2,1)S(1)}, bf16[512,256]{1,0:T(8,128)(2,1)S(1)}, u32[]{:S(2)}, u32[]{:S(2)}) collective-permute-start(bf16[512,256]{1,0:T(8,128)(2,1)S(1)} %book.1.refs_0_), channel_id=1, source_target_pairs={{6,0},{0,2},{2,4},{4,6},{7,1},{1,3},{3,5},{5,7},{14,8},{8,10},{10,... | collective-permute-start | bytes 786440 | tf_op jit(solution)/shard_map/ppermute | solution.py:240
  13.8 6.9 %collective-permute-start = (bf16[512,256]{1,0:T(8,128)(2,1)S(1)}, bf16[512,256]{1,0:T(8,128)(2,1)S(1)}, u32[]{:S(2)}, u32[]{:S(2)}) collective-permute-start(bf16[512,256]{1,0:T(8,128)(2,1)S(1)} %book.1.refs_0_), channel_id=1, source_target_pairs={{2,0},{4,2},{6,4},{0,6},{3,1},{5,3},{7,5},{1,7},{10,8},{12,10},{14... | collective-permute-start | bytes 786440 | tf_op jit(solution)/shard_map/ppermute | solution.py:240
  22.7 16.5 %all-to-all-start.1 = ((bf16[4,8,2,32,256]{4,3,2,1,0:T(8,128)(2,1)}), bf16[4,8,2,32,256]{4,3,2,1,0:T(8,128)(2,1)S(1)}, u32[]{:S(2)}, u32[]{:S(2)}) async-start(bf16[4,8,2,32,256]{4,3,2,1,0:T(8,128)(2,1)} %broadcast_in_dim.2), calls=%async_computation.1 | async-start | bytes 2097152 | tf_op jit(solution)/shard_map/all_to_all | solution.py:237
  26.7 6.7 %collective-permute-start.2 = (bf16[512,256]{1,0:T(8,128)(2,1)S(1)}, bf16[512,256]{1,0:T(8,128)(2,1)S(1)}, u32[]{:S(2)}, u32[]{:S(2)}) collective-permute-start(bf16[512,256]{1,0:T(8,128)(2,1)S(1)} %book.1.refs_0_), channel_id=1, source_target_pairs={{4,0},{6,2},{0,4},{2,6},{5,1},{7,3},{1,5},{3,7},{12,8},{14,10},{8,... | collective-permute-start | bytes 786440 | tf_op jit(solution)/shard_map/ppermute | solution.py:240
  29.7 8.3 %collective-permute-start.3 = (bf16[512,256]{1,0:T(8,128)(2,1)S(1)}, bf16[512,256]{1,0:T(8,128)(2,1)S(1)}, u32[]{:S(2)}, u32[]{:S(2)}) collective-permute-start(bf16[512,256]{1,0:T(8,128)(2,1)S(1)} %book.1.refs_0_), channel_id=1, source_target_pairs={{0,8},{8,0},{1,9},{9,1},{2,10},{10,2},{3,11},{11,3},{4,12},{12,4},... | collective-permute-start | bytes 786440 | tf_op jit(solution)/shard_map/ppermute | solution.py:243
  33.5 5.1 %collective-permute-start.5 = (bf16[512,256]{1,0:T(8,128)(2,1)S(1)}, bf16[512,256]{1,0:T(8,128)(2,1)S(1)}, u32[]{:S(2)}, u32[]{:S(2)}) collective-permute-start(bf16[512,256]{1,0:T(8,128)(2,1)S(1)} %collective-permute-done.2.refs_2_), channel_id=1, source_target_pairs={{0,8},{8,0},{1,9},{9,1},{2,10},{10,2},{3,11},{11,3},{4,12},{12,4},... | collective-permute-start | bytes 786440 | tf_op jit(solution)/shard_map/ppermute | solution.py:243
  37.4 1.5 collective-permute-start.4
  37.4 1.9 %collective-permute-start.6 = (bf16[512,256]{1,0:T(8,128)(2,1)S(1)}, bf16[512,256]{1,0:T(8,128)(2,1)S(1)}, u32[]{:S(2)}, u32[]{:S(2)}) collective-permute-start(bf16[512,256]{1,0:T(8,128)(2,1)S(1)} %collective-permute-done.1.refs_3_), channel_id=1, source_target_pairs={{0,8},{8,0},{1,9},{9,1},{2,10},{10,2},{3,11},{11,3},{4,12},{12,4},... | collective-permute-start | bytes 786440 | tf_op jit(solution)/shard_map/ppermute | solution.py:243
  55.2 25.6 %collective-permute-start.8 = (bf16[4,8,2,32,256]{4,3,2,1,0:T(8,128)(2,1)S(1)}, bf16[4,8,2,32,256]{4,3,2,1,0:T(8,128)(2,1)S(1)}, u32[]{:S(2)}, u32[]{:S(2)}) collective-permute-start(bf16[4,8,2,32,256]{4,3,2,1,0:T(8,128)(2,1)S(1)} %all-to-all-done.1.rows_ref.refs_3_), channel_id=1, source_target_pairs={{6,0},{0,2},{2,4},{4,6},{7,1},{1,3},{3,5},{5,7},{14,8},{8,10},{10,... | collective-permute-start | bytes 3145736 | tf_op jit(solution)/shard_map/ppermute | solution.py:240
  55.9 24.9 %collective-permute-start.7 = (bf16[4,8,2,32,256]{4,3,2,1,0:T(8,128)(2,1)S(1)}, bf16[4,8,2,32,256]{4,3,2,1,0:T(8,128)(2,1)S(1)}, u32[]{:S(2)}, u32[]{:S(2)}) collective-permute-start(bf16[4,8,2,32,256]{4,3,2,1,0:T(8,128)(2,1)S(1)} %all-to-all-done.1.rows_ref.refs_3_), channel_id=1, source_target_pairs={{2,0},{4,2},{6,4},{0,6},{3,1},{5,3},{7,5},{1,7},{10,8},{12,10},{14... | collective-permute-start | bytes 3145736 | tf_op jit(solution)/shard_map/ppermute | solution.py:240
  93.2 20.6 %collective-permute-start.10 = (bf16[2,8,2,32,256]{4,3,2,1,0:T(8,128)(2,1)S(1)}, bf16[2,8,2,32,256]{4,3,2,1,0:T(8,128)(2,1)S(1)}, u32[]{:S(2)}, u32[]{:S(2)}) collective-permute-start(bf16[2,8,2,32,256]{4,3,2,1,0:T(8,128)(2,1)S(1)} %slice.7), channel_id=1, source_target_pairs={{6,0},{0,2},{2,4},{4,6},{7,1},{1,3},{3,5},{5,7},{14,8},{8,10},{10,... | collective-permute-start | bytes 1572872 | tf_op jit(solution)/shard_map/ppermute | solution.py:240
  93.9 19.9 %collective-permute-start.9 = (bf16[2,8,2,32,256]{4,3,2,1,0:T(8,128)(2,1)S(1)}, bf16[2,8,2,32,256]{4,3,2,1,0:T(8,128)(2,1)S(1)}, u32[]{:S(2)}, u32[]{:S(2)}) collective-permute-start(bf16[2,8,2,32,256]{4,3,2,1,0:T(8,128)(2,1)S(1)} %slice.6), channel_id=1, source_target_pairs={{2,0},{4,2},{6,4},{0,6},{3,1},{5,3},{7,5},{1,7},{10,8},{12,10},{14... | collective-permute-start | bytes 1572872 | tf_op jit(solution)/shard_map/ppermute | solution.py:240
  123.7 34.1 %copy-start.1 = (f32[1,512,256]{2,1,0:T(8,128)S(1)}, f32[1,512,256]{2,1,0:T(8,128)}, u32[]{:S(2)}) copy-start(f32[1,512,256]{2,1,0:T(8,128)} %proto_ref.3) | copy-start | bytes 1572868
  123.7 34.1 %copy-start.2 = (f32[1,512,256]{2,1,0:T(8,128)S(1)}, f32[1,512,256]{2,1,0:T(8,128)}, u32[]{:S(2)}) copy-start(f32[1,512,256]{2,1,0:T(8,128)} %first_ref.1) | copy-start | bytes 1572868
  123.7 34.1 %copy-start.3 = (f32[1,512,256]{2,1,0:T(8,128)S(1)}, f32[1,512,256]{2,1,0:T(8,128)}, u32[]{:S(2)}) copy-start(f32[1,512,256]{2,1,0:T(8,128)} %second_ref.1) | copy-start | bytes 1572868
  141.6 6.3 %collective-permute-start.13 = (f32[2,8,128]{2,1,0:T(8,128)S(1)}, f32[2,8,128]{2,1,0:T(8,128)S(1)}, u32[]{:S(2)}, u32[]{:S(2)}) collective-permute-start(f32[2,8,128]{2,1,0:T(8,128)S(1)} %scales.1.refs_2_), channel_id=1, source_target_pairs={{4,0},{6,2},{0,4},{2,6},{5,1},{7,3},{1,5},{3,7},{12,8},{14,10},{8,... | collective-permute-start | bytes 24584 | tf_op jit(solution)/shard_map/ppermute | solution.py:240
  142.6 5.3 %collective-permute-start.12 = (f32[2,8,128]{2,1,0:T(8,128)S(1)}, f32[2,8,128]{2,1,0:T(8,128)S(1)}, u32[]{:S(2)}, u32[]{:S(2)}) collective-permute-start(f32[2,8,128]{2,1,0:T(8,128)S(1)} %scales.1.refs_2_), channel_id=1, source_target_pairs={{6,0},{0,2},{2,4},{4,6},{7,1},{1,3},{3,5},{5,7},{14,8},{8,10},{10,... | collective-permute-start | bytes 24584 | tf_op jit(solution)/shard_map/ppermute | solution.py:240
  142.7 5.2 %collective-permute-start.11 = (f32[2,8,128]{2,1,0:T(8,128)S(1)}, f32[2,8,128]{2,1,0:T(8,128)S(1)}, u32[]{:S(2)}, u32[]{:S(2)}) collective-permute-start(f32[2,8,128]{2,1,0:T(8,128)S(1)} %scales.1.refs_2_), channel_id=1, source_target_pairs={{2,0},{4,2},{6,4},{0,6},{3,1},{5,3},{7,5},{1,7},{10,8},{12,10},{14... | collective-permute-start | bytes 24584 | tf_op jit(solution)/shard_map/ppermute | solution.py:240
  151.4 6.4 %collective-permute-start.14 = (f32[512,256]{1,0:T(8,128)S(1)}, f32[512,256]{1,0:T(8,128)S(1)}, u32[]{:S(2)}, u32[]{:S(2)}) collective-permute-start(f32[512,256]{1,0:T(8,128)S(1)} %grad_of_other.1), channel_id=1, source_target_pairs={{0,8},{8,0},{1,9},{9,1},{2,10},{10,2},{3,11},{11,3},{4,12},{12,4},... | collective-permute-start | bytes 1572872 | tf_op jit(solution)/shard_map/ppermute | solution.py:243

commit v5 on v4

--- a/solution.py
+++ b/solution.py
@@ -303,7 +303,7 @@
         if step == 1:
             high, copies = lax.optimization_barrier((high, copies))
             far_high = from_y(high, -1)
-        sums = exchange(copies, ("xh", "z", "xl"))
+        sums = exchange(copies, ("z", "xh", "xl"))
         copies = pl.pallas_call(
             column_kernel,
             out_shape=f32(GROUP, GROUP, OWNED),
@@ -331,7 +331,7 @@
         compiler_params=params(8),
         name="last_row_sums",
     )(pos, columns, expd, total)
-    sums = exchange(copies, ("xh", "z", "xl"))
+    sums = exchange(copies, ("z", "xh", "xl"))
     copies = pl.pallas_call(
         scales_kernel,
         out_shape=f32(2, 8, 128),

time: 160 us -> 159 us (level)
  blocking collectives: 80.9 us -> 78.4 us
    all_to_all x6, blocking collectives: 80.9 us -> 78.4 us  [exchange(): return lax.all_to_all(copies, axes, 0, 0, tiled=True)]
where the time goes in v5:
time: 159 us; the launch traced here: 158 us
  blocking collectives  78.4 us (49%)
  starting transfers between devices  38.6 us (24%)
  Pallas kernels  27.5 us (17%)
  waiting for transfers between devices  9.48 us (6%)
  local copies, waits for them, and re-layouts  3 us (2%)
    all_to_all x6, blocking collectives, exchange(): return lax.all_to_all(copies, axes, 0, 0, tiled=True)  78.4 us
    ppermute x10, starting transfers between devices, from_y(): lax.ppermute(values, 'y', [((i + distance) % 4, i) for i in range(4)])  14.9 us
    all_to_all x2, starting transfers between devices, exchange(): return lax.all_to_all(copies, axes, 0, 0, tiled=True)  13 us
    ppermute x5, starting transfers between devices, from_core(): return lax.ppermute(values, 'c', [(0, 1), (1, 0)])  10.7 us
    pallas_call x3, Pallas kernels, grad_of(): pl.pallas_call(functools.partial(grad_kernel, halves, blocks), out_shape=...  9.7 us
    ppermute x10, waiting for transfers between devices, from_y(): lax.ppermute(values, 'y', [((i + distance) % 4, i) for i in range(4)])  7.29 us
    pallas_call x2, Pallas kernels, body(): pl.pallas_call(column_kernel, out_shape=f32(GROUP, GROUP, OWNED), in_spec...  3.97 us
    pallas_call x2, Pallas kernels, body(): pl.pallas_call(row_kernel, out_shape=f32(ROW_PEERS, 8, 128), in_specs=[SM...  3.89 us
  transfers between devices with their start and end apart: 17, of which 7 were waited for; matrix products, arithmetic and copies ran while one was open for 0% of the time, Pallas kernels for 9%

profile of v5, /device:TPU:1, one launch (start us, length us, event | category | flops | bytes accessed | tf_op | source)
XLA Modules:
  0.0 158.0 jit_solution(3856276820625885088)
XLA Ops:
  0.6 0.7 dynamic-slice_bitcast_fusion
  1.4 0.8 views.1
  2.2 9.0 %all-to-all-start = ((bf16[8,2,32,256]{3,2,1,0:T(8,128)(2,1)}), bf16[8,2,32,256]{3,2,1,0:T(8,128)(2,1)S(1)}, u32[]{:S(2)}, u32[]{:S(2)}) async-start(bf16[8,2,32,256]{3,2,1,0:T(8,128)(2,1)} %views.1), calls=%async_computation | async-start | bytes 524288 | tf_op jit(solution)/shard_map/all_to_all | solution.py:237
  11.2 0.0 copy-start
  11.2 1.0 copy-done
  12.3 0.2 book.1.refs_0_
  12.5 1.4 collective-permute-start.1
  13.8 1.5 collective-permute-start
  15.4 5.4 %collective-permute-done.1.refs_3_ = bf16[512,256]{1,0:T(8,128)(2,1)S(1)} collective-permute-done((bf16[512,256]{1,0:T(8,128)(2,1)S(1)}, bf16[512,256]{1,0:T(8,128)(2,1)S(1)}, u32[]{:S(2)}, u32[]{:S(2)}) %collective-permute-start.1) | collective-permute-done | bytes 262176 | tf_op jit(solution)/shard_map/ppermute | solution.py:240
  20.7 0.0 collective-permute-done.refs_1_
  20.7 0.9 all-to-all-done
  21.6 1.1 broadcast_in_dim.2
  22.7 4.0 %all-to-all-start.1 = ((bf16[4,8,2,32,256]{4,3,2,1,0:T(8,128)(2,1)}), bf16[4,8,2,32,256]{4,3,2,1,0:T(8,128)(2,1)S(1)}, u32[]{:S(2)}, u32[]{:S(2)}) async-start(bf16[4,8,2,32,256]{4,3,2,1,0:T(8,128)(2,1)} %broadcast_in_dim.2), calls=%async_computation.1 | async-start | bytes 2097152 | tf_op jit(solution)/shard_map/all_to_all | solution.py:237
  26.7 2.9 %collective-permute-start.2 = (bf16[512,256]{1,0:T(8,128)(2,1)S(1)}, bf16[512,256]{1,0:T(8,128)(2,1)S(1)}, u32[]{:S(2)}, u32[]{:S(2)}) collective-permute-start(bf16[512,256]{1,0:T(8,128)(2,1)S(1)} %book.1.refs_0_), channel_id=1, source_target_pairs={{4,0},{6,2},{0,4},{2,6},{5,1},{7,3},{1,5},{3,7},{12,8},{14,10},{8,... | collective-permute-start | bytes 786440 | tf_op jit(solution)/shard_map/ppermute | solution.py:240
  29.7 3.0 %collective-permute-start.3 = (bf16[512,256]{1,0:T(8,128)(2,1)S(1)}, bf16[512,256]{1,0:T(8,128)(2,1)S(1)}, u32[]{:S(2)}, u32[]{:S(2)}) collective-permute-start(bf16[512,256]{1,0:T(8,128)(2,1)S(1)} %book.1.refs_0_), channel_id=1, source_target_pairs={{0,8},{8,0},{1,9},{9,1},{2,10},{10,2},{3,11},{11,3},{4,12},{12,4},... | collective-permute-start | bytes 786440 | tf_op jit(solution)/shard_map/ppermute | solution.py:243
  32.7 0.8 collective-permute-done.2.refs_2_
  33.5 3.9 %collective-permute-start.5 = (bf16[512,256]{1,0:T(8,128)(2,1)S(1)}, bf16[512,256]{1,0:T(8,128)(2,1)S(1)}, u32[]{:S(2)}, u32[]{:S(2)}) collective-permute-start(bf16[512,256]{1,0:T(8,128)(2,1)S(1)} %collective-permute-done.2.refs_2_), channel_id=1, source_target_pairs={{0,8},{8,0},{1,9},{9,1},{2,10},{10,2},{3,11},{11,3},{4,12},{12,4},... | collective-permute-start | bytes 786440 | tf_op jit(solution)/shard_map/ppermute | solution.py:243
  37.4 0.0 collective-permute-start.4
  37.4 0.5 collective-permute-start.6
  37.9 0.1 pad_add_fusion.pos_ref
  37.9 0.0 collective-permute-done.3.refs_4_.refs_1_.refs_0_
  38.0 0.6 collective-permute-done.5.refs_6_
  38.5 0.4 collective-permute-done.4.refs_5_
  38.9 0.4 collective-permute-done.6.refs_7_
  39.3 0.0 all-to-all-done.1.rows_ref.refs_3_
  39.3 2.9 %expo.1 = (f32[8,1024,512]{2,1,0:T(8,128)S(1)}, f32[8,8,512]{2,1,0:T(8,128)S(1)}) custom-call(s32[3]{0:T(128)S(1)} %pad_add_fusion.pos_ref, bf16[4,8,2,32,256]{4,3,2,1,0:T(8,128)(2,1)S(1)} %all-to-all-done.1.rows_ref.refs_3_, bf16[512,256]{1,0:T(8,128)(2,1)S(1)} %book.1.refs_0_, bf16[512,256]{1,0:T(8,128)(2,1)S(1)} %collective-permute-done.refs_1_, ...), custom_call_target="tpu_custom_call" | custom-call | tf_op jit(solution)/shard_map/expo/pallas_call | solution.py:269
  42.2 12.9 %all_to_all.40.columns_ref = f32[8,8,512]{2,1,0:T(8,128)S(1)} all-to-all(f32[8,8,512]{2,1,0:T(8,128)S(1)} %get-tuple-element.31), channel_id=1, replica_groups=mesh['xh'=2,'z'=8,'c'=2,'y'=4,'xl'=2] {'c','y'}, dimensions={0} | all-to-all | bytes 262144 | tf_op jit(solution)/shard_map/all_to_all | solution.py:237
  55.2 0.7 collective-permute-start.8
  55.9 2.0 %collective-permute-start.7 = (bf16[4,8,2,32,256]{4,3,2,1,0:T(8,128)(2,1)S(1)}, bf16[4,8,2,32,256]{4,3,2,1,0:T(8,128)(2,1)S(1)}, u32[]{:S(2)}, u32[]{:S(2)}) collective-permute-start(bf16[4,8,2,32,256]{4,3,2,1,0:T(8,128)(2,1)S(1)} %all-to-all-done.1.rows_ref.refs_3_), channel_id=1, source_target_pairs={{2,0},{4,2},{6,4},{0,6},{3,1},{5,3},{7,5},{1,7},{10,8},{12,10},{14... | collective-permute-start | bytes 3145736 | tf_op jit(solution)/shard_map/ppermute | solution.py:240
  57.8 2.5 %totals.1.total_ref = f32[8,128]{1,0:T(8,128)S(1)} custom-call(bf16[4,8,2,32,256]{4,3,2,1,0:T(8,128)(2,1)S(1)} %all-to-all-done.1.rows_ref.refs_3_, bf16[512,256]{1,0:T(8,128)(2,1)S(1)} %book.1.refs_0_, bf16[512,256]{1,0:T(8,128)(2,1)S(1)} %collective-permute-done.refs_1_, bf16[512,256]{1,0:T(8,128)(2,1)S(1)} %collective-permute-done.2.refs_2_, ...), custom_call_target="tpu_custom_call" | custom-call | flops 2147483648 | bytes 3145728 | tf_op jit(solution)/shard_map/totals/pallas_call | solution.py:280
  60.3 1.9 %row_sums.2 = f32[32,8,128]{2,1,0:T(8,128)S(1)} custom-call(s32[3]{0:T(128)S(1)} %pad_add_fusion.pos_ref, f32[8,8,512]{2,1,0:T(8,128)S(1)} %all_to_all.40.columns_ref, f32[8,1024,512]{2,1,0:T(8,128)S(1)} %get-tuple-element.35.expd_ref), custom_call_target="tpu_custom_call" | custom-call | tf_op jit(solution)/shard_map/row_sums/pallas_call | solution.py:294
  62.3 15.3 %all_to_all.41.sums_ref = f32[32,8,128]{2,1,0:T(8,128)S(1)} all-to-all(f32[32,8,128]{2,1,0:T(8,128)S(1)} %row_sums.2), channel_id=1, replica_groups=mesh['xh'=2,'z'=8,'c'=2,'y'=4,'xl'=2] {'z','xh','xl'}, dimensions={0} | all-to-all | bytes 262144 | tf_op jit(solution)/shard_map/all_to_all | solution.py:237
  77.6 2.0 %column_sums.2 = f32[8,8,512]{2,1,0:T(8,128)S(1)} custom-call(s32[3]{0:T(128)S(1)} %pad_add_fusion.pos_ref, f32[32,8,128]{2,1,0:T(8,128)S(1)} %all_to_all.41.sums_ref, f32[8,1024,512]{2,1,0:T(8,128)S(1)} %get-tuple-element.35.expd_ref), custom_call_target="tpu_custom_call" | custom-call | tf_op jit(solution)/shard_map/column_sums/pallas_call | solution.py:307
  79.6 1.1 collective-permute-done.8.refs_5_
  80.7 0.0 collective-permute-done.7.refs_4_
  80.7 10.4 %all_to_all.42.columns_ref = f32[8,8,512]{2,1,0:T(8,128)S(1)} all-to-all(f32[8,8,512]{2,1,0:T(8,128)S(1)} %column_sums.2), channel_id=1, replica_groups=mesh['xh'=2,'z'=8,'c'=2,'y'=4,'xl'=2] {'c','y'}, dimensions={0} | all-to-all | bytes 262144 | tf_op jit(solution)/shard_map/all_to_all | solution.py:237
  91.1 1.9 %row_sums.3 = f32[32,8,128]{2,1,0:T(8,128)S(1)} custom-call(s32[3]{0:T(128)S(1)} %pad_add_fusion.pos_ref, f32[8,8,512]{2,1,0:T(8,128)S(1)} %all_to_all.42.columns_ref, f32[8,1024,512]{2,1,0:T(8,128)S(1)} %get-tuple-element.35.expd_ref), custom_call_target="tpu_custom_call" | custom-call | tf_op jit(solution)/shard_map/row_sums/pallas_call | solution.py:294
  93.2 0.8 collective-permute-start.10
  93.9 2.0 %collective-permute-start.9 = (bf16[2,8,2,32,256]{4,3,2,1,0:T(8,128)(2,1)S(1)}, bf16[2,8,2,32,256]{4,3,2,1,0:T(8,128)(2,1)S(1)}, u32[]{:S(2)}, u32[]{:S(2)}) collective-permute-start(bf16[2,8,2,32,256]{4,3,2,1,0:T(8,128)(2,1)S(1)} %slice.6), channel_id=1, source_target_pairs={{2,0},{4,2},{6,4},{0,6},{3,1},{5,3},{7,5},{1,7},{10,8},{12,10},{14... | collective-permute-start | bytes 1572872 | tf_op jit(solution)/shard_map/ppermute | solution.py:240
  95.9 15.3 %all_to_all.43.sums_ref = f32[32,8,128]{2,1,0:T(8,128)S(1)} all-to-all(f32[32,8,128]{2,1,0:T(8,128)S(1)} %row_sums.3), channel_id=1, replica_groups=mesh['xh'=2,'z'=8,'c'=2,'y'=4,'xl'=2] {'z','xh','xl'}, dimensions={0} | all-to-all | bytes 262144 | tf_op jit(solution)/shard_map/all_to_all | solution.py:237
  111.3 2.0 %column_sums.3 = f32[8,8,512]{2,1,0:T(8,128)S(1)} custom-call(s32[3]{0:T(128)S(1)} %pad_add_fusion.pos_ref, f32[32,8,128]{2,1,0:T(8,128)S(1)} %all_to_all.43.sums_ref, f32[8,1024,512]{2,1,0:T(8,128)S(1)} %get-tuple-element.35.expd_ref), custom_call_target="tpu_custom_call" | custom-call | tf_op jit(solution)/shard_map/column_sums/pallas_call | solution.py:307
  113.2 0.0 collective-permute-done.10.refs_7_
  113.3 0.0 collective-permute-done.9.refs_6_
  113.3 9.9 %all_to_all.44.columns_ref = f32[8,8,512]{2,1,0:T(8,128)S(1)} all-to-all(f32[8,8,512]{2,1,0:T(8,128)S(1)} %column_sums.3), channel_id=1, replica_groups=mesh['xh'=2,'z'=8,'c'=2,'y'=4,'xl'=2] {'c','y'}, dimensions={0} | all-to-all | bytes 262144 | tf_op jit(solution)/shard_map/all_to_all | solution.py:237
  123.2 0.0 copy-start.1
  123.2 0.0 copy-start.2
  123.2 0.0 copy-start.3
  123.2 1.9 %last_row_sums.1 = f32[32,2,8,128]{3,2,1,0:T(8,128)S(1)} custom-call(s32[3]{0:T(128)S(1)} %pad_add_fusion.pos_ref, f32[8,8,512]{2,1,0:T(8,128)S(1)} %all_to_all.44.columns_ref, f32[8,1024,512]{2,1,0:T(8,128)S(1)} %get-tuple-element.35.expd_ref, f32[8,128]{1,0:T(8,128)S(1)} %totals.1.total_ref), custom_call_target="tpu_custom_call" | custom-call | tf_op jit(solution)/shard_map/last_row_sums/pallas_call | solution.py:325
  125.1 14.5 %all_to_all.45.sums_ref = f32[32,2,8,128]{3,2,1,0:T(8,128)S(1)} all-to-all(f32[32,2,8,128]{3,2,1,0:T(8,128)S(1)} %last_row_sums.1), channel_id=1, replica_groups=mesh['xh'=2,'z'=8,'c'=2,'y'=4,'xl'=2] {'z','xh','xl'}, dimensions={0} | all-to-all | bytes 524288 | tf_op jit(solution)/shard_map/all_to_all | solution.py:237
  139.7 1.0 collective-permute-start.13
  140.6 0.2 collective-permute-start.12
  140.9 2.5 %collective-permute-start.11 = (f32[2,8,128]{2,1,0:T(8,128)S(1)}, f32[2,8,128]{2,1,0:T(8,128)S(1)}, u32[]{:S(2)}, u32[]{:S(2)}) collective-permute-start(f32[2,8,128]{2,1,0:T(8,128)S(1)} %scales.1.refs_2_), channel_id=1, source_target_pairs={{2,0},{4,2},{6,4},{0,6},{3,1},{5,3},{7,5},{1,7},{10,8},{12,10},{14... | collective-permute-start | bytes 24584 | tf_op jit(solution)/shard_map/ppermute | solution.py:240
  143.3 2.6 %grad_of_own_rows.1 = (f32[512,256]{1,0:T(8,128)S(1)}, f32[512,256]{1,0:T(8,128)S(1)}) custom-call(s32[3]{0:T(128)S(1)} %pad_add_fusion.pos_ref, f32[8,8,512]{2,1,0:T(8,128)S(1)} %all_to_all.44.columns_ref, bf16[512,256]{1,0:T(8,128)(2,1)S(1)} %book.1.refs_0_, bf16[512,256]{1,0:T(8,128)(2,1)S(1)} %collective-permute-done.3.refs_4_.refs_1_.refs_0_, ...), custom_call_target="tpu_custom_call" | custom-call | flops 1610612736 | bytes 6291456 | tf_op jit(solution)/shard_map/grad_of_own_rows/pallas_call | solution.py:349
  146.0 0.0 collective-permute-done.13.refs_3_
  146.0 0.0 collective-permute-done.12.refs_2_
  146.0 0.0 collective-permute-done.11.refs_1_
  146.0 3.5 %grad_of_other.1 = f32[512,256]{1,0:T(8,128)S(1)} custom-call(s32[3]{0:T(128)S(1)} %pad_add_fusion.pos_ref, f32[8,8,512]{2,1,0:T(8,128)S(1)} %all_to_all.44.columns_ref, bf16[512,256]{1,0:T(8,128)(2,1)S(1)} %collective-permute-done.3.refs_4_.refs_1_.refs_0_, f32[2,8,128]{2,1,0:T(8,128)S(1)} %collective-permute-done.11.refs_1_, ...), custom_call_target="tpu_custom_call" | custom-call | flops 2415919104 | bytes 6291456 | tf_op jit(solution)/shard_map/grad_of_other/pallas_call | solution.py:349
  149.5 3.3 %collective-permute-start.14 = (f32[512,256]{1,0:T(8,128)S(1)}, f32[512,256]{1,0:T(8,128)S(1)}, u32[]{:S(2)}, u32[]{:S(2)}) collective-permute-start(f32[512,256]{1,0:T(8,128)S(1)} %grad_of_other.1), channel_id=1, source_target_pairs={{0,8},{8,0},{1,9},{9,1},{2,10},{10,2},{3,11},{11,3},{4,12},{12,4},... | collective-permute-start | bytes 1572872 | tf_op jit(solution)/shard_map/ppermute | solution.py:243
  152.8 3.5 %grad_of_own.1.own_ref = f32[512,256]{1,0:T(8,128)S(1)} custom-call(s32[3]{0:T(128)S(1)} %pad_add_fusion.pos_ref, f32[8,8,512]{2,1,0:T(8,128)S(1)} %all_to_all.44.columns_ref, bf16[512,256]{1,0:T(8,128)(2,1)S(1)} %book.1.refs_0_, f32[2,8,128]{2,1,0:T(8,128)S(1)} %collective-permute-done.11.refs_1_, f32[2,8,128]{2,1,0:T(8,128)S(1)} %collective-permute-done.12.refs_2_, ...), custom_call_target="tpu_custom_call" | custom-call | flops 2415919104 | bytes 6291456 | tf_op jit(solution)/shard_map/grad_of_own/pallas_call | solution.py:349
  156.3 0.0 collective-permute-done.14.other_ref
  156.4 0.0 copy-done.1
  156.4 0.0 copy-done.2
  156.4 0.0 copy-done.3
  156.4 1.6 update.1
  (4 shorter events, 0.1 us)
Async XLA Ops:
  2.2 19.4 %all-to-all-start = ((bf16[8,2,32,256]{3,2,1,0:T(8,128)(2,1)}), bf16[8,2,32,256]{3,2,1,0:T(8,128)(2,1)S(1)}, u32[]{:S(2)}, u32[]{:S(2)}) async-start(bf16[8,2,32,256]{3,2,1,0:T(8,128)(2,1)} %views.1), calls=%async_computation | async-start | bytes 524288 | tf_op jit(solution)/shard_map/all_to_all | solution.py:237
  11.2 1.0 copy-start
  12.5 8.3 %collective-permute-start.1 = (bf16[512,256]{1,0:T(8,128)(2,1)S(1)}, bf16[512,256]{1,0:T(8,128)(2,1)S(1)}, u32[]{:S(2)}, u32[]{:S(2)}) collective-permute-start(bf16[512,256]{1,0:T(8,128)(2,1)S(1)} %book.1.refs_0_), channel_id=1, source_target_pairs={{6,0},{0,2},{2,4},{4,6},{7,1},{1,3},{3,5},{5,7},{14,8},{8,10},{10,... | collective-permute-start | bytes 786440 | tf_op jit(solution)/shard_map/ppermute | solution.py:240
  13.8 6.9 %collective-permute-start = (bf16[512,256]{1,0:T(8,128)(2,1)S(1)}, bf16[512,256]{1,0:T(8,128)(2,1)S(1)}, u32[]{:S(2)}, u32[]{:S(2)}) collective-permute-start(bf16[512,256]{1,0:T(8,128)(2,1)S(1)} %book.1.refs_0_), channel_id=1, source_target_pairs={{2,0},{4,2},{6,4},{0,6},{3,1},{5,3},{7,5},{1,7},{10,8},{12,10},{14... | collective-permute-start | bytes 786440 | tf_op jit(solution)/shard_map/ppermute | solution.py:240
  22.7 16.5 %all-to-all-start.1 = ((bf16[4,8,2,32,256]{4,3,2,1,0:T(8,128)(2,1)}), bf16[4,8,2,32,256]{4,3,2,1,0:T(8,128)(2,1)S(1)}, u32[]{:S(2)}, u32[]{:S(2)}) async-start(bf16[4,8,2,32,256]{4,3,2,1,0:T(8,128)(2,1)} %broadcast_in_dim.2), calls=%async_computation.1 | async-start | bytes 2097152 | tf_op jit(solution)/shard_map/all_to_all | solution.py:237
  26.7 6.7 %collective-permute-start.2 = (bf16[512,256]{1,0:T(8,128)(2,1)S(1)}, bf16[512,256]{1,0:T(8,128)(2,1)S(1)}, u32[]{:S(2)}, u32[]{:S(2)}) collective-permute-start(bf16[512,256]{1,0:T(8,128)(2,1)S(1)} %book.1.refs_0_), channel_id=1, source_target_pairs={{4,0},{6,2},{0,4},{2,6},{5,1},{7,3},{1,5},{3,7},{12,8},{14,10},{8,... | collective-permute-start | bytes 786440 | tf_op jit(solution)/shard_map/ppermute | solution.py:240
  29.7 8.3 %collective-permute-start.3 = (bf16[512,256]{1,0:T(8,128)(2,1)S(1)}, bf16[512,256]{1,0:T(8,128)(2,1)S(1)}, u32[]{:S(2)}, u32[]{:S(2)}) collective-permute-start(bf16[512,256]{1,0:T(8,128)(2,1)S(1)} %book.1.refs_0_), channel_id=1, source_target_pairs={{0,8},{8,0},{1,9},{9,1},{2,10},{10,2},{3,11},{11,3},{4,12},{12,4},... | collective-permute-start | bytes 786440 | tf_op jit(solution)/shard_map/ppermute | solution.py:243
  33.5 5.1 %collective-permute-start.5 = (bf16[512,256]{1,0:T(8,128)(2,1)S(1)}, bf16[512,256]{1,0:T(8,128)(2,1)S(1)}, u32[]{:S(2)}, u32[]{:S(2)}) collective-permute-start(bf16[512,256]{1,0:T(8,128)(2,1)S(1)} %collective-permute-done.2.refs_2_), channel_id=1, source_target_pairs={{0,8},{8,0},{1,9},{9,1},{2,10},{10,2},{3,11},{11,3},{4,12},{12,4},... | collective-permute-start | bytes 786440 | tf_op jit(solution)/shard_map/ppermute | solution.py:243
  37.4 1.5 collective-permute-start.4
  37.4 1.9 %collective-permute-start.6 = (bf16[512,256]{1,0:T(8,128)(2,1)S(1)}, bf16[512,256]{1,0:T(8,128)(2,1)S(1)}, u32[]{:S(2)}, u32[]{:S(2)}) collective-permute-start(bf16[512,256]{1,0:T(8,128)(2,1)S(1)} %collective-permute-done.1.refs_3_), channel_id=1, source_target_pairs={{0,8},{8,0},{1,9},{9,1},{2,10},{10,2},{3,11},{11,3},{4,12},{12,4},... | collective-permute-start | bytes 786440 | tf_op jit(solution)/shard_map/ppermute | solution.py:243
  55.2 25.6 %collective-permute-start.8 = (bf16[4,8,2,32,256]{4,3,2,1,0:T(8,128)(2,1)S(1)}, bf16[4,8,2,32,256]{4,3,2,1,0:T(8,128)(2,1)S(1)}, u32[]{:S(2)}, u32[]{:S(2)}) collective-permute-start(bf16[4,8,2,32,256]{4,3,2,1,0:T(8,128)(2,1)S(1)} %all-to-all-done.1.rows_ref.refs_3_), channel_id=1, source_target_pairs={{6,0},{0,2},{2,4},{4,6},{7,1},{1,3},{3,5},{5,7},{14,8},{8,10},{10,... | collective-permute-start | bytes 3145736 | tf_op jit(solution)/shard_map/ppermute | solution.py:240
  55.9 24.9 %collective-permute-start.7 = (bf16[4,8,2,32,256]{4,3,2,1,0:T(8,128)(2,1)S(1)}, bf16[4,8,2,32,256]{4,3,2,1,0:T(8,128)(2,1)S(1)}, u32[]{:S(2)}, u32[]{:S(2)}) collective-permute-start(bf16[4,8,2,32,256]{4,3,2,1,0:T(8,128)(2,1)S(1)} %all-to-all-done.1.rows_ref.refs_3_), channel_id=1, source_target_pairs={{2,0},{4,2},{6,4},{0,6},{3,1},{5,3},{7,5},{1,7},{10,8},{12,10},{14... | collective-permute-start | bytes 3145736 | tf_op jit(solution)/shard_map/ppermute | solution.py:240
  93.2 20.1 %collective-permute-start.10 = (bf16[2,8,2,32,256]{4,3,2,1,0:T(8,128)(2,1)S(1)}, bf16[2,8,2,32,256]{4,3,2,1,0:T(8,128)(2,1)S(1)}, u32[]{:S(2)}, u32[]{:S(2)}) collective-permute-start(bf16[2,8,2,32,256]{4,3,2,1,0:T(8,128)(2,1)S(1)} %slice.7), channel_id=1, source_target_pairs={{6,0},{0,2},{2,4},{4,6},{7,1},{1,3},{3,5},{5,7},{14,8},{8,10},{10,... | collective-permute-start | bytes 1572872 | tf_op jit(solution)/shard_map/ppermute | solution.py:240
  93.9 19.3 %collective-permute-start.9 = (bf16[2,8,2,32,256]{4,3,2,1,0:T(8,128)(2,1)S(1)}, bf16[2,8,2,32,256]{4,3,2,1,0:T(8,128)(2,1)S(1)}, u32[]{:S(2)}, u32[]{:S(2)}) collective-permute-start(bf16[2,8,2,32,256]{4,3,2,1,0:T(8,128)(2,1)S(1)} %slice.6), channel_id=1, source_target_pairs={{2,0},{4,2},{6,4},{0,6},{3,1},{5,3},{7,5},{1,7},{10,8},{12,10},{14... | collective-permute-start | bytes 1572872 | tf_op jit(solution)/shard_map/ppermute | solution.py:240
  123.2 33.2 %copy-start.1 = (f32[1,512,256]{2,1,0:T(8,128)S(1)}, f32[1,512,256]{2,1,0:T(8,128)}, u32[]{:S(2)}) copy-start(f32[1,512,256]{2,1,0:T(8,128)} %proto_ref.3) | copy-start | bytes 1572868
  123.2 33.2 %copy-start.2 = (f32[1,512,256]{2,1,0:T(8,128)S(1)}, f32[1,512,256]{2,1,0:T(8,128)}, u32[]{:S(2)}) copy-start(f32[1,512,256]{2,1,0:T(8,128)} %first_ref.1) | copy-start | bytes 1572868
  123.2 33.2 %copy-start.3 = (f32[1,512,256]{2,1,0:T(8,128)S(1)}, f32[1,512,256]{2,1,0:T(8,128)}, u32[]{:S(2)}) copy-start(f32[1,512,256]{2,1,0:T(8,128)} %second_ref.1) | copy-start | bytes 1572868
  139.7 6.3 %collective-permute-start.13 = (f32[2,8,128]{2,1,0:T(8,128)S(1)}, f32[2,8,128]{2,1,0:T(8,128)S(1)}, u32[]{:S(2)}, u32[]{:S(2)}) collective-permute-start(f32[2,8,128]{2,1,0:T(8,128)S(1)} %scales.1.refs_2_), channel_id=1, source_target_pairs={{4,0},{6,2},{0,4},{2,6},{5,1},{7,3},{1,5},{3,7},{12,8},{14,10},{8,... | collective-permute-start | bytes 24584 | tf_op jit(solution)/shard_map/ppermute | solution.py:240
  140.6 5.3 %collective-permute-start.12 = (f32[2,8,128]{2,1,0:T(8,128)S(1)}, f32[2,8,128]{2,1,0:T(8,128)S(1)}, u32[]{:S(2)}, u32[]{:S(2)}) collective-permute-start(f32[2,8,128]{2,1,0:T(8,128)S(1)} %scales.1.refs_2_), channel_id=1, source_target_pairs={{6,0},{0,2},{2,4},{4,6},{7,1},{1,3},{3,5},{5,7},{14,8},{8,10},{10,... | collective-permute-start | bytes 24584 | tf_op jit(solution)/shard_map/ppermute | solution.py:240
  140.9 5.1 %collective-permute-start.11 = (f32[2,8,128]{2,1,0:T(8,128)S(1)}, f32[2,8,128]{2,1,0:T(8,128)S(1)}, u32[]{:S(2)}, u32[]{:S(2)}) collective-permute-start(f32[2,8,128]{2,1,0:T(8,128)S(1)} %scales.1.refs_2_), channel_id=1, source_target_pairs={{2,0},{4,2},{6,4},{0,6},{3,1},{5,3},{7,5},{1,7},{10,8},{12,10},{14... | collective-permute-start | bytes 24584 | tf_op jit(solution)/shard_map/ppermute | solution.py:240
  149.5 6.8 %collective-permute-start.14 = (f32[512,256]{1,0:T(8,128)S(1)}, f32[512,256]{1,0:T(8,128)S(1)}, u32[]{:S(2)}, u32[]{:S(2)}) collective-permute-start(f32[512,256]{1,0:T(8,128)S(1)} %grad_of_other.1), channel_id=1, source_target_pairs={{0,8},{8,0},{1,9},{9,1},{2,10},{10,2},{3,11},{11,3},{4,12},{12,4},... | collective-permute-start | bytes 1572872 | tf_op jit(solution)/shard_map/ppermute | solution.py:243

commit v6 on v5

--- a/solution.py
+++ b/solution.py
@@ -264,7 +264,7 @@
     share = exchange(share, ("z",))
     shelves[1], shelves[3], share = lax.optimization_barrier((shelves[1], shelves[3], share))
     shelves += [from_core(shelf) for shelf in shelves]
-    own_rows = exchange(jnp.broadcast_to(share[None], (4,) + share.shape), ("xh", "xl"))
+    own_rows = exchange(jnp.broadcast_to(share[None], (4,) + share.shape), ("xl", "xh"))
 
     expd, copies = pl.pallas_call(
         expo_kernel,

time: 159 us -> 159 us (level)
  waiting for transfers between devices: 9.48 us -> 11.5 us
  blocking collectives: 78.4 us -> 76.5 us
    all_to_all x2, waiting for transfers between devices: 0.86 us -> 3.22 us  [exchange(): return lax.all_to_all(copies, axes, 0, 0, tiled=True)]
    all_to_all x6, blocking collectives: 78.4 us -> 76.5 us  [exchange(): return lax.all_to_all(copies, axes, 0, 0, tiled=True)]
  transfers between devices with their start and end apart: 17 -> 17, of which waited for: 7 -> 8; matrix products, arithmetic and copies ran while one was open for 0% -> 0% of each run, Pallas kernels for 9% -> 9%
where the time goes in v6:
time: 159 us; the launch traced here: 158 us
  blocking collectives  76.5 us (48%)
  starting transfers between devices  38.6 us (24%)
  Pallas kernels  27.5 us (17%)
  waiting for transfers between devices  11.5 us (7%)
  local copies, waits for them, and re-layouts  3 us (2%)
    all_to_all x6, blocking collectives, exchange(): return lax.all_to_all(copies, axes, 0, 0, tiled=True)  76.5 us
    ppermute x10, starting transfers between devices, from_y(): lax.ppermute(values, 'y', [((i + distance) % 4, i) for i in range(4)])  14.9 us
    all_to_all x2, starting transfers between devices, exchange(): return lax.all_to_all(copies, axes, 0, 0, tiled=True)  13 us
    ppermute x5, starting transfers between devices, from_core(): return lax.ppermute(values, 'c', [(0, 1), (1, 0)])  10.7 us
    pallas_call x3, Pallas kernels, grad_of(): pl.pallas_call(functools.partial(grad_kernel, halves, blocks), out_shape=...  9.7 us
    ppermute x10, waiting for transfers between devices, from_y(): lax.ppermute(values, 'y', [((i + distance) % 4, i) for i in range(4)])  6.95 us
    pallas_call x2, Pallas kernels, body(): pl.pallas_call(column_kernel, out_shape=f32(GROUP, GROUP, OWNED), in_spec...  3.97 us
    pallas_call x2, Pallas kernels, body(): pl.pallas_call(row_kernel, out_shape=f32(ROW_PEERS, 8, 128), in_specs=[SM...  3.89 us
  transfers between devices with their start and end apart: 17, of which 8 were waited for; matrix products, arithmetic and copies ran while one was open for 0% of the time, Pallas kernels for 9%

profile of v6, /device:TPU:1, one launch (start us, length us, event | category | flops | bytes accessed | tf_op | source)
XLA Modules:
  0.0 158.0 jit_solution(14028182445194395992)
XLA Ops:
  0.6 0.7 dynamic-slice_bitcast_fusion
  1.4 0.8 views.1
  2.2 9.0 %all-to-all-start = ((bf16[8,2,32,256]{3,2,1,0:T(8,128)(2,1)}), bf16[8,2,32,256]{3,2,1,0:T(8,128)(2,1)S(1)}, u32[]{:S(2)}, u32[]{:S(2)}) async-start(bf16[8,2,32,256]{3,2,1,0:T(8,128)(2,1)} %views.1), calls=%async_computation | async-start | bytes 524288 | tf_op jit(solution)/shard_map/all_to_all | solution.py:237
  11.2 0.0 copy-start
  11.2 1.0 copy-done
  12.3 0.2 book.1.refs_0_
  12.5 1.4 collective-permute-start.1
  13.8 1.5 collective-permute-start
  15.4 5.4 %collective-permute-done.1.refs_3_ = bf16[512,256]{1,0:T(8,128)(2,1)S(1)} collective-permute-done((bf16[512,256]{1,0:T(8,128)(2,1)S(1)}, bf16[512,256]{1,0:T(8,128)(2,1)S(1)}, u32[]{:S(2)}, u32[]{:S(2)}) %collective-permute-start.1) | collective-permute-done | bytes 262176 | tf_op jit(solution)/shard_map/ppermute | solution.py:240
  20.7 0.0 collective-permute-done.refs_1_
  20.7 0.9 all-to-all-done
  21.6 1.1 broadcast_in_dim.2
  22.7 4.0 %all-to-all-start.1 = ((bf16[4,8,2,32,256]{4,3,2,1,0:T(8,128)(2,1)}), bf16[4,8,2,32,256]{4,3,2,1,0:T(8,128)(2,1)S(1)}, u32[]{:S(2)}, u32[]{:S(2)}) async-start(bf16[4,8,2,32,256]{4,3,2,1,0:T(8,128)(2,1)} %broadcast_in_dim.2), calls=%async_computation.1 | async-start | bytes 2097152 | tf_op jit(solution)/shard_map/all_to_all | solution.py:237
  26.7 2.9 %collective-permute-start.2 = (bf16[512,256]{1,0:T(8,128)(2,1)S(1)}, bf16[512,256]{1,0:T(8,128)(2,1)S(1)}, u32[]{:S(2)}, u32[]{:S(2)}) collective-permute-start(bf16[512,256]{1,0:T(8,128)(2,1)S(1)} %book.1.refs_0_), channel_id=1, source_target_pairs={{4,0},{6,2},{0,4},{2,6},{5,1},{7,3},{1,5},{3,7},{12,8},{14,10},{8,... | collective-permute-start | bytes 786440 | tf_op jit(solution)/shard_map/ppermute | solution.py:240
  29.7 3.0 %collective-permute-start.3 = (bf16[512,256]{1,0:T(8,128)(2,1)S(1)}, bf16[512,256]{1,0:T(8,128)(2,1)S(1)}, u32[]{:S(2)}, u32[]{:S(2)}) collective-permute-start(bf16[512,256]{1,0:T(8,128)(2,1)S(1)} %book.1.refs_0_), channel_id=1, source_target_pairs={{0,8},{8,0},{1,9},{9,1},{2,10},{10,2},{3,11},{11,3},{4,12},{12,4},... | collective-permute-start | bytes 786440 | tf_op jit(solution)/shard_map/ppermute | solution.py:243
  32.7 0.8 collective-permute-done.2.refs_2_
  33.5 3.9 %collective-permute-start.5 = (bf16[512,256]{1,0:T(8,128)(2,1)S(1)}, bf16[512,256]{1,0:T(8,128)(2,1)S(1)}, u32[]{:S(2)}, u32[]{:S(2)}) collective-permute-start(bf16[512,256]{1,0:T(8,128)(2,1)S(1)} %collective-permute-done.2.refs_2_), channel_id=1, source_target_pairs={{0,8},{8,0},{1,9},{9,1},{2,10},{10,2},{3,11},{11,3},{4,12},{12,4},... | collective-permute-start | bytes 786440 | tf_op jit(solution)/shard_map/ppermute | solution.py:243
  37.4 0.0 collective-permute-start.4
  37.4 0.5 collective-permute-start.6
  37.9 0.1 pad_add_fusion.pos_ref
  37.9 0.0 collective-permute-done.3.refs_4_.refs_1_.refs_0_
  38.0 0.6 collective-permute-done.5.refs_6_
  38.5 0.4 collective-permute-done.4.refs_5_
  38.9 0.4 collective-permute-done.6.refs_7_
  39.3 2.4 %all-to-all-done.1.rows_ref.refs_3_ = bf16[4,8,2,32,256]{4,3,2,1,0:T(8,128)(2,1)S(1)} async-done(((bf16[4,8,2,32,256]{4,3,2,1,0:T(8,128)(2,1)}), bf16[4,8,2,32,256]{4,3,2,1,0:T(8,128)(2,1)S(1)}, u32[]{:S(2)}, u32[]{:S(2)}) %all-to-all-start.1) | async-done | bytes 1048608 | tf_op jit(solution)/shard_map/all_to_all | solution.py:237
  41.6 2.9 %expo.1 = (f32[8,1024,512]{2,1,0:T(8,128)S(1)}, f32[8,8,512]{2,1,0:T(8,128)S(1)}) custom-call(s32[3]{0:T(128)S(1)} %pad_add_fusion.pos_ref, bf16[4,8,2,32,256]{4,3,2,1,0:T(8,128)(2,1)S(1)} %all-to-all-done.1.rows_ref.refs_3_, bf16[512,256]{1,0:T(8,128)(2,1)S(1)} %book.1.refs_0_, bf16[512,256]{1,0:T(8,128)(2,1)S(1)} %collective-permute-done.refs_1_, ...), custom_call_target="tpu_custom_call" | custom-call | tf_op jit(solution)/shard_map/expo/pallas_call | solution.py:269
  44.6 10.3 %all_to_all.40.columns_ref = f32[8,8,512]{2,1,0:T(8,128)S(1)} all-to-all(f32[8,8,512]{2,1,0:T(8,128)S(1)} %get-tuple-element.31), channel_id=1, replica_groups=mesh['xh'=2,'z'=8,'c'=2,'y'=4,'xl'=2] {'c','y'}, dimensions={0} | all-to-all | bytes 262144 | tf_op jit(solution)/shard_map/all_to_all | solution.py:237
  54.9 0.7 collective-permute-start.8
  55.6 2.0 %collective-permute-start.7 = (bf16[4,8,2,32,256]{4,3,2,1,0:T(8,128)(2,1)S(1)}, bf16[4,8,2,32,256]{4,3,2,1,0:T(8,128)(2,1)S(1)}, u32[]{:S(2)}, u32[]{:S(2)}) collective-permute-start(bf16[4,8,2,32,256]{4,3,2,1,0:T(8,128)(2,1)S(1)} %all-to-all-done.1.rows_ref.refs_3_), channel_id=1, source_target_pairs={{2,0},{4,2},{6,4},{0,6},{3,1},{5,3},{7,5},{1,7},{10,8},{12,10},{14... | collective-permute-start | bytes 3145736 | tf_op jit(solution)/shard_map/ppermute | solution.py:240
  57.5 2.5 %totals.1.total_ref = f32[8,128]{1,0:T(8,128)S(1)} custom-call(bf16[4,8,2,32,256]{4,3,2,1,0:T(8,128)(2,1)S(1)} %all-to-all-done.1.rows_ref.refs_3_, bf16[512,256]{1,0:T(8,128)(2,1)S(1)} %book.1.refs_0_, bf16[512,256]{1,0:T(8,128)(2,1)S(1)} %collective-permute-done.refs_1_, bf16[512,256]{1,0:T(8,128)(2,1)S(1)} %collective-permute-done.2.refs_2_, ...), custom_call_target="tpu_custom_call" | custom-call | flops 2147483648 | bytes 3145728 | tf_op jit(solution)/shard_map/totals/pallas_call | solution.py:280
  60.0 1.9 %row_sums.2 = f32[32,8,128]{2,1,0:T(8,128)S(1)} custom-call(s32[3]{0:T(128)S(1)} %pad_add_fusion.pos_ref, f32[8,8,512]{2,1,0:T(8,128)S(1)} %all_to_all.40.columns_ref, f32[8,1024,512]{2,1,0:T(8,128)S(1)} %get-tuple-element.35.expd_ref), custom_call_target="tpu_custom_call" | custom-call | tf_op jit(solution)/shard_map/row_sums/pallas_call | solution.py:294
  62.0 15.7 %all_to_all.41.sums_ref = f32[32,8,128]{2,1,0:T(8,128)S(1)} all-to-all(f32[32,8,128]{2,1,0:T(8,128)S(1)} %row_sums.2), channel_id=1, replica_groups=mesh['xh'=2,'z'=8,'c'=2,'y'=4,'xl'=2] {'z','xh','xl'}, dimensions={0} | all-to-all | bytes 262144 | tf_op jit(solution)/shard_map/all_to_all | solution.py:237
  77.7 2.0 %column_sums.2 = f32[8,8,512]{2,1,0:T(8,128)S(1)} custom-call(s32[3]{0:T(128)S(1)} %pad_add_fusion.pos_ref, f32[32,8,128]{2,1,0:T(8,128)S(1)} %all_to_all.41.sums_ref, f32[8,1024,512]{2,1,0:T(8,128)S(1)} %get-tuple-element.35.expd_ref), custom_call_target="tpu_custom_call" | custom-call | tf_op jit(solution)/shard_map/column_sums/pallas_call | solution.py:307
  79.7 0.8 collective-permute-done.8.refs_5_
  80.4 0.0 collective-permute-done.7.refs_4_
  80.4 10.4 %all_to_all.42.columns_ref = f32[8,8,512]{2,1,0:T(8,128)S(1)} all-to-all(f32[8,8,512]{2,1,0:T(8,128)S(1)} %column_sums.2), channel_id=1, replica_groups=mesh['xh'=2,'z'=8,'c'=2,'y'=4,'xl'=2] {'c','y'}, dimensions={0} | all-to-all | bytes 262144 | tf_op jit(solution)/shard_map/all_to_all | solution.py:237
  90.8 1.9 %row_sums.3 = f32[32,8,128]{2,1,0:T(8,128)S(1)} custom-call(s32[3]{0:T(128)S(1)} %pad_add_fusion.pos_ref, f32[8,8,512]{2,1,0:T(8,128)S(1)} %all_to_all.42.columns_ref, f32[8,1024,512]{2,1,0:T(8,128)S(1)} %get-tuple-element.35.expd_ref), custom_call_target="tpu_custom_call" | custom-call | tf_op jit(solution)/shard_map/row_sums/pallas_call | solution.py:294
  92.9 0.8 collective-permute-start.10
  93.6 2.0 %collective-permute-start.9 = (bf16[2,8,2,32,256]{4,3,2,1,0:T(8,128)(2,1)S(1)}, bf16[2,8,2,32,256]{4,3,2,1,0:T(8,128)(2,1)S(1)}, u32[]{:S(2)}, u32[]{:S(2)}) collective-permute-start(bf16[2,8,2,32,256]{4,3,2,1,0:T(8,128)(2,1)S(1)} %slice.6), channel_id=1, source_target_pairs={{2,0},{4,2},{6,4},{0,6},{3,1},{5,3},{7,5},{1,7},{10,8},{12,10},{14... | collective-permute-start | bytes 1572872 | tf_op jit(solution)/shard_map/ppermute | solution.py:240
  95.6 15.7 %all_to_all.43.sums_ref = f32[32,8,128]{2,1,0:T(8,128)S(1)} all-to-all(f32[32,8,128]{2,1,0:T(8,128)S(1)} %row_sums.3), channel_id=1, replica_groups=mesh['xh'=2,'z'=8,'c'=2,'y'=4,'xl'=2] {'z','xh','xl'}, dimensions={0} | all-to-all | bytes 262144 | tf_op jit(solution)/shard_map/all_to_all | solution.py:237
  111.3 2.0 %column_sums.3 = f32[8,8,512]{2,1,0:T(8,128)S(1)} custom-call(s32[3]{0:T(128)S(1)} %pad_add_fusion.pos_ref, f32[32,8,128]{2,1,0:T(8,128)S(1)} %all_to_all.43.sums_ref, f32[8,1024,512]{2,1,0:T(8,128)S(1)} %get-tuple-element.35.expd_ref), custom_call_target="tpu_custom_call" | custom-call | tf_op jit(solution)/shard_map/column_sums/pallas_call | solution.py:307
  113.3 0.0 collective-permute-done.10.refs_7_
  113.3 0.0 collective-permute-done.9.refs_6_
  113.3 9.9 %all_to_all.44.columns_ref = f32[8,8,512]{2,1,0:T(8,128)S(1)} all-to-all(f32[8,8,512]{2,1,0:T(8,128)S(1)} %column_sums.3), channel_id=1, replica_groups=mesh['xh'=2,'z'=8,'c'=2,'y'=4,'xl'=2] {'c','y'}, dimensions={0} | all-to-all | bytes 262144 | tf_op jit(solution)/shard_map/all_to_all | solution.py:237
  123.2 0.0 copy-start.1
  123.2 0.0 copy-start.2
  123.2 0.0 copy-start.3
  123.2 1.9 %last_row_sums.1 = f32[32,2,8,128]{3,2,1,0:T(8,128)S(1)} custom-call(s32[3]{0:T(128)S(1)} %pad_add_fusion.pos_ref, f32[8,8,512]{2,1,0:T(8,128)S(1)} %all_to_all.44.columns_ref, f32[8,1024,512]{2,1,0:T(8,128)S(1)} %get-tuple-element.35.expd_ref, f32[8,128]{1,0:T(8,128)S(1)} %totals.1.total_ref), custom_call_target="tpu_custom_call" | custom-call | tf_op jit(solution)/shard_map/last_row_sums/pallas_call | solution.py:325
  125.2 14.5 %all_to_all.45.sums_ref = f32[32,2,8,128]{3,2,1,0:T(8,128)S(1)} all-to-all(f32[32,2,8,128]{3,2,1,0:T(8,128)S(1)} %last_row_sums.1), channel_id=1, replica_groups=mesh['xh'=2,'z'=8,'c'=2,'y'=4,'xl'=2] {'z','xh','xl'}, dimensions={0} | all-to-all | bytes 524288 | tf_op jit(solution)/shard_map/all_to_all | solution.py:237
  139.7 1.0 collective-permute-start.13
  140.7 0.2 collective-permute-start.12
  140.9 2.5 %collective-permute-start.11 = (f32[2,8,128]{2,1,0:T(8,128)S(1)}, f32[2,8,128]{2,1,0:T(8,128)S(1)}, u32[]{:S(2)}, u32[]{:S(2)}) collective-permute-start(f32[2,8,128]{2,1,0:T(8,128)S(1)} %scales.1.refs_2_), channel_id=1, source_target_pairs={{2,0},{4,2},{6,4},{0,6},{3,1},{5,3},{7,5},{1,7},{10,8},{12,10},{14... | collective-permute-start | bytes 24584 | tf_op jit(solution)/shard_map/ppermute | solution.py:240
  143.4 2.6 %grad_of_own_rows.1 = (f32[512,256]{1,0:T(8,128)S(1)}, f32[512,256]{1,0:T(8,128)S(1)}) custom-call(s32[3]{0:T(128)S(1)} %pad_add_fusion.pos_ref, f32[8,8,512]{2,1,0:T(8,128)S(1)} %all_to_all.44.columns_ref, bf16[512,256]{1,0:T(8,128)(2,1)S(1)} %book.1.refs_0_, bf16[512,256]{1,0:T(8,128)(2,1)S(1)} %collective-permute-done.3.refs_4_.refs_1_.refs_0_, ...), custom_call_target="tpu_custom_call" | custom-call | flops 1610612736 | bytes 6291456 | tf_op jit(solution)/shard_map/grad_of_own_rows/pallas_call | solution.py:349
  146.0 0.0 collective-permute-done.13.refs_3_
  146.0 0.0 collective-permute-done.12.refs_2_
  146.0 0.0 collective-permute-done.11.refs_1_
  146.1 3.5 %grad_of_other.1 = f32[512,256]{1,0:T(8,128)S(1)} custom-call(s32[3]{0:T(128)S(1)} %pad_add_fusion.pos_ref, f32[8,8,512]{2,1,0:T(8,128)S(1)} %all_to_all.44.columns_ref, bf16[512,256]{1,0:T(8,128)(2,1)S(1)} %collective-permute-done.3.refs_4_.refs_1_.refs_0_, f32[2,8,128]{2,1,0:T(8,128)S(1)} %collective-permute-done.11.refs_1_, ...), custom_call_target="tpu_custom_call" | custom-call | flops 2415919104 | bytes 6291456 | tf_op jit(solution)/shard_map/grad_of_other/pallas_call | solution.py:349
  149.6 3.3 %collective-permute-start.14 = (f32[512,256]{1,0:T(8,128)S(1)}, f32[512,256]{1,0:T(8,128)S(1)}, u32[]{:S(2)}, u32[]{:S(2)}) collective-permute-start(f32[512,256]{1,0:T(8,128)S(1)} %grad_of_other.1), channel_id=1, source_target_pairs={{0,8},{8,0},{1,9},{9,1},{2,10},{10,2},{3,11},{11,3},{4,12},{12,4},... | collective-permute-start | bytes 1572872 | tf_op jit(solution)/shard_map/ppermute | solution.py:243
  152.9 3.5 %grad_of_own.1.own_ref = f32[512,256]{1,0:T(8,128)S(1)} custom-call(s32[3]{0:T(128)S(1)} %pad_add_fusion.pos_ref, f32[8,8,512]{2,1,0:T(8,128)S(1)} %all_to_all.44.columns_ref, bf16[512,256]{1,0:T(8,128)(2,1)S(1)} %book.1.refs_0_, f32[2,8,128]{2,1,0:T(8,128)S(1)} %collective-permute-done.11.refs_1_, f32[2,8,128]{2,1,0:T(8,128)S(1)} %collective-permute-done.12.refs_2_, ...), custom_call_target="tpu_custom_call" | custom-call | flops 2415919104 | bytes 6291456 | tf_op jit(solution)/shard_map/grad_of_own/pallas_call | solution.py:349
  156.4 0.0 collective-permute-done.14.other_ref
  156.4 0.0 copy-done.1
  156.4 0.0 copy-done.2
  156.4 0.0 copy-done.3
  156.4 1.6 update.1
  (4 shorter events, 0.1 us)
Async XLA Ops:
  2.2 19.4 %all-to-all-start = ((bf16[8,2,32,256]{3,2,1,0:T(8,128)(2,1)}), bf16[8,2,32,256]{3,2,1,0:T(8,128)(2,1)S(1)}, u32[]{:S(2)}, u32[]{:S(2)}) async-start(bf16[8,2,32,256]{3,2,1,0:T(8,128)(2,1)} %views.1), calls=%async_computation | async-start | bytes 524288 | tf_op jit(solution)/shard_map/all_to_all | solution.py:237
  11.2 1.0 copy-start
  12.5 8.3 %collective-permute-start.1 = (bf16[512,256]{1,0:T(8,128)(2,1)S(1)}, bf16[512,256]{1,0:T(8,128)(2,1)S(1)}, u32[]{:S(2)}, u32[]{:S(2)}) collective-permute-start(bf16[512,256]{1,0:T(8,128)(2,1)S(1)} %book.1.refs_0_), channel_id=1, source_target_pairs={{6,0},{0,2},{2,4},{4,6},{7,1},{1,3},{3,5},{5,7},{14,8},{8,10},{10,... | collective-permute-start | bytes 786440 | tf_op jit(solution)/shard_map/ppermute | solution.py:240
  13.8 6.9 %collective-permute-start = (bf16[512,256]{1,0:T(8,128)(2,1)S(1)}, bf16[512,256]{1,0:T(8,128)(2,1)S(1)}, u32[]{:S(2)}, u32[]{:S(2)}) collective-permute-start(bf16[512,256]{1,0:T(8,128)(2,1)S(1)} %book.1.refs_0_), channel_id=1, source_target_pairs={{2,0},{4,2},{6,4},{0,6},{3,1},{5,3},{7,5},{1,7},{10,8},{12,10},{14... | collective-permute-start | bytes 786440 | tf_op jit(solution)/shard_map/ppermute | solution.py:240
  22.7 18.9 %all-to-all-start.1 = ((bf16[4,8,2,32,256]{4,3,2,1,0:T(8,128)(2,1)}), bf16[4,8,2,32,256]{4,3,2,1,0:T(8,128)(2,1)S(1)}, u32[]{:S(2)}, u32[]{:S(2)}) async-start(bf16[4,8,2,32,256]{4,3,2,1,0:T(8,128)(2,1)} %broadcast_in_dim.2), calls=%async_computation.1 | async-start | bytes 2097152 | tf_op jit(solution)/shard_map/all_to_all | solution.py:237
  26.7 6.7 %collective-permute-start.2 = (bf16[512,256]{1,0:T(8,128)(2,1)S(1)}, bf16[512,256]{1,0:T(8,128)(2,1)S(1)}, u32[]{:S(2)}, u32[]{:S(2)}) collective-permute-start(bf16[512,256]{1,0:T(8,128)(2,1)S(1)} %book.1.refs_0_), channel_id=1, source_target_pairs={{4,0},{6,2},{0,4},{2,6},{5,1},{7,3},{1,5},{3,7},{12,8},{14,10},{8,... | collective-permute-start | bytes 786440 | tf_op jit(solution)/shard_map/ppermute | solution.py:240
  29.7 8.3 %collective-permute-start.3 = (bf16[512,256]{1,0:T(8,128)(2,1)S(1)}, bf16[512,256]{1,0:T(8,128)(2,1)S(1)}, u32[]{:S(2)}, u32[]{:S(2)}) collective-permute-start(bf16[512,256]{1,0:T(8,128)(2,1)S(1)} %book.1.refs_0_), channel_id=1, source_target_pairs={{0,8},{8,0},{1,9},{9,1},{2,10},{10,2},{3,11},{11,3},{4,12},{12,4},... | collective-permute-start | bytes 786440 | tf_op jit(solution)/shard_map/ppermute | solution.py:243
  33.5 5.1 %collective-permute-start.5 = (bf16[512,256]{1,0:T(8,128)(2,1)S(1)}, bf16[512,256]{1,0:T(8,128)(2,1)S(1)}, u32[]{:S(2)}, u32[]{:S(2)}) collective-permute-start(bf16[512,256]{1,0:T(8,128)(2,1)S(1)} %collective-permute-done.2.refs_2_), channel_id=1, source_target_pairs={{0,8},{8,0},{1,9},{9,1},{2,10},{10,2},{3,11},{11,3},{4,12},{12,4},... | collective-permute-start | bytes 786440 | tf_op jit(solution)/shard_map/ppermute | solution.py:243
  37.4 1.5 collective-permute-start.4
  37.4 1.9 %collective-permute-start.6 = (bf16[512,256]{1,0:T(8,128)(2,1)S(1)}, bf16[512,256]{1,0:T(8,128)(2,1)S(1)}, u32[]{:S(2)}, u32[]{:S(2)}) collective-permute-start(bf16[512,256]{1,0:T(8,128)(2,1)S(1)} %collective-permute-done.1.refs_3_), channel_id=1, source_target_pairs={{0,8},{8,0},{1,9},{9,1},{2,10},{10,2},{3,11},{11,3},{4,12},{12,4},... | collective-permute-start | bytes 786440 | tf_op jit(solution)/shard_map/ppermute | solution.py:243
  54.9 25.6 %collective-permute-start.8 = (bf16[4,8,2,32,256]{4,3,2,1,0:T(8,128)(2,1)S(1)}, bf16[4,8,2,32,256]{4,3,2,1,0:T(8,128)(2,1)S(1)}, u32[]{:S(2)}, u32[]{:S(2)}) collective-permute-start(bf16[4,8,2,32,256]{4,3,2,1,0:T(8,128)(2,1)S(1)} %all-to-all-done.1.rows_ref.refs_3_), channel_id=1, source_target_pairs={{6,0},{0,2},{2,4},{4,6},{7,1},{1,3},{3,5},{5,7},{14,8},{8,10},{10,... | collective-permute-start | bytes 3145736 | tf_op jit(solution)/shard_map/ppermute | solution.py:240
  55.6 24.9 %collective-permute-start.7 = (bf16[4,8,2,32,256]{4,3,2,1,0:T(8,128)(2,1)S(1)}, bf16[4,8,2,32,256]{4,3,2,1,0:T(8,128)(2,1)S(1)}, u32[]{:S(2)}, u32[]{:S(2)}) collective-permute-start(bf16[4,8,2,32,256]{4,3,2,1,0:T(8,128)(2,1)S(1)} %all-to-all-done.1.rows_ref.refs_3_), channel_id=1, source_target_pairs={{2,0},{4,2},{6,4},{0,6},{3,1},{5,3},{7,5},{1,7},{10,8},{12,10},{14... | collective-permute-start | bytes 3145736 | tf_op jit(solution)/shard_map/ppermute | solution.py:240
  92.9 20.4 %collective-permute-start.10 = (bf16[2,8,2,32,256]{4,3,2,1,0:T(8,128)(2,1)S(1)}, bf16[2,8,2,32,256]{4,3,2,1,0:T(8,128)(2,1)S(1)}, u32[]{:S(2)}, u32[]{:S(2)}) collective-permute-start(bf16[2,8,2,32,256]{4,3,2,1,0:T(8,128)(2,1)S(1)} %slice.7), channel_id=1, source_target_pairs={{6,0},{0,2},{2,4},{4,6},{7,1},{1,3},{3,5},{5,7},{14,8},{8,10},{10,... | collective-permute-start | bytes 1572872 | tf_op jit(solution)/shard_map/ppermute | solution.py:240
  93.6 19.7 %collective-permute-start.9 = (bf16[2,8,2,32,256]{4,3,2,1,0:T(8,128)(2,1)S(1)}, bf16[2,8,2,32,256]{4,3,2,1,0:T(8,128)(2,1)S(1)}, u32[]{:S(2)}, u32[]{:S(2)}) collective-permute-start(bf16[2,8,2,32,256]{4,3,2,1,0:T(8,128)(2,1)S(1)} %slice.6), channel_id=1, source_target_pairs={{2,0},{4,2},{6,4},{0,6},{3,1},{5,3},{7,5},{1,7},{10,8},{12,10},{14... | collective-permute-start | bytes 1572872 | tf_op jit(solution)/shard_map/ppermute | solution.py:240
  123.2 33.2 %copy-start.1 = (f32[1,512,256]{2,1,0:T(8,128)S(1)}, f32[1,512,256]{2,1,0:T(8,128)}, u32[]{:S(2)}) copy-start(f32[1,512,256]{2,1,0:T(8,128)} %proto_ref.3) | copy-start | bytes 1572868
  123.2 33.2 %copy-start.2 = (f32[1,512,256]{2,1,0:T(8,128)S(1)}, f32[1,512,256]{2,1,0:T(8,128)}, u32[]{:S(2)}) copy-start(f32[1,512,256]{2,1,0:T(8,128)} %first_ref.1) | copy-start | bytes 1572868
  123.2 33.2 %copy-start.3 = (f32[1,512,256]{2,1,0:T(8,128)S(1)}, f32[1,512,256]{2,1,0:T(8,128)}, u32[]{:S(2)}) copy-start(f32[1,512,256]{2,1,0:T(8,128)} %second_ref.1) | copy-start | bytes 1572868
  139.7 6.3 %collective-permute-start.13 = (f32[2,8,128]{2,1,0:T(8,128)S(1)}, f32[2,8,128]{2,1,0:T(8,128)S(1)}, u32[]{:S(2)}, u32[]{:S(2)}) collective-permute-start(f32[2,8,128]{2,1,0:T(8,128)S(1)} %scales.1.refs_2_), channel_id=1, source_target_pairs={{4,0},{6,2},{0,4},{2,6},{5,1},{7,3},{1,5},{3,7},{12,8},{14,10},{8,... | collective-permute-start | bytes 24584 | tf_op jit(solution)/shard_map/ppermute | solution.py:240
  140.7 5.3 %collective-permute-start.12 = (f32[2,8,128]{2,1,0:T(8,128)S(1)}, f32[2,8,128]{2,1,0:T(8,128)S(1)}, u32[]{:S(2)}, u32[]{:S(2)}) collective-permute-start(f32[2,8,128]{2,1,0:T(8,128)S(1)} %scales.1.refs_2_), channel_id=1, source_target_pairs={{6,0},{0,2},{2,4},{4,6},{7,1},{1,3},{3,5},{5,7},{14,8},{8,10},{10,... | collective-permute-start | bytes 24584 | tf_op jit(solution)/shard_map/ppermute | solution.py:240
  140.9 5.1 %collective-permute-start.11 = (f32[2,8,128]{2,1,0:T(8,128)S(1)}, f32[2,8,128]{2,1,0:T(8,128)S(1)}, u32[]{:S(2)}, u32[]{:S(2)}) collective-permute-start(f32[2,8,128]{2,1,0:T(8,128)S(1)} %scales.1.refs_2_), channel_id=1, source_target_pairs={{2,0},{4,2},{6,4},{0,6},{3,1},{5,3},{7,5},{1,7},{10,8},{12,10},{14... | collective-permute-start | bytes 24584 | tf_op jit(solution)/shard_map/ppermute | solution.py:240
  149.6 6.8 %collective-permute-start.14 = (f32[512,256]{1,0:T(8,128)S(1)}, f32[512,256]{1,0:T(8,128)S(1)}, u32[]{:S(2)}, u32[]{:S(2)}) collective-permute-start(f32[512,256]{1,0:T(8,128)S(1)} %grad_of_other.1), channel_id=1, source_target_pairs={{0,8},{8,0},{1,9},{9,1},{2,10},{10,2},{3,11},{11,3},{4,12},{12,4},... | collective-permute-start | bytes 1572872 | tf_op jit(solution)/shard_map/ppermute | solution.py:243

commit v7 on v6

--- a/solution.py
+++ b/solution.py
@@ -164,15 +164,17 @@
     scales = [refs.pop(0) for _ in blocks]
     rows = [[refs.pop(0) for _ in range(2 if block == 2 else 1)] for block in blocks]
     before = [refs.pop(0) for _ in halves] if 0 not in blocks else None
-    outs, scale_ref = refs[:count], refs[count]
-    scale_a = 1.0 / (K * jnp.sum(columns_ref[...], axis=0))
-    line = lax.broadcasted_iota(jnp.int32, (GROUP, OWNED), 0)
+    outs, weights = (refs[:count], refs[count:]) if before is None else (refs[count:], refs[:count])
     for i, half in enumerate(halves):
-        picked = jnp.sum(jnp.where(line == place_of(pos_ref, 4 * half), scale_a, 0.0), axis=0, keepdims=True)
-        for j in range(OWNED // 128):
-            scale_ref[j * 128 : (j + 1) * 128, :] = jnp.broadcast_to(
-                picked[:, j * 128 : (j + 1) * 128], (128, 128)
-            ).T
+        scale_ref = weights[i]
+        if before is None:
+            scale_a = 1.0 / (K * jnp.sum(columns_ref[...], axis=0))
+            line = lax.broadcasted_iota(jnp.int32, (GROUP, OWNED), 0)
+            picked = jnp.sum(jnp.where(line == place_of(pos_ref, 4 * half), scale_a, 0.0), axis=0, keepdims=True)
+            for j in range(OWNED // 128):
+                scale_ref[j * 128 : (j + 1) * 128, :] = jnp.broadcast_to(
+                    picked[:, j * 128 : (j + 1) * 128], (128, 128)
+                ).T
         book = books[i][...]
         fresh = before is None
         for pieces, scale in zip(rows, scales):
@@ -348,20 +350,19 @@
         operands += [piece for block in blocks for piece in row_blocks[block]] + sums_so_far
         return pl.pallas_call(
             functools.partial(grad_kernel, halves, blocks),
-            out_shape=[f32(OWNED, D)] * len(halves),
+            out_shape=[f32(OWNED, D)] * len(halves) + ([] if sums_so_far else [f32(OWNED, 128)] * len(halves)),
             in_specs=[SMEM] + [VMEM] * (1 + len(operands)),
-            out_specs=[VMEM] * len(halves),
-            scratch_shapes=[pltpu.VMEM((OWNED, 128), jnp.float32)],
+            out_specs=[VMEM] * (len(halves) * (1 if sums_so_far else 2)),
             compiler_params=params(8),
             cost_estimate=cost(3 * len(halves) * len(blocks) * HELD * OWNED, 6 * MIB),
             name=name,
         )(pos, columns, *operands)
 
-    own, away = grad_of((0, 1), (0,), [], "grad_of_own_rows")
-    (away,) = grad_of((1,), (1, 3, 2), [away], "grad_of_other")
+    own, away, own_weights, away_weights = grad_of((0, 1), (0,), [], "grad_of_own_rows")
+    (away,) = grad_of((1,), (1, 3, 2), [away, away_weights], "grad_of_other")
     own, away = lax.optimization_barrier((own, away))
     other = from_core(away)
-    (own,) = grad_of((0,), (1, 3, 2), [own], "grad_of_own")
+    (own,) = grad_of((0,), (1, 3, 2), [own, own_weights], "grad_of_own")
     block = pl.BlockSpec((1, OWNED // 2, D), lambda i: (0, i, 0))
     return pl.pallas_call(
         update_kernel,

time: 159 us -> 159 us (level)
  no operation moved by 1% of the time
where the time goes in v7:
time: 159 us; the launch traced here: 158 us
  blocking collectives  76.5 us (48%)
  starting transfers between devices  38.6 us (24%)
  Pallas kernels  27.5 us (17%)
  waiting for transfers between devices  11.5 us (7%)
  local copies, waits for them, and re-layouts  3 us (2%)
    all_to_all x6, blocking collectives, exchange(): return lax.all_to_all(copies, axes, 0, 0, tiled=True)  76.5 us
    ppermute x10, starting transfers between devices, from_y(): lax.ppermute(values, 'y', [((i + distance) % 4, i) for i in range(4)])  14.9 us
    all_to_all x2, starting transfers between devices, exchange(): return lax.all_to_all(copies, axes, 0, 0, tiled=True)  13 us
    ppermute x5, starting transfers between devices, from_core(): return lax.ppermute(values, 'c', [(0, 1), (1, 0)])  10.7 us
    pallas_call x3, Pallas kernels, grad_of(): pl.pallas_call(functools.partial(grad_kernel, halves, blocks), out_shape=...  9.73 us
    ppermute x10, waiting for transfers between devices, from_y(): lax.ppermute(values, 'y', [((i + distance) % 4, i) for i in range(4)])  6.95 us
    pallas_call x2, Pallas kernels, body(): pl.pallas_call(column_kernel, out_shape=f32(GROUP, GROUP, OWNED), in_spec...  3.97 us
    pallas_call x2, Pallas kernels, body(): pl.pallas_call(row_kernel, out_shape=f32(ROW_PEERS, 8, 128), in_specs=[SM...  3.89 us
  transfers between devices with their start and end apart: 17, of which 8 were waited for; matrix products, arithmetic and copies ran while one was open for 0% of the time, Pallas kernels for 9%

profile of v7, /device:TPU:1, one launch (start us, length us, event | category | flops | bytes accessed | tf_op | source)
XLA Modules:
  0.0 158.0 jit_solution(18025110844260201782)
XLA Ops:
  0.6 0.7 dynamic-slice_bitcast_fusion
  1.4 0.8 views.1
  2.2 9.0 %all-to-all-start = ((bf16[8,2,32,256]{3,2,1,0:T(8,128)(2,1)}), bf16[8,2,32,256]{3,2,1,0:T(8,128)(2,1)S(1)}, u32[]{:S(2)}, u32[]{:S(2)}) async-start(bf16[8,2,32,256]{3,2,1,0:T(8,128)(2,1)} %views.1), calls=%async_computation | async-start | bytes 524288 | tf_op jit(solution)/shard_map/all_to_all | solution.py:239
  11.2 0.0 copy-start
  11.2 1.0 copy-done
  12.3 0.2 book.1.refs_0_
  12.5 1.4 collective-permute-start.1
  13.8 1.5 collective-permute-start
  15.4 5.4 %collective-permute-done.1.refs_3_ = bf16[512,256]{1,0:T(8,128)(2,1)S(1)} collective-permute-done((bf16[512,256]{1,0:T(8,128)(2,1)S(1)}, bf16[512,256]{1,0:T(8,128)(2,1)S(1)}, u32[]{:S(2)}, u32[]{:S(2)}) %collective-permute-start.1) | collective-permute-done | bytes 262176 | tf_op jit(solution)/shard_map/ppermute | solution.py:242
  20.7 0.0 collective-permute-done.refs_1_
  20.7 0.9 all-to-all-done
  21.6 1.1 broadcast_in_dim.2
  22.7 4.0 %all-to-all-start.1 = ((bf16[4,8,2,32,256]{4,3,2,1,0:T(8,128)(2,1)}), bf16[4,8,2,32,256]{4,3,2,1,0:T(8,128)(2,1)S(1)}, u32[]{:S(2)}, u32[]{:S(2)}) async-start(bf16[4,8,2,32,256]{4,3,2,1,0:T(8,128)(2,1)} %broadcast_in_dim.2), calls=%async_computation.1 | async-start | bytes 2097152 | tf_op jit(solution)/shard_map/all_to_all | solution.py:239
  26.7 2.9 %collective-permute-start.2 = (bf16[512,256]{1,0:T(8,128)(2,1)S(1)}, bf16[512,256]{1,0:T(8,128)(2,1)S(1)}, u32[]{:S(2)}, u32[]{:S(2)}) collective-permute-start(bf16[512,256]{1,0:T(8,128)(2,1)S(1)} %book.1.refs_0_), channel_id=1, source_target_pairs={{4,0},{6,2},{0,4},{2,6},{5,1},{7,3},{1,5},{3,7},{12,8},{14,10},{8,... | collective-permute-start | bytes 786440 | tf_op jit(solution)/shard_map/ppermute | solution.py:242
  29.7 3.0 %collective-permute-start.3 = (bf16[512,256]{1,0:T(8,128)(2,1)S(1)}, bf16[512,256]{1,0:T(8,128)(2,1)S(1)}, u32[]{:S(2)}, u32[]{:S(2)}) collective-permute-start(bf16[512,256]{1,0:T(8,128)(2,1)S(1)} %book.1.refs_0_), channel_id=1, source_target_pairs={{0,8},{8,0},{1,9},{9,1},{2,10},{10,2},{3,11},{11,3},{4,12},{12,4},... | collective-permute-start | bytes 786440 | tf_op jit(solution)/shard_map/ppermute | solution.py:245
  32.7 0.8 collective-permute-done.2.refs_2_
  33.5 3.9 %collective-permute-start.5 = (bf16[512,256]{1,0:T(8,128)(2,1)S(1)}, bf16[512,256]{1,0:T(8,128)(2,1)S(1)}, u32[]{:S(2)}, u32[]{:S(2)}) collective-permute-start(bf16[512,256]{1,0:T(8,128)(2,1)S(1)} %collective-permute-done.2.refs_2_), channel_id=1, source_target_pairs={{0,8},{8,0},{1,9},{9,1},{2,10},{10,2},{3,11},{11,3},{4,12},{12,4},... | collective-permute-start | bytes 786440 | tf_op jit(solution)/shard_map/ppermute | solution.py:245
  37.4 0.0 collective-permute-start.4
  37.4 0.5 collective-permute-start.6
  37.9 0.1 pad_add_fusion.pos_ref
  37.9 0.0 collective-permute-done.3.refs_4_.refs_1_.refs_0_
  38.0 0.6 collective-permute-done.5.refs_6_
  38.5 0.4 collective-permute-done.4.refs_5_
  38.9 0.4 collective-permute-done.6.refs_7_
  39.3 2.4 %all-to-all-done.1.rows_ref.refs_3_ = bf16[4,8,2,32,256]{4,3,2,1,0:T(8,128)(2,1)S(1)} async-done(((bf16[4,8,2,32,256]{4,3,2,1,0:T(8,128)(2,1)}), bf16[4,8,2,32,256]{4,3,2,1,0:T(8,128)(2,1)S(1)}, u32[]{:S(2)}, u32[]{:S(2)}) %all-to-all-start.1) | async-done | bytes 1048608 | tf_op jit(solution)/shard_map/all_to_all | solution.py:239
  41.6 2.9 %expo.1 = (f32[8,1024,512]{2,1,0:T(8,128)S(1)}, f32[8,8,512]{2,1,0:T(8,128)S(1)}) custom-call(s32[3]{0:T(128)S(1)} %pad_add_fusion.pos_ref, bf16[4,8,2,32,256]{4,3,2,1,0:T(8,128)(2,1)S(1)} %all-to-all-done.1.rows_ref.refs_3_, bf16[512,256]{1,0:T(8,128)(2,1)S(1)} %book.1.refs_0_, bf16[512,256]{1,0:T(8,128)(2,1)S(1)} %collective-permute-done.refs_1_, ...), custom_call_target="tpu_custom_call" | custom-call | tf_op jit(solution)/shard_map/expo/pallas_call | solution.py:271
  44.6 10.3 %all_to_all.40.columns_ref = f32[8,8,512]{2,1,0:T(8,128)S(1)} all-to-all(f32[8,8,512]{2,1,0:T(8,128)S(1)} %get-tuple-element.33), channel_id=1, replica_groups=mesh['xh'=2,'z'=8,'c'=2,'y'=4,'xl'=2] {'c','y'}, dimensions={0} | all-to-all | bytes 262144 | tf_op jit(solution)/shard_map/all_to_all | solution.py:239
  54.9 0.7 collective-permute-start.8
  55.6 2.0 %collective-permute-start.7 = (bf16[4,8,2,32,256]{4,3,2,1,0:T(8,128)(2,1)S(1)}, bf16[4,8,2,32,256]{4,3,2,1,0:T(8,128)(2,1)S(1)}, u32[]{:S(2)}, u32[]{:S(2)}) collective-permute-start(bf16[4,8,2,32,256]{4,3,2,1,0:T(8,128)(2,1)S(1)} %all-to-all-done.1.rows_ref.refs_3_), channel_id=1, source_target_pairs={{2,0},{4,2},{6,4},{0,6},{3,1},{5,3},{7,5},{1,7},{10,8},{12,10},{14... | collective-permute-start | bytes 3145736 | tf_op jit(solution)/shard_map/ppermute | solution.py:242
  57.5 2.5 %totals.1.total_ref = f32[8,128]{1,0:T(8,128)S(1)} custom-call(bf16[4,8,2,32,256]{4,3,2,1,0:T(8,128)(2,1)S(1)} %all-to-all-done.1.rows_ref.refs_3_, bf16[512,256]{1,0:T(8,128)(2,1)S(1)} %book.1.refs_0_, bf16[512,256]{1,0:T(8,128)(2,1)S(1)} %collective-permute-done.refs_1_, bf16[512,256]{1,0:T(8,128)(2,1)S(1)} %collective-permute-done.2.refs_2_, ...), custom_call_target="tpu_custom_call" | custom-call | flops 2147483648 | bytes 3145728 | tf_op jit(solution)/shard_map/totals/pallas_call | solution.py:282
  60.0 1.9 %row_sums.2 = f32[32,8,128]{2,1,0:T(8,128)S(1)} custom-call(s32[3]{0:T(128)S(1)} %pad_add_fusion.pos_ref, f32[8,8,512]{2,1,0:T(8,128)S(1)} %all_to_all.40.columns_ref, f32[8,1024,512]{2,1,0:T(8,128)S(1)} %get-tuple-element.37.expd_ref), custom_call_target="tpu_custom_call" | custom-call | tf_op jit(solution)/shard_map/row_sums/pallas_call | solution.py:296
  62.0 15.7 %all_to_all.41.sums_ref = f32[32,8,128]{2,1,0:T(8,128)S(1)} all-to-all(f32[32,8,128]{2,1,0:T(8,128)S(1)} %row_sums.2), channel_id=1, replica_groups=mesh['xh'=2,'z'=8,'c'=2,'y'=4,'xl'=2] {'z','xh','xl'}, dimensions={0} | all-to-all | bytes 262144 | tf_op jit(solution)/shard_map/all_to_all | solution.py:239
  77.7 2.0 %column_sums.2 = f32[8,8,512]{2,1,0:T(8,128)S(1)} custom-call(s32[3]{0:T(128)S(1)} %pad_add_fusion.pos_ref, f32[32,8,128]{2,1,0:T(8,128)S(1)} %all_to_all.41.sums_ref, f32[8,1024,512]{2,1,0:T(8,128)S(1)} %get-tuple-element.37.expd_ref), custom_call_target="tpu_custom_call" | custom-call | tf_op jit(solution)/shard_map/column_sums/pallas_call | solution.py:309
  79.7 0.8 collective-permute-done.8.refs_5_
  80.4 0.0 collective-permute-done.7.refs_4_
  80.4 10.4 %all_to_all.42.columns_ref = f32[8,8,512]{2,1,0:T(8,128)S(1)} all-to-all(f32[8,8,512]{2,1,0:T(8,128)S(1)} %column_sums.2), channel_id=1, replica_groups=mesh['xh'=2,'z'=8,'c'=2,'y'=4,'xl'=2] {'c','y'}, dimensions={0} | all-to-all | bytes 262144 | tf_op jit(solution)/shard_map/all_to_all | solution.py:239
  90.8 1.9 %row_sums.3 = f32[32,8,128]{2,1,0:T(8,128)S(1)} custom-call(s32[3]{0:T(128)S(1)} %pad_add_fusion.pos_ref, f32[8,8,512]{2,1,0:T(8,128)S(1)} %all_to_all.42.columns_ref, f32[8,1024,512]{2,1,0:T(8,128)S(1)} %get-tuple-element.37.expd_ref), custom_call_target="tpu_custom_call" | custom-call | tf_op jit(solution)/shard_map/row_sums/pallas_call | solution.py:296
  92.9 0.8 collective-permute-start.10
  93.6 2.0 %collective-permute-start.9 = (bf16[2,8,2,32,256]{4,3,2,1,0:T(8,128)(2,1)S(1)}, bf16[2,8,2,32,256]{4,3,2,1,0:T(8,128)(2,1)S(1)}, u32[]{:S(2)}, u32[]{:S(2)}) collective-permute-start(bf16[2,8,2,32,256]{4,3,2,1,0:T(8,128)(2,1)S(1)} %slice.6), channel_id=1, source_target_pairs={{2,0},{4,2},{6,4},{0,6},{3,1},{5,3},{7,5},{1,7},{10,8},{12,10},{14... | collective-permute-start | bytes 1572872 | tf_op jit(solution)/shard_map/ppermute | solution.py:242
  95.6 15.7 %all_to_all.43.sums_ref = f32[32,8,128]{2,1,0:T(8,128)S(1)} all-to-all(f32[32,8,128]{2,1,0:T(8,128)S(1)} %row_sums.3), channel_id=1, replica_groups=mesh['xh'=2,'z'=8,'c'=2,'y'=4,'xl'=2] {'z','xh','xl'}, dimensions={0} | all-to-all | bytes 262144 | tf_op jit(solution)/shard_map/all_to_all | solution.py:239
  111.3 2.0 %column_sums.3 = f32[8,8,512]{2,1,0:T(8,128)S(1)} custom-call(s32[3]{0:T(128)S(1)} %pad_add_fusion.pos_ref, f32[32,8,128]{2,1,0:T(8,128)S(1)} %all_to_all.43.sums_ref, f32[8,1024,512]{2,1,0:T(8,128)S(1)} %get-tuple-element.37.expd_ref), custom_call_target="tpu_custom_call" | custom-call | tf_op jit(solution)/shard_map/column_sums/pallas_call | solution.py:309
  113.3 0.0 collective-permute-done.10.refs_7_
  113.3 0.0 collective-permute-done.9.refs_6_
  113.3 9.9 %all_to_all.44.columns_ref = f32[8,8,512]{2,1,0:T(8,128)S(1)} all-to-all(f32[8,8,512]{2,1,0:T(8,128)S(1)} %column_sums.3), channel_id=1, replica_groups=mesh['xh'=2,'z'=8,'c'=2,'y'=4,'xl'=2] {'c','y'}, dimensions={0} | all-to-all | bytes 262144 | tf_op jit(solution)/shard_map/all_to_all | solution.py:239
  123.2 0.0 copy-start.1
  123.2 0.0 copy-start.2
  123.2 0.0 copy-start.3
  123.2 1.9 %last_row_sums.1 = f32[32,2,8,128]{3,2,1,0:T(8,128)S(1)} custom-call(s32[3]{0:T(128)S(1)} %pad_add_fusion.pos_ref, f32[8,8,512]{2,1,0:T(8,128)S(1)} %all_to_all.44.columns_ref, f32[8,1024,512]{2,1,0:T(8,128)S(1)} %get-tuple-element.37.expd_ref, f32[8,128]{1,0:T(8,128)S(1)} %totals.1.total_ref), custom_call_target="tpu_custom_call" | custom-call | tf_op jit(solution)/shard_map/last_row_sums/pallas_call | solution.py:327
  125.2 14.5 %all_to_all.45.sums_ref = f32[32,2,8,128]{3,2,1,0:T(8,128)S(1)} all-to-all(f32[32,2,8,128]{3,2,1,0:T(8,128)S(1)} %last_row_sums.1), channel_id=1, replica_groups=mesh['xh'=2,'z'=8,'c'=2,'y'=4,'xl'=2] {'z','xh','xl'}, dimensions={0} | all-to-all | bytes 524288 | tf_op jit(solution)/shard_map/all_to_all | solution.py:239
  139.7 1.0 collective-permute-start.13
  140.7 0.2 collective-permute-start.12
  140.9 2.5 %collective-permute-start.11 = (f32[2,8,128]{2,1,0:T(8,128)S(1)}, f32[2,8,128]{2,1,0:T(8,128)S(1)}, u32[]{:S(2)}, u32[]{:S(2)}) collective-permute-start(f32[2,8,128]{2,1,0:T(8,128)S(1)} %scales.1.refs_2_), channel_id=1, source_target_pairs={{2,0},{4,2},{6,4},{0,6},{3,1},{5,3},{7,5},{1,7},{10,8},{12,10},{14... | collective-permute-start | bytes 24584 | tf_op jit(solution)/shard_map/ppermute | solution.py:242
  143.4 2.6 %grad_of_own_rows.1 = (f32[512,256]{1,0:T(8,128)S(1)}, f32[512,256]{1,0:T(8,128)S(1)}, f32[512,128]{1,0:T(8,128)S(1)}, f32[512,128]{1,0:T(8,128)S(1)}) custom-call(s32[3]{0:T(128)S(1)} %pad_add_fusion.pos_ref, f32[8,8,512]{2,1,0:T(8,128)S(1)} %all_to_all.44.columns_ref, bf16[512,256]{1,0:T(8,128)(2,1)S(1)} %book.1.refs_0_, ...), custom_call_target="tpu_custom_call" | custom-call | flops 1610612736 | bytes 6291456 | tf_op jit(solution)/shard_map/grad_of_own_rows/pallas_call | solution.py:351
  146.0 0.0 collective-permute-done.13.refs_3_
  146.0 0.0 collective-permute-done.12.refs_2_
  146.1 0.0 collective-permute-done.11.refs_1_
  146.1 3.5 %grad_of_other.1 = f32[512,256]{1,0:T(8,128)S(1)} custom-call(s32[3]{0:T(128)S(1)} %pad_add_fusion.pos_ref, f32[8,8,512]{2,1,0:T(8,128)S(1)} %all_to_all.44.columns_ref, bf16[512,256]{1,0:T(8,128)(2,1)S(1)} %collective-permute-done.3.refs_4_.refs_1_.refs_0_, f32[2,8,128]{2,1,0:T(8,128)S(1)} %collective-permute-done.11.refs_1_, ...), custom_call_target="tpu_custom_call" | custom-call | flops 2415919104 | bytes 6291456 | tf_op jit(solution)/shard_map/grad_of_other/pallas_call | solution.py:351
  149.6 3.3 %collective-permute-start.14 = (f32[512,256]{1,0:T(8,128)S(1)}, f32[512,256]{1,0:T(8,128)S(1)}, u32[]{:S(2)}, u32[]{:S(2)}) collective-permute-start(f32[512,256]{1,0:T(8,128)S(1)} %grad_of_other.1), channel_id=1, source_target_pairs={{0,8},{8,0},{1,9},{9,1},{2,10},{10,2},{3,11},{11,3},{4,12},{12,4},... | collective-permute-start | bytes 1572872 | tf_op jit(solution)/shard_map/ppermute | solution.py:245
  152.9 3.5 %grad_of_own.1.own_ref = f32[512,256]{1,0:T(8,128)S(1)} custom-call(s32[3]{0:T(128)S(1)} %pad_add_fusion.pos_ref, f32[8,8,512]{2,1,0:T(8,128)S(1)} %all_to_all.44.columns_ref, bf16[512,256]{1,0:T(8,128)(2,1)S(1)} %book.1.refs_0_, f32[2,8,128]{2,1,0:T(8,128)S(1)} %collective-permute-done.11.refs_1_, f32[2,8,128]{2,1,0:T(8,128)S(1)} %collective-permute-done.12.refs_2_, ...), custom_call_target="tpu_custom_call" | custom-call | flops 2415919104 | bytes 6291456 | tf_op jit(solution)/shard_map/grad_of_own/pallas_call | solution.py:351
  156.4 0.0 collective-permute-done.14.other_ref
  156.4 0.0 copy-done.1
  156.4 0.0 copy-done.2
  156.4 0.0 copy-done.3
  156.5 1.6 update.1
  (4 shorter events, 0.1 us)
Async XLA Ops:
  2.2 19.4 %all-to-all-start = ((bf16[8,2,32,256]{3,2,1,0:T(8,128)(2,1)}), bf16[8,2,32,256]{3,2,1,0:T(8,128)(2,1)S(1)}, u32[]{:S(2)}, u32[]{:S(2)}) async-start(bf16[8,2,32,256]{3,2,1,0:T(8,128)(2,1)} %views.1), calls=%async_computation | async-start | bytes 524288 | tf_op jit(solution)/shard_map/all_to_all | solution.py:239
  11.2 1.0 copy-start
  12.5 8.3 %collective-permute-start.1 = (bf16[512,256]{1,0:T(8,128)(2,1)S(1)}, bf16[512,256]{1,0:T(8,128)(2,1)S(1)}, u32[]{:S(2)}, u32[]{:S(2)}) collective-permute-start(bf16[512,256]{1,0:T(8,128)(2,1)S(1)} %book.1.refs_0_), channel_id=1, source_target_pairs={{6,0},{0,2},{2,4},{4,6},{7,1},{1,3},{3,5},{5,7},{14,8},{8,10},{10,... | collective-permute-start | bytes 786440 | tf_op jit(solution)/shard_map/ppermute | solution.py:242
  13.8 6.9 %collective-permute-start = (bf16[512,256]{1,0:T(8,128)(2,1)S(1)}, bf16[512,256]{1,0:T(8,128)(2,1)S(1)}, u32[]{:S(2)}, u32[]{:S(2)}) collective-permute-start(bf16[512,256]{1,0:T(8,128)(2,1)S(1)} %book.1.refs_0_), channel_id=1, source_target_pairs={{2,0},{4,2},{6,4},{0,6},{3,1},{5,3},{7,5},{1,7},{10,8},{12,10},{14... | collective-permute-start | bytes 786440 | tf_op jit(solution)/shard_map/ppermute | solution.py:242
  22.7 18.9 %all-to-all-start.1 = ((bf16[4,8,2,32,256]{4,3,2,1,0:T(8,128)(2,1)}), bf16[4,8,2,32,256]{4,3,2,1,0:T(8,128)(2,1)S(1)}, u32[]{:S(2)}, u32[]{:S(2)}) async-start(bf16[4,8,2,32,256]{4,3,2,1,0:T(8,128)(2,1)} %broadcast_in_dim.2), calls=%async_computation.1 | async-start | bytes 2097152 | tf_op jit(solution)/shard_map/all_to_all | solution.py:239
  26.7 6.7 %collective-permute-start.2 = (bf16[512,256]{1,0:T(8,128)(2,1)S(1)}, bf16[512,256]{1,0:T(8,128)(2,1)S(1)}, u32[]{:S(2)}, u32[]{:S(2)}) collective-permute-start(bf16[512,256]{1,0:T(8,128)(2,1)S(1)} %book.1.refs_0_), channel_id=1, source_target_pairs={{4,0},{6,2},{0,4},{2,6},{5,1},{7,3},{1,5},{3,7},{12,8},{14,10},{8,... | collective-permute-start | bytes 786440 | tf_op jit(solution)/shard_map/ppermute | solution.py:242
  29.7 8.3 %collective-permute-start.3 = (bf16[512,256]{1,0:T(8,128)(2,1)S(1)}, bf16[512,256]{1,0:T(8,128)(2,1)S(1)}, u32[]{:S(2)}, u32[]{:S(2)}) collective-permute-start(bf16[512,256]{1,0:T(8,128)(2,1)S(1)} %book.1.refs_0_), channel_id=1, source_target_pairs={{0,8},{8,0},{1,9},{9,1},{2,10},{10,2},{3,11},{11,3},{4,12},{12,4},... | collective-permute-start | bytes 786440 | tf_op jit(solution)/shard_map/ppermute | solution.py:245
  33.5 5.1 %collective-permute-start.5 = (bf16[512,256]{1,0:T(8,128)(2,1)S(1)}, bf16[512,256]{1,0:T(8,128)(2,1)S(1)}, u32[]{:S(2)}, u32[]{:S(2)}) collective-permute-start(bf16[512,256]{1,0:T(8,128)(2,1)S(1)} %collective-permute-done.2.refs_2_), channel_id=1, source_target_pairs={{0,8},{8,0},{1,9},{9,1},{2,10},{10,2},{3,11},{11,3},{4,12},{12,4},... | collective-permute-start | bytes 786440 | tf_op jit(solution)/shard_map/ppermute | solution.py:245
  37.4 1.5 collective-permute-start.4
  37.4 1.9 %collective-permute-start.6 = (bf16[512,256]{1,0:T(8,128)(2,1)S(1)}, bf16[512,256]{1,0:T(8,128)(2,1)S(1)}, u32[]{:S(2)}, u32[]{:S(2)}) collective-permute-start(bf16[512,256]{1,0:T(8,128)(2,1)S(1)} %collective-permute-done.1.refs_3_), channel_id=1, source_target_pairs={{0,8},{8,0},{1,9},{9,1},{2,10},{10,2},{3,11},{11,3},{4,12},{12,4},... | collective-permute-start | bytes 786440 | tf_op jit(solution)/shard_map/ppermute | solution.py:245
  54.9 25.6 %collective-permute-start.8 = (bf16[4,8,2,32,256]{4,3,2,1,0:T(8,128)(2,1)S(1)}, bf16[4,8,2,32,256]{4,3,2,1,0:T(8,128)(2,1)S(1)}, u32[]{:S(2)}, u32[]{:S(2)}) collective-permute-start(bf16[4,8,2,32,256]{4,3,2,1,0:T(8,128)(2,1)S(1)} %all-to-all-done.1.rows_ref.refs_3_), channel_id=1, source_target_pairs={{6,0},{0,2},{2,4},{4,6},{7,1},{1,3},{3,5},{5,7},{14,8},{8,10},{10,... | collective-permute-start | bytes 3145736 | tf_op jit(solution)/shard_map/ppermute | solution.py:242
  55.6 24.9 %collective-permute-start.7 = (bf16[4,8,2,32,256]{4,3,2,1,0:T(8,128)(2,1)S(1)}, bf16[4,8,2,32,256]{4,3,2,1,0:T(8,128)(2,1)S(1)}, u32[]{:S(2)}, u32[]{:S(2)}) collective-permute-start(bf16[4,8,2,32,256]{4,3,2,1,0:T(8,128)(2,1)S(1)} %all-to-all-done.1.rows_ref.refs_3_), channel_id=1, source_target_pairs={{2,0},{4,2},{6,4},{0,6},{3,1},{5,3},{7,5},{1,7},{10,8},{12,10},{14... | collective-permute-start | bytes 3145736 | tf_op jit(solution)/shard_map/ppermute | solution.py:242
  92.9 20.4 %collective-permute-start.10 = (bf16[2,8,2,32,256]{4,3,2,1,0:T(8,128)(2,1)S(1)}, bf16[2,8,2,32,256]{4,3,2,1,0:T(8,128)(2,1)S(1)}, u32[]{:S(2)}, u32[]{:S(2)}) collective-permute-start(bf16[2,8,2,32,256]{4,3,2,1,0:T(8,128)(2,1)S(1)} %slice.7), channel_id=1, source_target_pairs={{6,0},{0,2},{2,4},{4,6},{7,1},{1,3},{3,5},{5,7},{14,8},{8,10},{10,... | collective-permute-start | bytes 1572872 | tf_op jit(solution)/shard_map/ppermute | solution.py:242
  93.6 19.7 %collective-permute-start.9 = (bf16[2,8,2,32,256]{4,3,2,1,0:T(8,128)(2,1)S(1)}, bf16[2,8,2,32,256]{4,3,2,1,0:T(8,128)(2,1)S(1)}, u32[]{:S(2)}, u32[]{:S(2)}) collective-permute-start(bf16[2,8,2,32,256]{4,3,2,1,0:T(8,128)(2,1)S(1)} %slice.6), channel_id=1, source_target_pairs={{2,0},{4,2},{6,4},{0,6},{3,1},{5,3},{7,5},{1,7},{10,8},{12,10},{14... | collective-permute-start | bytes 1572872 | tf_op jit(solution)/shard_map/ppermute | solution.py:242
  123.2 33.2 %copy-start.1 = (f32[1,512,256]{2,1,0:T(8,128)S(1)}, f32[1,512,256]{2,1,0:T(8,128)}, u32[]{:S(2)}) copy-start(f32[1,512,256]{2,1,0:T(8,128)} %proto_ref.3) | copy-start | bytes 1572868
  123.2 33.2 %copy-start.2 = (f32[1,512,256]{2,1,0:T(8,128)S(1)}, f32[1,512,256]{2,1,0:T(8,128)}, u32[]{:S(2)}) copy-start(f32[1,512,256]{2,1,0:T(8,128)} %first_ref.1) | copy-start | bytes 1572868
  123.2 33.2 %copy-start.3 = (f32[1,512,256]{2,1,0:T(8,128)S(1)}, f32[1,512,256]{2,1,0:T(8,128)}, u32[]{:S(2)}) copy-start(f32[1,512,256]{2,1,0:T(8,128)} %second_ref.1) | copy-start | bytes 1572868
  139.7 6.3 %collective-permute-start.13 = (f32[2,8,128]{2,1,0:T(8,128)S(1)}, f32[2,8,128]{2,1,0:T(8,128)S(1)}, u32[]{:S(2)}, u32[]{:S(2)}) collective-permute-start(f32[2,8,128]{2,1,0:T(8,128)S(1)} %scales.1.refs_2_), channel_id=1, source_target_pairs={{4,0},{6,2},{0,4},{2,6},{5,1},{7,3},{1,5},{3,7},{12,8},{14,10},{8,... | collective-permute-start | bytes 24584 | tf_op jit(solution)/shard_map/ppermute | solution.py:242
  140.7 5.3 %collective-permute-start.12 = (f32[2,8,128]{2,1,0:T(8,128)S(1)}, f32[2,8,128]{2,1,0:T(8,128)S(1)}, u32[]{:S(2)}, u32[]{:S(2)}) collective-permute-start(f32[2,8,128]{2,1,0:T(8,128)S(1)} %scales.1.refs_2_), channel_id=1, source_target_pairs={{6,0},{0,2},{2,4},{4,6},{7,1},{1,3},{3,5},{5,7},{14,8},{8,10},{10,... | collective-permute-start | bytes 24584 | tf_op jit(solution)/shard_map/ppermute | solution.py:242
  140.9 5.1 %collective-permute-start.11 = (f32[2,8,128]{2,1,0:T(8,128)S(1)}, f32[2,8,128]{2,1,0:T(8,128)S(1)}, u32[]{:S(2)}, u32[]{:S(2)}) collective-permute-start(f32[2,8,128]{2,1,0:T(8,128)S(1)} %scales.1.refs_2_), channel_id=1, source_target_pairs={{2,0},{4,2},{6,4},{0,6},{3,1},{5,3},{7,5},{1,7},{10,8},{12,10},{14... | collective-permute-start | bytes 24584 | tf_op jit(solution)/shard_map/ppermute | solution.py:242
  149.6 6.8 %collective-permute-start.14 = (f32[512,256]{1,0:T(8,128)S(1)}, f32[512,256]{1,0:T(8,128)S(1)}, u32[]{:S(2)}, u32[]{:S(2)}) collective-permute-start(f32[512,256]{1,0:T(8,128)S(1)} %grad_of_other.1), channel_id=1, source_target_pairs={{0,8},{8,0},{1,9},{9,1},{2,10},{10,2},{3,11},{11,3},{4,12},{12,4},... | collective-permute-start | bytes 1572872 | tf_op jit(solution)/shard_map/ppermute | solution.py:245
